TPU v7x, 256 devices: a whole 4x4x8 slice. The times are simulated.
256 devices in a mesh: tm: 16 (over x_lo, y, core), space: 16 (over z, x_hi).
Axes of the slice: x: 4 (x_hi: 2, x_lo: 2; x = x_hi * 2 + x_lo), y: 4, z: 8, core: 2. Of those that a mesh axis runs over, the one named last changes fastest.
Arguments:
- sources: float32 [4, 32, 32, 128, 128], P(None, 'tm', 'space'), may hold values from -6 to 6
- regions: int32 [128, 128], replicated, may hold values from 0 to 3
- material: float32 [3, 4], replicated, may hold values from 0.05 to 3, as said below
Outputs:
- response: float32 [4, 32, 32, 128, 128], P(None, 'tm', 'space')
Inputs may be any that keep to these rules, and one draw needn't show every extreme that they name: `material`: row 0 (shear moduli) lies within 0.3 to 3.
All inputs are finite; a program needn't handle non-finite values.
Results may differ from a plain program's by a relative error of at most 0.00007.
Values sent between devices are 32-bit elements; how exact they have to be, the bound alone decides.
No kernel may reach another device: no remote copies, remote signals or barrier semaphores. Data moves between devices by JAX's collectives and lax.ppermute only.
A program may use at most 64 MiB of HBM per device.

v0:
```python
import jax
import jax.numpy as jnp
from jax import lax
from jax.sharding import PartitionSpec as P

SWEEPS = 4


HIGHEST = lax.Precision.HIGHEST
BIOT_ALPHA = 0.6
STORAGE_COEF = 0.5
TIME_STEP = 0.5
RELAXATION = 0.8


def padded_2(cells, sides, width):
    for axis, dim in sides:
        count = lax.axis_size(axis)
        ends = count - 1
        head = lax.slice_in_dim(cells, 0, width, axis=dim)
        tail = lax.slice_in_dim(cells, cells.shape[dim] - width, cells.shape[dim], axis=dim)
        cells = jnp.concatenate(
            [
                lax.ppermute(tail, axis, [(i, (i + 1) % count) for i in range(ends)]),
                cells,
                lax.ppermute(head, axis, [((i + 1) % count, i) for i in range(ends)]),
            ],
            axis=dim,
        )
    return cells


def plane_faces(regions, material):
    classes = jnp.arange(material.shape[1], dtype=jnp.int32)
    onehot = (regions[None, :, :] == classes[:, None, None]).astype(jnp.float32)
    cell_value = jnp.sum(material[:, :, None, None] * onehot[None], axis=1)
    mean_cols = (cell_value[:, :, :-1] + cell_value[:, :, 1:]) * 0.5
    mean_rows = (cell_value[:, :-1, :] + cell_value[:, 1:, :]) * 0.5
    east_side = jnp.concatenate([mean_cols, cell_value[:, :, -1:]], axis=2)
    west_side = jnp.concatenate([cell_value[:, :, :1], mean_cols], axis=2)
    north_side = jnp.concatenate([mean_rows, cell_value[:, -1:, :]], axis=1)
    south_side = jnp.concatenate([cell_value[:, :1, :], mean_rows], axis=1)
    return jnp.stack([east_side, west_side, north_side, south_side, cell_value])


def dft_tables(cycle_len):
    counter = jnp.arange(cycle_len, dtype=jnp.int32)
    phases = (counter[:, None] * counter[None, :] % cycle_len).astype(jnp.float32) * (
        2.0 * jnp.pi / cycle_len
    )
    return (jnp.cos(phases), jnp.sin(phases))


def shift_factors(frequency, cycle_len):
    phases = (frequency % cycle_len).astype(jnp.float32) * (2.0 * jnp.pi / cycle_len)
    return (1.0 - jnp.cos(phases), jnp.sin(phases))


def to_spectrum(portion, cosine, sine_table):
    real_part = jnp.einsum("kt,ctzyx->ckzyx", cosine, portion, precision=HIGHEST)
    imag_part = -jnp.einsum("kt,ctzyx->ckzyx", sine_table, portion, precision=HIGHEST)
    return jnp.stack([real_part, imag_part], axis=1)


def to_samples(spectral, cosine, sine_table):
    cycle_len = spectral.shape[2]
    summed = jnp.einsum("kt,ckzyx->ctzyx", cosine, spectral[:, 0], precision=HIGHEST) - jnp.einsum(
        "kt,ckzyx->ctzyx", sine_table, spectral[:, 1], precision=HIGHEST
    )
    return summed / cycle_len


def operate(padded, face_table, lam_real, lam_imag):
    centre = padded[..., 1:-1, 1:-1, 1:-1]
    east_side = padded[..., 1:-1, 1:-1, 2:]
    west_side = padded[..., 1:-1, 1:-1, :-2]
    north_side = padded[..., 1:-1, 2:, 1:-1]
    south_side = padded[..., 1:-1, :-2, 1:-1]
    upward = padded[..., 2:, 1:-1, 1:-1]
    downward = padded[..., :-2, 1:-1, 1:-1]
    shear = face_table[:, 0]
    kappa_side = face_table[:4, 1]
    kappa_axis = face_table[4, 2]
    shear_diag = shear[0] + shear[1] + shear[2] + shear[3] + 2.0 * shear[4]
    kappa_diag = kappa_side[0] + kappa_side[1] + kappa_side[2] + kappa_side[3] + 2.0 * kappa_axis
    elastic = (
        shear[0] * east_side[:3]
        + shear[1] * west_side[:3]
        + shear[2] * north_side[:3]
        + shear[3] * south_side[:3]
        + shear[4] * (upward[:3] + downward[:3])
    )
    gradient = 0.5 * jnp.stack(
        [east_side[3] - west_side[3], north_side[3] - south_side[3], upward[3] - downward[3]]
    )
    momentum = shear_diag * centre[:3] - elastic + BIOT_ALPHA * gradient
    divergence = 0.5 * (
        east_side[0] - west_side[0] + (north_side[1] - south_side[1]) + (upward[2] - downward[2])
    )
    flow_sum = (
        kappa_side[0] * east_side[3]
        + kappa_side[1] * west_side[3]
        + kappa_side[2] * north_side[3]
        + kappa_side[3] * south_side[3]
        + kappa_axis * (upward[3] + downward[3])
    )
    content = BIOT_ALPHA * divergence + STORAGE_COEF * centre[3]
    lam_r = lam_real[:, None, None, None]
    lam_i = lam_imag[:, None, None, None]
    rate_term = jnp.stack(
        [lam_r * content[0] - lam_i * content[1], lam_r * content[1] + lam_i * content[0]]
    )
    pressure = rate_term + TIME_STEP * (kappa_diag * centre[3] - flow_sum)
    return jnp.concatenate([momentum, pressure[None]], axis=0)


def smooth(source_hat, face_table, lam_real, lam_imag, add_rims):
    shear = face_table[:, 0]
    kappa_side = face_table[:4, 1]
    kappa_axis = face_table[4, 2]
    shear_diag = shear[0] + shear[1] + shear[2] + shear[3] + 2.0 * shear[4]
    kappa_diag = kappa_side[0] + kappa_side[1] + kappa_side[2] + kappa_side[3] + 2.0 * kappa_axis
    diag_real = STORAGE_COEF * lam_real[:, None, None, None] + TIME_STEP * kappa_diag
    diag_imag = STORAGE_COEF * lam_imag[:, None, None, None]
    modulus = diag_real * diag_real + diag_imag * diag_imag

    def scaled(residual):
        moment = residual[:3] / shear_diag
        quot_real = (residual[3, 0] * diag_real + residual[3, 1] * diag_imag) / modulus
        quot_imag = (residual[3, 1] * diag_real - residual[3, 0] * diag_imag) / modulus
        return jnp.concatenate([moment, jnp.stack([quot_real, quot_imag])[None]], axis=0)

    iterate = RELAXATION * scaled(source_hat)
    for sweep_index in range(SWEEPS - 1):
        residual = source_hat - operate(add_rims(iterate), face_table, lam_real, lam_imag)
        iterate = iterate + RELAXATION * scaled(residual)
    return iterate


def on_device(sources, regions, material):
    local_steps = sources.shape[1]
    ranks = lax.axis_size("tm")
    cycle_len = local_steps * ranks
    cosine, sine_table = dft_tables(cycle_len)
    face_table = plane_faces(regions, material)
    spectral = lax.all_to_all(
        to_spectrum(
            lax.all_to_all(sources, "tm", split_axis=3, concat_axis=1, tiled=True),
            cosine,
            sine_table,
        ),
        "tm",
        split_axis=2,
        concat_axis=4,
        tiled=True,
    )
    frequency = lax.axis_index("tm") * local_steps + jnp.arange(local_steps, dtype=jnp.int32)
    lam_real, lam_imag = shift_factors(frequency, cycle_len)

    def add_rims(iterate):
        haloed = padded_2(iterate, (("space", 3),), 1)
        return jnp.pad(haloed, ((0, 0), (0, 0), (0, 0), (0, 0), (1, 1), (1, 1)))

    solved = smooth(spectral, face_table, lam_real, lam_imag, add_rims)
    return lax.all_to_all(
        to_samples(
            lax.all_to_all(solved, "tm", split_axis=4, concat_axis=2, tiled=True),
            cosine,
            sine_table,
        ),
        "tm",
        split_axis=1,
        concat_axis=3,
        tiled=True,
    )


def solution(mesh):
    in_specs = (P(None, "tm", "space", None, None), P(), P())
    out_specs = P(None, "tm", "space", None, None)
    return jax.shard_map(
        on_device, mesh=mesh, in_specs=in_specs, out_specs=out_specs, check_vma=False
    )
```

profile of v0, /device:TPU:96, one launch (start us, length us, event | category | flops | bytes accessed | tf_op | source)
XLA Modules:
  0.0 306.3 jit_solution(9163546020600346040)
XLA Ops:
  0.0 2.9 copy.50
  2.9 5.5 %all-to-all-start = ((f32[4,2,2,128,128]{4,0,2,1,3:T(4,128)}), f32[4,2,2,128,128]{4,0,2,1,3:T(4,128)S(1)}, u32[]{:S(2)}, u32[]{:S(2)}) async-start(f32[4,2,2,128,128]{4,0,2,1,3:T(4,128)} %copy.50), calls=%async_computation | async-start | bytes 2097152 | tf_op jit(solution)/shard_map/all_to_all | solution.py:148
  8.5 16.5 %all-to-all-done = f32[4,2,2,128,128]{4,0,2,1,3:T(4,128)S(1)} async-done(((f32[4,2,2,128,128]{4,0,2,1,3:T(4,128)}), f32[4,2,2,128,128]{4,0,2,1,3:T(4,128)S(1)}, u32[]{:S(2)}, u32[]{:S(2)}) %all-to-all-start) | async-done | bytes 1048608 | tf_op jit(solution)/shard_map/all_to_all | solution.py:148
  28.0 2.6 copy.54
  30.6 3.8 %all-to-all-start.1 = ((f32[4,2,32,2,8,128]{5,4,3,0,1,2:T(8,128)}), f32[4,2,32,2,8,128]{5,4,3,0,1,2:T(8,128)S(1)}, u32[]{:S(2)}, u32[]{:S(2)}) async-start(f32[4,2,32,2,8,128]{5,4,3,0,1,2:T(8,128)} %copy.54), calls=%async_computation.1 | async-start | bytes 4194304 | tf_op jit(solution)/shard_map/all_to_all | solution.py:146
  35.3 27.9 %all-to-all-done.1 = f32[4,2,32,2,8,128]{5,4,3,0,1,2:T(8,128)S(1)} async-done(((f32[4,2,32,2,8,128]{5,4,3,0,1,2:T(8,128)}), f32[4,2,32,2,8,128]{5,4,3,0,1,2:T(8,128)S(1)}, u32[]{:S(2)}, u32[]{:S(2)}) %all-to-all-start.1) | async-done | bytes 2097184 | tf_op jit(solution)/shard_map/all_to_all | solution.py:146
  64.6 4.6 %collective-permute-start = (f32[4,2,2,1,128,128]{5,4,3,2,1,0:T(8,128)S(1)}, f32[4,2,2,1,128,128]{5,4,3,2,1,0:T(8,128)S(1)}, u32[]{:S(2)}, u32[]{:S(2)}) collective-permute-start(f32[4,2,2,1,128,128]{5,4,3,2,1,0:T(8,128)S(1)} %get-tuple-element.30), channel_id=1, source_target_pairs={{0,1},{1,2},{2,3},{3,4},{4,5},{5,6},{6,7},{7,8},{8,9},{9,10},{10,1... | collective-permute-start | bytes 3145736 | tf_op jit(solution)/shard_map/ppermute | solution.py:24
  69.3 3.8 %collective-permute-start.1 = (f32[4,2,2,1,128,128]{5,4,3,2,1,0:T(8,128)S(1)}, f32[4,2,2,1,128,128]{5,4,3,2,1,0:T(8,128)S(1)}, u32[]{:S(2)}, u32[]{:S(2)}) collective-permute-start(f32[4,2,2,1,128,128]{5,4,3,2,1,0:T(8,128)S(1)} %get-tuple-element.29), channel_id=1, source_target_pairs={{1,0},{2,1},{3,2},{4,3},{5,4},{6,5},{7,6},{8,7},{9,8},{10,9},{11,1... | collective-permute-start | bytes 3145736 | tf_op jit(solution)/shard_map/ppermute | solution.py:26
  73.1 40.8 %collective-permute-done = f32[4,2,2,1,128,128]{5,4,3,2,1,0:T(8,128)S(1)} collective-permute-done((f32[4,2,2,1,128,128]{5,4,3,2,1,0:T(8,128)S(1)}, f32[4,2,2,1,128,128]{5,4,3,2,1,0:T(8,128)S(1)}, u32[]{:S(2)}, u32[]{:S(2)}) %collective-permute-start) | collective-permute-done | bytes 1048608 | tf_op jit(solution)/shard_map/ppermute | solution.py:24
  113.9 2.2 collective-permute-done.1
  116.1 3.8 %select_maximum_fusion.4 = f32[4,2,2,4,130,130]{5,4,3,2,1,0:T(8,128)S(1)} fusion(f32[4,2,2,1,128,128]{5,4,3,2,1,0:T(8,128)S(1)} %collective-permute-done.1, f32[4,2,2,2,128,128]{5,4,3,2,1,0:T(8,128)S(1)} %maximum_multiply_fusion, f32[4,2,2,1,128,128]{5,4,3,2,1,0:T(8,128)S(1)} %collective-permute-done), kind=kLoop, calls=%fused_computation.8 | loop fusion | flops 16224000 | bytes 8520704 | tf_op jit(solution)/shard_map/concatenate | solution.py:22
  124.7 3.7 %collective-permute-start.2 = (f32[4,2,2,1,128,128]{5,4,3,2,1,0:T(8,128)S(1)}, f32[4,2,2,1,128,128]{5,4,3,2,1,0:T(8,128)S(1)}, u32[]{:S(2)}, u32[]{:S(2)}) collective-permute-start(f32[4,2,2,1,128,128]{5,4,3,2,1,0:T(8,128)S(1)} %get-tuple-element.28), channel_id=1, source_target_pairs={{0,1},{1,2},{2,3},{3,4},{4,5},{5,6},{6,7},{7,8},{8,9},{9,10},{10,1... | collective-permute-start | bytes 3145736 | tf_op jit(solution)/shard_map/ppermute | solution.py:24
  128.5 4.5 %collective-permute-start.3 = (f32[4,2,2,1,128,128]{5,4,3,2,1,0:T(8,128)S(1)}, f32[4,2,2,1,128,128]{5,4,3,2,1,0:T(8,128)S(1)}, u32[]{:S(2)}, u32[]{:S(2)}) collective-permute-start(f32[4,2,2,1,128,128]{5,4,3,2,1,0:T(8,128)S(1)} %get-tuple-element.27), channel_id=1, source_target_pairs={{1,0},{2,1},{3,2},{4,3},{5,4},{6,5},{7,6},{8,7},{9,8},{10,9},{11,1... | collective-permute-start | bytes 3145736 | tf_op jit(solution)/shard_map/ppermute | solution.py:26
  133.0 39.3 %collective-permute-done.2 = f32[4,2,2,1,128,128]{5,4,3,2,1,0:T(8,128)S(1)} collective-permute-done((f32[4,2,2,1,128,128]{5,4,3,2,1,0:T(8,128)S(1)}, f32[4,2,2,1,128,128]{5,4,3,2,1,0:T(8,128)S(1)}, u32[]{:S(2)}, u32[]{:S(2)}) %collective-permute-start.2) | collective-permute-done | bytes 1048608 | tf_op jit(solution)/shard_map/ppermute | solution.py:24
  172.3 4.3 %collective-permute-done.3 = f32[4,2,2,1,128,128]{5,4,3,2,1,0:T(8,128)S(1)} collective-permute-done((f32[4,2,2,1,128,128]{5,4,3,2,1,0:T(8,128)S(1)}, f32[4,2,2,1,128,128]{5,4,3,2,1,0:T(8,128)S(1)}, u32[]{:S(2)}, u32[]{:S(2)}) %collective-permute-start.3) | collective-permute-done | bytes 1048608 | tf_op jit(solution)/shard_map/ppermute | solution.py:26
  176.6 3.8 %select_maximum_fusion.2 = f32[4,2,2,4,130,130]{5,4,3,2,1,0:T(8,128)S(1)} fusion(f32[4,2,2,1,128,128]{5,4,3,2,1,0:T(8,128)S(1)} %collective-permute-done.3, f32[4,2,2,2,128,128]{5,4,3,2,1,0:T(8,128)S(1)} %fusion.3, f32[4,2,2,1,128,128]{5,4,3,2,1,0:T(8,128)S(1)} %collective-permute-done.2), kind=kLoop, calls=%fused_computation.6 | loop fusion | flops 16224000 | bytes 8520704 | tf_op jit(solution)/shard_map/concatenate | solution.py:22
  182.0 1.9 fusion.18
  185.1 1.9 collective-permute-start.4
  187.1 6.5 %collective-permute-start.5 = (f32[4,2,2,1,128,128]{5,4,3,2,1,0:T(8,128)S(1)}, f32[4,2,2,1,128,128]{5,4,3,2,1,0:T(8,128)S(1)}, u32[]{:S(2)}, u32[]{:S(2)}) collective-permute-start(f32[4,2,2,1,128,128]{5,4,3,2,1,0:T(8,128)S(1)} %get-tuple-element.25), channel_id=1, source_target_pairs={{1,0},{2,1},{3,2},{4,3},{5,4},{6,5},{7,6},{8,7},{9,8},{10,9},{11,1... | collective-permute-start | bytes 3145736 | tf_op jit(solution)/shard_map/ppermute | solution.py:26
  193.6 38.8 %collective-permute-done.4 = f32[4,2,2,1,128,128]{5,4,3,2,1,0:T(8,128)S(1)} collective-permute-done((f32[4,2,2,1,128,128]{5,4,3,2,1,0:T(8,128)S(1)}, f32[4,2,2,1,128,128]{5,4,3,2,1,0:T(8,128)S(1)}, u32[]{:S(2)}, u32[]{:S(2)}) %collective-permute-start.4) | collective-permute-done | bytes 1048608 | tf_op jit(solution)/shard_map/ppermute | solution.py:24
  232.4 4.6 %collective-permute-done.5 = f32[4,2,2,1,128,128]{5,4,3,2,1,0:T(8,128)S(1)} collective-permute-done((f32[4,2,2,1,128,128]{5,4,3,2,1,0:T(8,128)S(1)}, f32[4,2,2,1,128,128]{5,4,3,2,1,0:T(8,128)S(1)}, u32[]{:S(2)}, u32[]{:S(2)}) %collective-permute-start.5) | collective-permute-done | bytes 1048608 | tf_op jit(solution)/shard_map/ppermute | solution.py:26
  237.0 3.8 %select_maximum_fusion = f32[4,2,2,4,130,130]{5,4,3,2,1,0:T(8,128)S(1)} fusion(f32[4,2,2,1,128,128]{5,4,3,2,1,0:T(8,128)S(1)} %collective-permute-done.5, f32[4,2,2,2,128,128]{5,4,3,2,1,0:T(8,128)S(1)} %fusion.4, f32[4,2,2,1,128,128]{5,4,3,2,1,0:T(8,128)S(1)} %collective-permute-done.4), kind=kLoop, calls=%fused_computation.4 | loop fusion | flops 16224000 | bytes 8520704 | tf_op jit(solution)/shard_map/concatenate | solution.py:22
  247.0 33.4 %all_to_all.72 = f32[4,2,2,2,128,128]{5,3,2,1,0,4:T(2,128)S(1)} all-to-all(f32[4,2,2,2,128,128]{5,3,2,1,0,4:T(2,128)S(1)} %copy.58), channel_id=1, replica_groups=mesh['tm'=16,'space'=16] {'tm'}, dimensions={4} | all-to-all | bytes 4194304 | tf_op jit(solution)/shard_map/all_to_all | solution.py:167
  286.1 19.1 %all_to_all.73 = f32[4,32,2,8,128]{4,3,2,0,1:T(8,128)S(1)} all-to-all(f32[4,32,2,8,128]{4,3,2,0,1:T(8,128)S(1)} %copy.61), channel_id=1, replica_groups=mesh['tm'=16,'space'=16] {'tm'}, dimensions={1} | all-to-all | bytes 2097152 | tf_op jit(solution)/shard_map/all_to_all | solution.py:165
  (63 shorter events, 25.7 us)
Async XLA Ops:
  0.0 8.5 %copy-start = (s32[128,128]{1,0:T(8,128)S(1)}, s32[128,128]{1,0:T(8,128)}, u32[]{:S(2)}) copy-start(s32[128,128]{1,0:T(8,128)} %param.4) | copy-start | bytes 196612
  2.9 22.1 %all-to-all-start = ((f32[4,2,2,128,128]{4,0,2,1,3:T(4,128)}), f32[4,2,2,128,128]{4,0,2,1,3:T(4,128)S(1)}, u32[]{:S(2)}, u32[]{:S(2)}) async-start(f32[4,2,2,128,128]{4,0,2,1,3:T(4,128)} %copy.50), calls=%async_computation | async-start | bytes 2097152 | tf_op jit(solution)/shard_map/all_to_all | solution.py:148
  30.6 3.9 %copy-start.1 = (f32[3,4]{1,0:T(4,128)S(1)}, f32[3,4]{1,0:T(4,128)}, u32[]{:S(2)}) copy-start(f32[3,4]{1,0:T(4,128)} %param.5) | copy-start | bytes 148
  30.6 32.7 %all-to-all-start.1 = ((f32[4,2,32,2,8,128]{5,4,3,0,1,2:T(8,128)}), f32[4,2,32,2,8,128]{5,4,3,0,1,2:T(8,128)S(1)}, u32[]{:S(2)}, u32[]{:S(2)}) async-start(f32[4,2,32,2,8,128]{5,4,3,0,1,2:T(8,128)} %copy.54), calls=%async_computation.1 | async-start | bytes 4194304 | tf_op jit(solution)/shard_map/all_to_all | solution.py:146
  64.6 49.3 %collective-permute-start = (f32[4,2,2,1,128,128]{5,4,3,2,1,0:T(8,128)S(1)}, f32[4,2,2,1,128,128]{5,4,3,2,1,0:T(8,128)S(1)}, u32[]{:S(2)}, u32[]{:S(2)}) collective-permute-start(f32[4,2,2,1,128,128]{5,4,3,2,1,0:T(8,128)S(1)} %get-tuple-element.30), channel_id=1, source_target_pairs={{0,1},{1,2},{2,3},{3,4},{4,5},{5,6},{6,7},{7,8},{8,9},{9,10},{10,1... | collective-permute-start | bytes 3145736 | tf_op jit(solution)/shard_map/ppermute | solution.py:24
  69.3 46.8 %collective-permute-start.1 = (f32[4,2,2,1,128,128]{5,4,3,2,1,0:T(8,128)S(1)}, f32[4,2,2,1,128,128]{5,4,3,2,1,0:T(8,128)S(1)}, u32[]{:S(2)}, u32[]{:S(2)}) collective-permute-start(f32[4,2,2,1,128,128]{5,4,3,2,1,0:T(8,128)S(1)} %get-tuple-element.29), channel_id=1, source_target_pairs={{1,0},{2,1},{3,2},{4,3},{5,4},{6,5},{7,6},{8,7},{9,8},{10,9},{11,1... | collective-permute-start | bytes 3145736 | tf_op jit(solution)/shard_map/ppermute | solution.py:26
  124.7 47.5 %collective-permute-start.2 = (f32[4,2,2,1,128,128]{5,4,3,2,1,0:T(8,128)S(1)}, f32[4,2,2,1,128,128]{5,4,3,2,1,0:T(8,128)S(1)}, u32[]{:S(2)}, u32[]{:S(2)}) collective-permute-start(f32[4,2,2,1,128,128]{5,4,3,2,1,0:T(8,128)S(1)} %get-tuple-element.28), channel_id=1, source_target_pairs={{0,1},{1,2},{2,3},{3,4},{4,5},{5,6},{6,7},{7,8},{8,9},{9,10},{10,1... | collective-permute-start | bytes 3145736 | tf_op jit(solution)/shard_map/ppermute | solution.py:24
  128.5 48.1 %collective-permute-start.3 = (f32[4,2,2,1,128,128]{5,4,3,2,1,0:T(8,128)S(1)}, f32[4,2,2,1,128,128]{5,4,3,2,1,0:T(8,128)S(1)}, u32[]{:S(2)}, u32[]{:S(2)}) collective-permute-start(f32[4,2,2,1,128,128]{5,4,3,2,1,0:T(8,128)S(1)} %get-tuple-element.27), channel_id=1, source_target_pairs={{1,0},{2,1},{3,2},{4,3},{5,4},{6,5},{7,6},{8,7},{9,8},{10,9},{11,1... | collective-permute-start | bytes 3145736 | tf_op jit(solution)/shard_map/ppermute | solution.py:26
  185.1 47.3 %collective-permute-start.4 = (f32[4,2,2,1,128,128]{5,4,3,2,1,0:T(8,128)S(1)}, f32[4,2,2,1,128,128]{5,4,3,2,1,0:T(8,128)S(1)}, u32[]{:S(2)}, u32[]{:S(2)}) collective-permute-start(f32[4,2,2,1,128,128]{5,4,3,2,1,0:T(8,128)S(1)} %get-tuple-element.26), channel_id=1, source_target_pairs={{0,1},{1,2},{2,3},{3,4},{4,5},{5,6},{6,7},{7,8},{8,9},{9,10},{10,1... | collective-permute-start | bytes 3145736 | tf_op jit(solution)/shard_map/ppermute | solution.py:24
  187.1 49.9 %collective-permute-start.5 = (f32[4,2,2,1,128,128]{5,4,3,2,1,0:T(8,128)S(1)}, f32[4,2,2,1,128,128]{5,4,3,2,1,0:T(8,128)S(1)}, u32[]{:S(2)}, u32[]{:S(2)}) collective-permute-start(f32[4,2,2,1,128,128]{5,4,3,2,1,0:T(8,128)S(1)} %get-tuple-element.25), channel_id=1, source_target_pairs={{1,0},{2,1},{3,2},{4,3},{5,4},{6,5},{7,6},{8,7},{9,8},{10,9},{11,1... | collective-permute-start | bytes 3145736 | tf_op jit(solution)/shard_map/ppermute | solution.py:26
where the time goes:
time: 310 us; the launch traced here: 306 us
  waiting for transfers between devices  174 us (56%)
  blocking collectives  52.5 us (17%)
  starting transfers between devices  34.5 us (11%)
  other arithmetic  26.8 us (9%)
  local copies, waits for them, and re-layouts  13.2 us (4%)
  matrix products  4.42 us (1%)
    ppermute x3, waiting for transfers between devices, padded_2(): lax.ppermute(tail, axis, [(i, (i + 1) % count) for i in range(ends)])  119 us
    all_to_all x1, blocking collectives, on_device(): lax.all_to_all(solved, 'tm', split_axis=4, concat_axis=2, tiled=True)  33.4 us
    all_to_all x1, waiting for transfers between devices, on_device(): lax.all_to_all(to_spectrum(lax.all_to_all(sources, 'tm', split_axis=3, co...  27.9 us
    all_to_all x1, blocking collectives, on_device(): lax.all_to_all(to_samples(lax.all_to_all(solved, 'tm', split_axis=4, conc...  19.1 us
    all_to_all x1, waiting for transfers between devices, on_device(): lax.all_to_all(sources, 'tm', split_axis=3, concat_axis=1, tiled=True)  16.5 us
    ppermute x3, starting transfers between devices, padded_2(): lax.ppermute(head, axis, [((i + 1) % count, i) for i in range(ends)])  14.8 us
    concatenate x3, other arithmetic, padded_2(): jnp.concatenate([lax.ppermute(tail, axis, [(i, (i + 1) % count) for i in...  11.3 us
    ppermute x3, waiting for transfers between devices, padded_2(): lax.ppermute(head, axis, [((i + 1) % count, i) for i in range(ends)])  11.1 us
  transfers between devices with their start and end apart: 8, of which 8 were waited for; matrix products, arithmetic and copies ran while one was open for 0% of the time, Pallas kernels for 0%

commit v1 on v0

v1 whole, which is shorter than its diff:
```python
import functools
import math

import jax
import jax.numpy as jnp
import numpy as np
from jax import lax
from jax.experimental import pallas as pl
from jax.experimental.pallas import tpu as pltpu
from jax.sharding import Mesh
from jax.sharding import PartitionSpec as P

AXES = ("xl", "y", "c", "z", "xh")
SIZES = dict(xl=2, y=4, c=2, z=8, xh=2)
LEVEL = ("xl", "y", "c", "xh")
STEPS = 32
PAIRS = 16
FIELDS = 4
MIB = 1 << 20


def chip_at(pos):
    y, x = divmod(pos, 4)
    return (3 - x if y % 2 else x), y


def level_index(pos, core):
    x, y = chip_at(pos)
    return ((((x % 2) * 4 + y) * 2 + core) * 2) + x // 2


def device_index(z, block):
    x, y = chip_at(block // 2)
    return ((((x % 2) * 4 + y) * 2 + block % 2) * 8 + z) * 2 + x // 2


def shift(dz, db):
    return [
        (device_index(z, b), device_index(z + dz, b + db))
        for z in range(8)
        for b in range(32)
        if 0 <= z + dz < 8 and 0 <= b + db < 32
    ]


def rows():
    return lax.broadcasted_iota(jnp.int32, (8, 128), 0)


def lanes():
    return lax.broadcasted_iota(jnp.int32, (8, 128), 1)


def among(index, members):
    mask = index == members[0]
    for member in members[1:]:
        mask = mask | (index == member)
    return mask


def roll(tile, amount):
    amount %= 8
    return tile if amount == 0 else pltpu.roll(tile, amount, 0)


def mul_const(re, im, cr, ci):
    def axpy(a, x, b, y):
        terms = []
        for k, v in ((a, x), (b, y)):
            if abs(k) > 1e-12:
                terms.append((k, v))
        total = None
        for k, v in terms:
            if total is None:
                total = v if abs(k - 1) < 1e-12 else (-v if abs(k + 1) < 1e-12 else v * np.float32(k))
            elif abs(k - 1) < 1e-12:
                total = total + v
            elif abs(k + 1) < 1e-12:
                total = total - v
            else:
                total = total + v * np.float32(k)
        return total

    if abs(abs(cr) - abs(ci)) < 1e-12:
        root = np.float32(abs(cr))
        sr, si = math.copysign(1, cr), math.copysign(1, ci)
        return axpy(sr, re * root, -si, im * root), axpy(si, re * root, sr, im * root)
    return axpy(cr, re, -ci, im), axpy(ci, re, cr, im)


def rfft(x):
    n = len(x)
    if n == 2:
        return [(x[0] + x[1], None), (x[0] - x[1], None)]
    even, odd = rfft(x[0::2]), rfft(x[1::2])
    out = [None] * (n // 2 + 1)
    out[0] = (even[0][0] + odd[0][0], None)
    out[n // 2] = (even[0][0] - odd[0][0], None)
    out[n // 4] = (even[n // 4][0], -odd[n // 4][0])
    for k in range(1, n // 4):
        angle = -2 * math.pi * k / n
        tr, ti = mul_const(*odd[k], math.cos(angle), math.sin(angle))
        er, ei = even[k]
        out[k] = (er + tr, ei + ti)
        out[n // 2 - k] = (er - tr, ti - ei)
    return out


def irfft(spec):
    n = 2 * (len(spec) - 1)
    if n == 2:
        return [spec[0][0] + spec[1][0], spec[0][0] - spec[1][0]]
    q = n // 4
    even, odd = [None] * (q + 1), [None] * (q + 1)
    even[0] = (spec[0][0] + spec[2 * q][0], None)
    odd[0] = (spec[0][0] - spec[2 * q][0], None)
    even[q] = (2.0 * spec[q][0], None)
    odd[q] = (-2.0 * spec[q][1], None)
    for k in range(1, q):
        ar, ai = spec[k]
        br, bi = spec[2 * q - k]
        even[k] = (ar + br, ai - bi)
        angle = 2 * math.pi * k / n
        odd[k] = mul_const(ar - br, ai + bi, math.cos(angle), math.sin(angle))
    a, b = irfft(even), irfft(odd)
    return [v for two in zip(a, b) for v in two]


def split_kernel(src, out):
    upper = rows() < 4

    def body(i, _):
        f, t = i // 2, i % 2
        for pos in range(16):
            a = src[f, t, 0, pl.ds(8 * pos, 8), :]
            b = src[f, t, 1, pl.ds(8 * pos, 8), :]
            out[level_index(pos, 0), f, t] = jnp.where(upper, a, roll(b, 4))
            out[level_index(pos, 1), f, t] = jnp.where(upper, roll(a, 4), b)
        return 0

    lax.fori_loop(0, 8, body, 0)


def join_kernel(src, out):
    upper = rows() < 4

    def body(i, _):
        f, t = i // 2, i % 2
        for pos in range(16):
            a = src[level_index(pos, 0), f, t]
            b = src[level_index(pos, 1), f, t]
            out[f, t, 0, pl.ds(8 * pos, 8), :] = jnp.where(upper, a, roll(b, 4))
            out[f, t, 1, pl.ds(8 * pos, 8), :] = jnp.where(upper, roll(a, 4), b)
        return 0

    lax.fori_loop(0, 8, body, 0)


def spectrum_kernel(src, own, zup, zdn):
    upper = rows() < 4

    def body(f, _):
        for half in range(2):
            spec = rfft([src[(t // 2) * 2 + half, f, t % 2] for t in range(STEPS)])
            pairs = [(spec[0][0], spec[16][0])] + spec[1:16]
            for q, (re, im) in enumerate(pairs):
                own[q, half, f, 0] = re
                own[q, half, f, 1] = im
                if half == 0:
                    zdn[q, f, 0] = re
                    zdn[q, f, 1] = im
                    zup[q, f, 2] = jnp.where(upper, roll(re, 4), im)
                else:
                    zup[q, f, 0] = re
                    zup[q, f, 1] = im
                    zdn[q, f, 2] = jnp.where(upper, re, roll(im, 4))
        return 0

    lax.fori_loop(0, FIELDS, body, 0)


def corner_kernel(zlo, zhi, cup, cdn):
    r = rows()
    for_up = among(r, (3, 6, 7))
    for_dn = among(r, (0, 4, 5))

    def body(q, _):
        for f in range(FIELDS):
            for c in range(2):
                low = zlo[q, f, c]
                high = roll(zhi[q, f, c], 2)
                cup[q, f, c] = jnp.where(for_up, low, high)
                cdn[q, f, c] = jnp.where(for_dn, low, high)
        return 0

    lax.fori_loop(0, PAIRS, body, 0)


(A, AE, AW, AN, AS, AC, GE, GW, G, KE, KW, KN, KS, KZ, HKD, VALID) = range(16)


def solve_kernel(flags, lam, coef, edge, own, rlo, rhi, zlo, zhi, clo, chi, out, x0, x0e, x1, x2, sol):
    r, l = rows(), lanes()
    middle = among(r, (2, 3, 4, 5))
    upper = r < 4
    first, last = r == 0, r == 7
    east = jnp.where(l == 127, 0.0, 0.3).astype(jnp.float32)
    west = jnp.where(l == 0, 0.0, 0.3).astype(jnp.float32)
    near_low = among(r, (2, 3, 6, 7))
    far_low = among(r, (1, 5))
    pick_lo = among(r, (3, 6, 7))
    pick_hi = among(r, (1, 4, 5))

    def pair(q, _):
        m00, m11, m01 = lam[q, 0], lam[q, 1], lam[q, 2]
        di = -0.5 * m01

        def inverse(hkd, valid):
            d0, d1 = hkd + 0.5 * m00, hkd + 0.5 * m11
            inv = 0.8 * valid / (d0 * d1 + di * di)
            return inv * d1, inv * d0, inv * di

        pa, pb, pc = inverse(coef[HKD], coef[VALID])
        ea, eb, ec = inverse(edge[1], edge[2])

        def scale(dest, plane, f, tiles, a, b00, b11, b01):
            re, im = tiles
            if f < 3:
                dest[plane, f, 0] = a * re
                dest[plane, f, 1] = a * im
            else:
                dest[plane, f, 0] = b00 * re + b01 * im
                dest[plane, f, 1] = b11 * im - b01 * re

        a_mid, a_edge = coef[A], edge[0]
        for f in range(FIELDS):
            planes = [[None, None] for _ in range(10)]
            edges = [[None, None] for _ in range(4)]
            for c in range(2):
                for half in range(2):
                    centre = own[q, half, f, c]
                    low, high = rlo[q, half, f, c], rhi[q, half, f, c]
                    near = jnp.where(near_low, low, high)
                    far = jnp.where(far_low, low, high)
                    for odd in range(2):
                        p = 2 * half + odd
                        inner, outer = (6, 2) if odd else (2, 6)
                        planes[3 + p][c] = jnp.where(middle, roll(centre, inner), roll(near, outer))
                        edges[p][c] = roll(far, outer)
                cu, cd = clo[q, f, c], chi[q, f, c]
                lo, hi = zlo[q, f, c], zhi[q, f, c]
                g1 = jnp.where(pick_lo, cu, cd)
                g2 = jnp.where(pick_hi, cu, cd)
                planes[2][c] = jnp.where(middle, roll(lo, 6), roll(g1, 2))
                planes[1][c] = jnp.where(middle, roll(lo, 2), roll(g1, 6))
                planes[7][c] = jnp.where(middle, roll(hi, 2), roll(g2, 4))
                planes[8][c] = jnp.where(middle, roll(hi, 6), g2)
            lo, hi = zlo[q, f, 2], zhi[q, f, 2]
            planes[0] = [roll(lo, 2), roll(lo, 6)]
            planes[9] = [roll(hi, 2), roll(hi, 6)]
            for p in range(10):
                scale(x0, p, f, planes[p], a_mid, pa, pb, pc)
            for p in range(4):
                scale(x0e, p, f, edges[p], a_edge, ea, eb, ec)

        def update(src, at, plane, base, edges=None):
            new = [[None, None] for _ in range(FIELDS)]
            div, flow = [None, None], [None, None]
            for c in range(2):
                cur = [src[plane - at, f, c] for f in range(FIELDS)]
                up = [src[plane - at + 1, f, c] for f in range(FIELDS)]
                dn = [src[plane - at - 1, f, c] for f in range(FIELDS)]
                es = [pltpu.roll(v, 127, 1) for v in cur]
                ws = [pltpu.roll(v, 1, 1) for v in cur]
                if edges is None:
                    ns = [roll(v, 7) for v in cur]
                    ss = [roll(v, 1) for v in cur]
                else:
                    ed = [x0e[edges, f, c] for f in range(FIELDS)]
                    ns = [roll(jnp.where(first, e, v), 7) for e, v in zip(ed, cur)]
                    ss = [roll(jnp.where(last, e, v), 1) for e, v in zip(ed, cur)]
                grad = [
                    coef[GE] * es[3] - coef[GW] * ws[3],
                    coef[G] * (ns[3] - ss[3]),
                    coef[G] * (up[3] - dn[3]),
                ]
                for f in range(3):
                    v = base(plane, f, c, cur[f])
                    v = v + coef[AE] * es[f] + coef[AW] * ws[f]
                    v = v + coef[AN] * ns[f] + coef[AS] * ss[f]
                    new[f][c] = v + coef[AC] * (up[f] + dn[f]) - grad[f]
                flow[c] = (
                    coef[KE] * es[3]
                    + coef[KW] * ws[3]
                    + coef[KN] * ns[3]
                    + coef[KS] * ss[3]
                    + coef[KZ] * (up[3] + dn[3])
                )
                div[c] = east * es[0] - west * ws[0] + 0.3 * ((ns[1] - ss[1]) + (up[2] - dn[2]))
                new[3][c] = base(plane, 3, c, cur[3])
            g0 = flow[0] - (m00 * div[0] + m01 * div[1])
            g1 = flow[1] - (m11 * div[1] - m01 * div[0])
            new[3][0] = new[3][0] + pa * g0 + pc * g1
            new[3][1] = new[3][1] + pb * g1 - pc * g0
            return new

        def later(plane, f, c, cur):
            return x0[plane, f, c] + 0.2 * cur

        def sweep(src, at, dest, dest_at, low, high, base, with_edges):
            for plane in range(low, high):
                inside = 3 <= plane <= 6
                new = update(src, at, plane, base, plane - 3 if with_edges and inside else None)
                keep = flags[0] if plane < 3 else flags[1]
                for f in range(FIELDS):
                    for c in range(2):
                        dest[plane - dest_at, f, c] = new[f][c] if inside else keep * new[f][c]

        sweep(x0, 0, x1, 1, 1, 9, lambda plane, f, c, cur: 1.2 * cur, True)
        sweep(x1, 1, x2, 2, 2, 8, later, False)
        for half in range(2):
            one = update(x2, 2, 3 + 2 * half, later)
            two = update(x2, 2, 4 + 2 * half, later)
            for f in range(FIELDS):
                for c in range(2):
                    sol[q, half, f, c] = jnp.where(upper, roll(one[f][c], 6), roll(two[f][c], 2))
        return 0

    lax.fori_loop(0, PAIRS, pair, 0)

    scale32 = np.float32(1.0 / STEPS)

    def back(f, _):
        for half in range(2):
            tiles = [
                (sol[q, half, f, 0] * scale32, sol[q, half, f, 1] * scale32) for q in range(PAIRS)
            ]
            spec = [(tiles[0][0], None)] + tiles[1:] + [(tiles[0][1], None)]
            for t, v in enumerate(irfft(spec)):
                out[(t // 2) * 2 + half, f, t % 2] = v
        return 0

    lax.fori_loop(0, FIELDS, back, 0)


def call(kernel, outs, in_spaces, scratch=(), limit=16):
    f32 = jnp.float32
    shapes = [jax.ShapeDtypeStruct(s, f32) for s in outs]
    specs = [pl.BlockSpec(memory_space=pltpu.VMEM) for _ in outs]
    single = len(outs) == 1
    return pl.pallas_call(
        kernel,
        out_shape=shapes[0] if single else shapes,
        in_specs=[pl.BlockSpec(memory_space=m) for m in in_spaces],
        out_specs=specs[0] if single else specs,
        scratch_shapes=[pltpu.VMEM(s, f32) for s in scratch],
        compiler_params=pltpu.CompilerParams(vmem_limit_bytes=limit * MIB),
    )


def coefficients(regions, material, block):
    classes = jnp.arange(material.shape[1], dtype=jnp.int32)
    onehot = (regions[None, :, :] == classes[:, None, None]).astype(jnp.float32)
    value = jnp.sum(material[:, :, None, None] * onehot[None], axis=1)
    mean_cols = (value[:, :, :-1] + value[:, :, 1:]) * 0.5
    mean_rows = (value[:, :-1, :] + value[:, 1:, :]) * 0.5
    e = jnp.concatenate([mean_cols, value[:, :, -1:]], axis=2)
    w = jnp.concatenate([value[:, :, :1], mean_cols], axis=2)
    n = jnp.concatenate([mean_rows, value[:, -1:, :]], axis=1)
    s = jnp.concatenate([value[:, :1, :], mean_rows], axis=1)
    shear_diag = e[0] + w[0] + n[0] + s[0] + 2.0 * value[0]
    kappa_diag = e[1] + w[1] + n[1] + s[1] + 2.0 * value[2]
    column = jnp.arange(128, dtype=jnp.int32)[None, :]
    has_e = (column < 127).astype(jnp.float32)
    has_w = (column > 0).astype(jnp.float32)
    a = 0.8 / shear_diag
    one = jnp.ones_like(a)
    table = jnp.stack(
        [
            a, a * e[0] * has_e, a * w[0] * has_w, a * n[0], a * s[0], a * value[0],
            0.3 * a * has_e, 0.3 * a * has_w, 0.3 * a,
            0.5 * e[1] * has_e, 0.5 * w[1] * has_w, 0.5 * n[1], 0.5 * s[1], 0.5 * value[2],
            0.5 * kappa_diag, one,
        ]
    )
    pad = jnp.zeros((16, 4, 128), jnp.float32).at[HKD].set(1.0)
    table = jnp.concatenate([pad, table, pad], axis=1)
    window = lax.dynamic_slice_in_dim(table, 4 * block + 1, 10, axis=1)
    few = jnp.stack([window[A], window[HKD], window[VALID]])
    edge = jnp.concatenate([few[:, 9:10], few[:, 1:7], few[:, 0:1]], axis=1)
    return window[:, 1:9], edge


def lam_table():
    k = np.arange(1, PAIRS)
    real, imag = 1 - np.cos(2 * np.pi * k / STEPS), np.sin(2 * np.pi * k / STEPS)
    rest = np.stack([real, real, -imag], axis=1)
    return np.concatenate([[[0.0, 2.0, 0.0]], rest]).astype(np.float32)


def on_device(sources, regions, material):
    vmem, smem = pltpu.VMEM, pltpu.SMEM
    x = lax.axis_index("xh") * 2 + lax.axis_index("xl")
    y = lax.axis_index("y")
    z = lax.axis_index("z")
    pos = y * 4 + jnp.where(y % 2 == 1, 3 - x, x)
    block = 2 * pos + lax.axis_index("c")
    piece = (32, FIELDS, 2, 8, 128)

    def level(v):
        return lax.all_to_all(v, LEVEL, 0, 0, tiled=True)

    def move(v, dz, db):
        return lax.ppermute(v, AXES, shift(dz, db))

    arrived = level(call(split_kernel, [piece], [vmem])(sources))
    own, zup, zdn = call(
        spectrum_kernel,
        [(PAIRS, 2, FIELDS, 2, 8, 128), (PAIRS, FIELDS, 3, 8, 128), (PAIRS, FIELDS, 3, 8, 128)],
        [vmem],
    )(arrived)
    zlo, zhi = move(zup, 1, 0), move(zdn, -1, 0)
    rlo, rhi = move(own, 0, 1), move(own, 0, -1)
    cup, cdn = call(corner_kernel, [(PAIRS, FIELDS, 2, 8, 128)] * 2, [vmem, vmem])(zlo, zhi)
    clo, chi = move(cup, 0, 1), move(cdn, 0, -1)
    coef, edge = coefficients(regions, material, block)
    flags = jnp.stack([(z > 0), (z < 7)]).astype(jnp.float32)
    answer = call(
        solve_kernel,
        [piece],
        [smem, smem] + [vmem] * 9,
        scratch=[
            (10, FIELDS, 2, 8, 128),
            (4, FIELDS, 2, 8, 128),
            (8, FIELDS, 2, 8, 128),
            (6, FIELDS, 2, 8, 128),
            (PAIRS, 2, FIELDS, 2, 8, 128),
        ],
        limit=24,
    )(flags, jnp.asarray(lam_table()), coef, edge, own, rlo, rhi, zlo, zhi, clo, chi)
    return call(join_kernel, [(FIELDS, 2, 2, 128, 128)], [vmem])(level(answer))


def solution(mesh):
    fine = Mesh(mesh.devices.reshape([SIZES[a] for a in AXES]), AXES)
    spec = P(None, ("xl", "y", "c"), ("z", "xh"), None, None)
    return jax.shard_map(
        on_device, mesh=fine, in_specs=(spec, P(), P()), out_specs=spec, check_vma=False
    )
```

time: 310 us -> 103 us (0.33); the launches traced: 306 us -> 103 us
  waiting for transfers between devices: 174 us -> 21 us
  blocking collectives: 52.5 us -> 28.2 us
  Pallas kernels: 0 us -> 14.9 us
  other arithmetic: 26.8 us -> 13.9 us
  starting transfers between devices: 34.5 us -> 22.5 us
  local copies, waits for them, and re-layouts: 13.2 us -> 2.04 us
  matrix products: 4.42 us -> 0 us
    ppermute x6, waiting for transfers between devices: 130 us -> 10.6 us  [move(): return lax.ppermute(v, AXES, shift(dz, db))]
    all_to_all x2 -> x1, waiting for transfers between devices: 44.4 us -> 10.4 us  [level(): return lax.all_to_all(v, LEVEL, 0, 0, tiled=True)]
    all_to_all x2 -> x1, blocking collectives: 52.5 us -> 28.2 us  [level(): return lax.all_to_all(v, LEVEL, 0, 0, tiled=True)]
    pallas_call x0 -> x5, Pallas kernels: none -> 14.9 us  [the longest x1 10.2 us: on_device(): call(solve_kernel, [piece], [smem, smem] + [vmem] * 9, scratch=[(10, FIEL...]
    unnamed x0 -> x15, other arithmetic: none -> 12.5 us
    concatenate x3 -> x2, other arithmetic: 11.3 us -> 1 us  [the longest x1 0.99 us: coefficients(): table = jnp.concatenate([pad, table, pad], axis=1)]
    ppermute x6, starting transfers between devices: 25.1 us -> 15 us  [move(): return lax.ppermute(v, AXES, shift(dz, db))]
    add x11 -> x0, other arithmetic: 8.77 us -> none  [the longest x3 5.72 us: operate(): momentum = shear_diag * centre[:3] - elastic + BIOT_ALPHA * gradient]
  transfers between devices with their start and end apart: 8 -> 7, of which waited for: 8 -> 4; matrix products, arithmetic and copies ran while one was open for 0% -> 14% of each run, Pallas kernels for 0% -> 1%
where the time goes in v1:
time: 103 us
  blocking collectives  28.2 us (27%)
  starting transfers between devices  22.5 us (22%)
  waiting for transfers between devices  21 us (20%)
  Pallas kernels  14.9 us (14%)
  other arithmetic  13.9 us (13%)
  local copies, waits for them, and re-layouts  2.04 us (2%)
    all_to_all x1, blocking collectives, level(): return lax.all_to_all(v, LEVEL, 0, 0, tiled=True)  28.2 us
    ppermute x6, starting transfers between devices, move(): return lax.ppermute(v, AXES, shift(dz, db))  15 us
    unnamed x15, other arithmetic  12.5 us
    ppermute x6, waiting for transfers between devices, move(): return lax.ppermute(v, AXES, shift(dz, db))  10.6 us
    all_to_all x1, waiting for transfers between devices, level(): return lax.all_to_all(v, LEVEL, 0, 0, tiled=True)  10.4 us
    pallas_call x1, Pallas kernels, on_device(): call(solve_kernel, [piece], [smem, smem] + [vmem] * 9, scratch=[(10, FIEL...  10.2 us
    all_to_all x1, starting transfers between devices, level(): return lax.all_to_all(v, LEVEL, 0, 0, tiled=True)  7.45 us
  transfers between devices with their start and end apart: 7, of which 4 were waited for; matrix products, arithmetic and copies ran while one was open for 14% of the time, Pallas kernels for 1%

profile of v1, /device:TPU:96, one launch (start us, length us, event | category | flops | bytes accessed | tf_op | source)
XLA Modules:
  0.0 102.8 jit_solution(17898106056095222061)
XLA Ops:
  0.0 1.2 %copy-done = f32[4,2,2,128,128]{4,3,2,1,0:T(8,128)S(1)} copy-done((f32[4,2,2,128,128]{4,3,2,1,0:T(8,128)S(1)}, f32[4,2,2,128,128]{4,3,2,1,0:T(8,128)}, u32[]{:S(2)}) %copy-start) | copy-done | bytes 1048600
  1.2 1.2 %shard_map.46 = f32[32,4,2,8,128]{4,3,2,1,0:T(8,128)} custom-call(f32[4,2,2,128,128]{4,3,2,1,0:T(8,128)S(1)} %copy-done), custom_call_target="tpu_custom_call" | custom-call | tf_op jit(solution)/shard_map/pallas_call | solution.py:416
  2.4 7.5 %all-to-all-start = ((f32[32,4,2,8,128]{4,3,2,1,0:T(8,128)}), f32[32,4,2,8,128]{4,3,2,1,0:T(8,128)S(1)}, u32[]{:S(2)}, u32[]{:S(2)}) async-start(f32[32,4,2,8,128]{4,3,2,1,0:T(8,128)} %shard_map.46), calls=%async_computation | async-start | bytes 2097152 | tf_op jit(solution)/shard_map/all_to_all | solution.py:411
  10.4 0.7 constant_dynamic-update-slice_fusion.1
  17.0 10.4 %all-to-all-done.src = f32[32,4,2,8,128]{4,3,2,1,0:T(8,128)S(1)} async-done(((f32[32,4,2,8,128]{4,3,2,1,0:T(8,128)}), f32[32,4,2,8,128]{4,3,2,1,0:T(8,128)S(1)}, u32[]{:S(2)}, u32[]{:S(2)}) %all-to-all-start) | async-done | bytes 1048608 | tf_op jit(solution)/shard_map/all_to_all | solution.py:411
  27.4 1.3 %shard_map.47 = (f32[16,2,4,2,8,128]{5,4,3,2,1,0:T(8,128)S(1)}, f32[16,4,3,8,128]{4,3,2,1,0:T(8,128)}, f32[16,4,3,8,128]{4,3,2,1,0:T(8,128)S(1)}) custom-call(f32[32,4,2,8,128]{4,3,2,1,0:T(8,128)S(1)} %all-to-all-done.src), custom_call_target="tpu_custom_call" | custom-call | tf_op jit(solution)/shard_map/pallas_call | solution.py:417
  28.6 5.0 %collective-permute-start.2 = (f32[16,4,3,8,128]{4,3,2,1,0:T(8,128)}, f32[16,4,3,8,128]{4,3,2,1,0:T(8,128)S(1)}, u32[]{:S(2)}, u32[]{:S(2)}) collective-permute-start(f32[16,4,3,8,128]{4,3,2,1,0:T(8,128)} %get-tuple-element.23), channel_id=1, source_target_pairs={{0,2},{16,18},{128,130},{144,146},{1,3},{17,19},{129,131},{145,147... | collective-permute-start | bytes 2359304 | tf_op jit(solution)/shard_map/ppermute | solution.py:414
  33.7 1.9 %collective-permute-start.3 = (f32[16,4,3,8,128]{4,3,2,1,0:T(8,128)S(1)}, f32[16,4,3,8,128]{4,3,2,1,0:T(8,128)S(1)}, u32[]{:S(2)}, u32[]{:S(2)}) collective-permute-start(f32[16,4,3,8,128]{4,3,2,1,0:T(8,128)S(1)} %get-tuple-element.24), channel_id=1, source_target_pairs={{2,0},{18,16},{130,128},{146,144},{3,1},{19,17},{131,129},{147,145... | collective-permute-start | bytes 2359304 | tf_op jit(solution)/shard_map/ppermute | solution.py:414
  35.6 0.7 multiply_dynamic-update-slice_fusion.4
  36.3 1.5 %multiply_dynamic-update-slice_fusion.3 = (f32[16,128,128]{2,1,0:T(8,128)}, f32[1,128,128]{2,1,0:T(8,128)}) fusion(f32[16,128,128]{2,1,0:T(8,128)} %get-tuple-element.31, f32[3,1,128]{2,1,0:T(1,128)S(1)} %get-tuple-element.42, f32[3,127,128]{2,1,0:T(8,128)} %copy-done.3), kind=kLoop, calls=%fused_computation.23 | loop fusion | flops 32768 | bytes 329216
  37.8 1.3 %collective-permute-start.1 = (f32[16,2,4,2,8,128]{5,4,3,2,1,0:T(8,128)S(1)}, f32[16,2,4,2,8,128]{5,4,3,2,1,0:T(8,128)}, u32[]{:S(2)}, u32[]{:S(2)}) collective-permute-start(f32[16,2,4,2,8,128]{5,4,3,2,1,0:T(8,128)S(1)} %get-tuple-element.22.own), channel_id=1, source_target_pairs={{16,0},{128,16},{144,128},{1,144},{17,1},{129,17},{145,129},{161,1... | collective-permute-start | bytes 3145736 | tf_op jit(solution)/shard_map/ppermute | solution.py:414
  39.1 4.1 %collective-permute-start = (f32[16,2,4,2,8,128]{5,4,3,2,1,0:T(8,128)S(1)}, f32[16,2,4,2,8,128]{5,4,3,2,1,0:T(8,128)}, u32[]{:S(2)}, u32[]{:S(2)}) collective-permute-start(f32[16,2,4,2,8,128]{5,4,3,2,1,0:T(8,128)S(1)} %get-tuple-element.22.own), channel_id=1, source_target_pairs={{0,16},{16,128},{128,144},{144,1},{1,17},{17,129},{129,145},{145,1... | collective-permute-start | bytes 3145736 | tf_op jit(solution)/shard_map/ppermute | solution.py:414
  43.8 1.5 %multiply_dynamic-update-slice_fusion.1 = f32[16,128,128]{2,1,0:T(8,128)} fusion(f32[16,128,128]{2,1,0:T(8,128)} %get-tuple-element.27, f32[3,128,128]{2,1,0:T(8,128)} %copy-done.2), kind=kLoop, calls=%fused_computation.21 | loop fusion | flops 16384 | bytes 131072
  45.3 1.6 %multiply_dynamic-update-slice_fusion = f32[16,128,128]{2,1,0:T(8,128)} fusion(f32[16,128,128]{2,1,0:T(8,128)} %multiply_dynamic-update-slice_fusion.1, f32[1,128,128]{2,1,0:T(8,128)} %get-tuple-element.28, f32[1,128,128]{2,1,0:T(8,128)} %get-tuple-element.30, f32[1,128,128]{2,1,0:T(8,128)S(1)} %get-tuple-element.34, ...), kind=kLoop, calls=%fused_computation.20 | loop fusion | flops 98304 | bytes 393216
  46.9 3.7 %collective-permute-done.2.zlo = f32[16,4,3,8,128]{4,3,2,1,0:T(8,128)S(1)} collective-permute-done((f32[16,4,3,8,128]{4,3,2,1,0:T(8,128)}, f32[16,4,3,8,128]{4,3,2,1,0:T(8,128)S(1)}, u32[]{:S(2)}, u32[]{:S(2)}) %collective-permute-start.2) | collective-permute-done | bytes 786464 | tf_op jit(solution)/shard_map/ppermute | solution.py:414
  50.6 5.0 %collective-permute-done.3.zhi = f32[16,4,3,8,128]{4,3,2,1,0:T(8,128)S(1)} collective-permute-done((f32[16,4,3,8,128]{4,3,2,1,0:T(8,128)S(1)}, f32[16,4,3,8,128]{4,3,2,1,0:T(8,128)S(1)}, u32[]{:S(2)}, u32[]{:S(2)}) %collective-permute-start.3) | collective-permute-done | bytes 786464 | tf_op jit(solution)/shard_map/ppermute | solution.py:414
  55.6 1.1 %shard_map.48 = (f32[16,4,2,8,128]{4,3,2,1,0:T(8,128)}, f32[16,4,2,8,128]{4,3,2,1,0:T(8,128)}) custom-call(f32[16,4,3,8,128]{4,3,2,1,0:T(8,128)S(1)} %collective-permute-done.2.zlo, f32[16,4,3,8,128]{4,3,2,1,0:T(8,128)S(1)} %collective-permute-done.3.zhi), custom_call_target="tpu_custom_call" | custom-call | tf_op jit(solution)/shard_map/pallas_call | solution.py:424
  56.7 1.4 %collective-permute-start.4 = (f32[16,4,2,8,128]{4,3,2,1,0:T(8,128)}, f32[16,4,2,8,128]{4,3,2,1,0:T(8,128)S(1)}, u32[]{:S(2)}, u32[]{:S(2)}) collective-permute-start(f32[16,4,2,8,128]{4,3,2,1,0:T(8,128)} %get-tuple-element.25), channel_id=1, source_target_pairs={{0,16},{16,128},{128,144},{144,1},{1,17},{17,129},{129,145},{145,1... | collective-permute-start | bytes 1572872 | tf_op jit(solution)/shard_map/ppermute | solution.py:414
  58.2 1.3 %collective-permute-start.5 = (f32[16,4,2,8,128]{4,3,2,1,0:T(8,128)}, f32[16,4,2,8,128]{4,3,2,1,0:T(8,128)}, u32[]{:S(2)}, u32[]{:S(2)}) collective-permute-start(f32[16,4,2,8,128]{4,3,2,1,0:T(8,128)} %get-tuple-element.26), channel_id=1, source_target_pairs={{16,0},{128,16},{144,128},{1,144},{17,1},{129,17},{145,129},{161,1... | collective-permute-start | bytes 1572872 | tf_op jit(solution)/shard_map/ppermute | solution.py:414
  60.1 1.0 fusion.4
  61.3 1.9 %collective-permute-done.5.chi = f32[16,4,2,8,128]{4,3,2,1,0:T(8,128)} collective-permute-done((f32[16,4,2,8,128]{4,3,2,1,0:T(8,128)}, f32[16,4,2,8,128]{4,3,2,1,0:T(8,128)}, u32[]{:S(2)}, u32[]{:S(2)}) %collective-permute-start.5) | collective-permute-done | bytes 524320 | tf_op jit(solution)/shard_map/ppermute | solution.py:414
  63.2 10.2 %shard_map.49 = f32[32,4,2,8,128]{4,3,2,1,0:T(8,128)S(1)} custom-call(f32[2]{0:T(128)S(1)} %add_convert_fusion.flags, f32[16,3]{1,0:T(8,128)S(1)} %copy-done.1, f32[16,8,128]{2,1,0:T(8,128)S(1)} %slice.137.coef, f32[3,8,128]{2,1,0:T(8,128)S(1)} %fusion.6.edge, f32[16,2,4,2,8,128]{5,4,3,2,1,0:T(8,128)S(1)} %get-tuple-element.22.own, ...), custom_call_target="tpu_custom_call" | custom-call | tf_op jit(solution)/shard_map/pallas_call | solution.py:428
  73.4 28.2 %all_to_all.10.src = f32[32,4,2,8,128]{4,3,2,1,0:T(8,128)S(1)} all-to-all(f32[32,4,2,8,128]{4,3,2,1,0:T(8,128)S(1)} %shard_map.49), channel_id=1, replica_groups=mesh['xl'=2,'y'=4,'c'=2,'z'=8,'xh'=2] {'xl','y','c','xh'}, dimensions={0} | all-to-all | bytes 2097152 | tf_op jit(solution)/shard_map/all_to_all | solution.py:411
  101.6 1.2 %shard_map.50 = f32[4,2,2,128,128]{4,3,2,1,0:T(8,128)} custom-call(f32[32,4,2,8,128]{4,3,2,1,0:T(8,128)S(1)} %all_to_all.10.src), custom_call_target="tpu_custom_call" | custom-call | tf_op jit(solution)/shard_map/pallas_call | solution.py:441
  (54 shorter events, 7.7 us)
Async XLA Ops:
  0.0 1.2 %copy-start = (f32[4,2,2,128,128]{4,3,2,1,0:T(8,128)S(1)}, f32[4,2,2,128,128]{4,3,2,1,0:T(8,128)}, u32[]{:S(2)}) copy-start(f32[4,2,2,128,128]{4,3,2,1,0:T(8,128)} %src.1) | copy-start | bytes 3145732
  2.4 7.5 %copy-start.9 = (s32[128,128]{1,0:T(8,128)S(1)}, s32[128,128]{1,0:T(8,128)}, u32[]{:S(2)}) copy-start(s32[128,128]{1,0:T(8,128)} %param.7) | copy-start | bytes 196612
  2.4 7.5 %copy-start.11 = (f32[3,4]{1,0:T(4,128)S(1)}, f32[3,4]{1,0:T(4,128)}, u32[]{:S(2)}) copy-start(f32[3,4]{1,0:T(4,128)} %param.8) | copy-start | bytes 148
  2.4 25.0 %all-to-all-start = ((f32[32,4,2,8,128]{4,3,2,1,0:T(8,128)}), f32[32,4,2,8,128]{4,3,2,1,0:T(8,128)S(1)}, u32[]{:S(2)}, u32[]{:S(2)}) async-start(f32[32,4,2,8,128]{4,3,2,1,0:T(8,128)} %shard_map.46), calls=%async_computation | async-start | bytes 2097152 | tf_op jit(solution)/shard_map/all_to_all | solution.py:411
  10.1 3.6 %copy-start.2 = (f32[3,128,128]{2,1,0:T(8,128)}, f32[3,128,128]{2,1,0:T(8,128)S(1)}, u32[]{:S(2)}) copy-start(f32[3,128,128]{2,1,0:T(8,128)S(1)} %multiply_reduce_fusion) | copy-start | bytes 589828
  10.1 1.0 copy-start.3
  10.3 6.0 %copy-start.5 = (f32[3,128,127]{2,1,0:T(8,128)}, f32[3,128,127]{2,1,0:T(8,128)S(1)}, u32[]{:S(2)}) copy-start(f32[3,128,127]{2,1,0:T(8,128)S(1)} %fusion.2) | copy-start | bytes 585220
  10.4 4.0 %copy-start.7 = (f32[3,128,1]{2,1,0:T(8,128)}, f32[3,128,1]{2,1,0:T(8,128)S(1)}, u32[]{:S(2)}) copy-start(f32[3,128,1]{2,1,0:T(8,128)S(1)} %get-tuple-element.44) | copy-start | bytes 4612
  27.4 8.2 %copy-start.6 = (f32[3,128,127]{2,1,0:T(8,128)S(1)}, f32[3,128,127]{2,1,0:T(8,128)}, u32[]{:S(2)}) copy-start(f32[3,128,127]{2,1,0:T(8,128)} %copy-done.5) | copy-start | bytes 585220
  27.4 8.2 %copy-start.8 = (f32[3,128,1]{2,1,0:T(8,128)S(1)}, f32[3,128,1]{2,1,0:T(8,128)}, u32[]{:S(2)}) copy-start(f32[3,128,1]{2,1,0:T(8,128)} %copy-done.7) | copy-start | bytes 4612
  27.4 15.8 %copy-start.4 = (f32[3,127,128]{2,1,0:T(8,128)S(1)}, f32[3,127,128]{2,1,0:T(8,128)}, u32[]{:S(2)}) copy-start(f32[3,127,128]{2,1,0:T(8,128)} %copy-done.3) | copy-start | bytes 585220
  28.6 22.0 %collective-permute-start.2 = (f32[16,4,3,8,128]{4,3,2,1,0:T(8,128)}, f32[16,4,3,8,128]{4,3,2,1,0:T(8,128)S(1)}, u32[]{:S(2)}, u32[]{:S(2)}) collective-permute-start(f32[16,4,3,8,128]{4,3,2,1,0:T(8,128)} %get-tuple-element.23), channel_id=1, source_target_pairs={{0,2},{16,18},{128,130},{144,146},{1,3},{17,19},{129,131},{145,147... | collective-permute-start | bytes 2359304 | tf_op jit(solution)/shard_map/ppermute | solution.py:414
  33.7 22.0 %collective-permute-start.3 = (f32[16,4,3,8,128]{4,3,2,1,0:T(8,128)S(1)}, f32[16,4,3,8,128]{4,3,2,1,0:T(8,128)S(1)}, u32[]{:S(2)}, u32[]{:S(2)}) collective-permute-start(f32[16,4,3,8,128]{4,3,2,1,0:T(8,128)S(1)} %get-tuple-element.24), channel_id=1, source_target_pairs={{2,0},{18,16},{130,128},{146,144},{3,1},{19,17},{131,129},{147,145... | collective-permute-start | bytes 2359304 | tf_op jit(solution)/shard_map/ppermute | solution.py:414
  37.8 23.4 %collective-permute-start.1 = (f32[16,2,4,2,8,128]{5,4,3,2,1,0:T(8,128)S(1)}, f32[16,2,4,2,8,128]{5,4,3,2,1,0:T(8,128)}, u32[]{:S(2)}, u32[]{:S(2)}) collective-permute-start(f32[16,2,4,2,8,128]{5,4,3,2,1,0:T(8,128)S(1)} %get-tuple-element.22.own), channel_id=1, source_target_pairs={{16,0},{128,16},{144,128},{1,144},{17,1},{129,17},{145,129},{161,1... | collective-permute-start | bytes 3145736 | tf_op jit(solution)/shard_map/ppermute | solution.py:414
  39.1 22.2 %collective-permute-start = (f32[16,2,4,2,8,128]{5,4,3,2,1,0:T(8,128)S(1)}, f32[16,2,4,2,8,128]{5,4,3,2,1,0:T(8,128)}, u32[]{:S(2)}, u32[]{:S(2)}) collective-permute-start(f32[16,2,4,2,8,128]{5,4,3,2,1,0:T(8,128)S(1)} %get-tuple-element.22.own), channel_id=1, source_target_pairs={{0,16},{16,128},{128,144},{144,1},{1,17},{17,129},{129,145},{145,1... | collective-permute-start | bytes 3145736 | tf_op jit(solution)/shard_map/ppermute | solution.py:414
  45.3 14.8 %copy-start.10 = (f32[16,4,128]{2,1,0:T(4,128)S(1)}, f32[16,4,128]{2,1,0:T(4,128)}, u32[]{:S(2)}) copy-start(f32[16,4,128]{2,1,0:T(4,128)} %constant.83.clone.1) | copy-start | bytes 98308
  56.7 6.4 %copy-start.1 = (f32[16,3]{1,0:T(8,128)S(1)}, f32[16,3]{1,0:T(8,128)}, u32[]{:S(2)}) copy-start(f32[16,3]{1,0:T(8,128)} %constant.99.clone.lam) | copy-start | bytes 580
  56.7 4.5 %collective-permute-start.4 = (f32[16,4,2,8,128]{4,3,2,1,0:T(8,128)}, f32[16,4,2,8,128]{4,3,2,1,0:T(8,128)S(1)}, u32[]{:S(2)}, u32[]{:S(2)}) collective-permute-start(f32[16,4,2,8,128]{4,3,2,1,0:T(8,128)} %get-tuple-element.25), channel_id=1, source_target_pairs={{0,16},{16,128},{128,144},{144,1},{1,17},{17,129},{129,145},{145,1... | collective-permute-start | bytes 1572872 | tf_op jit(solution)/shard_map/ppermute | solution.py:414
  58.2 5.0 %collective-permute-start.5 = (f32[16,4,2,8,128]{4,3,2,1,0:T(8,128)}, f32[16,4,2,8,128]{4,3,2,1,0:T(8,128)}, u32[]{:S(2)}, u32[]{:S(2)}) collective-permute-start(f32[16,4,2,8,128]{4,3,2,1,0:T(8,128)} %get-tuple-element.26), channel_id=1, source_target_pairs={{16,0},{128,16},{144,128},{1,144},{17,1},{129,17},{145,129},{161,1... | collective-permute-start | bytes 1572872 | tf_op jit(solution)/shard_map/ppermute | solution.py:414

commit v2 on v1

v2 whole, which is shorter than its diff:
```python
import functools
import math

import jax
import jax.numpy as jnp
import numpy as np
from jax import lax
from jax.experimental import pallas as pl
from jax.experimental.pallas import tpu as pltpu
from jax.sharding import Mesh
from jax.sharding import PartitionSpec as P

AXES = ("xl", "y", "c", "z", "xh")
SIZES = dict(xl=2, y=4, c=2, z=8, xh=2)
LEVEL = ("xl", "y", "c", "xh")
STEPS = 32
PAIRS = 16
FIELDS = 4
MIB = 1 << 20


def chip_at(pos):
    y, x = divmod(pos, 4)
    return (3 - x if y % 2 else x), y


def level_index(pos, core):
    x, y = chip_at(pos)
    return ((((x % 2) * 4 + y) * 2 + core) * 2) + x // 2


def device_index(z, block):
    x, y = chip_at(block // 2)
    return ((((x % 2) * 4 + y) * 2 + block % 2) * 8 + z) * 2 + x // 2


def level_swap(parity):
    low = [z for z in range(7) if z % 2 == parity]
    up = [(device_index(z, b), device_index(z + 1, b)) for z in low for b in range(32)]
    return up + [(t, s) for s, t in up]


def block_swap(parity):
    low = [b for b in range(31) if b % 2 == parity]
    up = [(device_index(z, b), device_index(z, b + 1)) for z in range(8) for b in low]
    return up + [(t, s) for s, t in up]


def rows():
    return lax.broadcasted_iota(jnp.int32, (8, 128), 0)


def lanes():
    return lax.broadcasted_iota(jnp.int32, (8, 128), 1)


def among(index, members):
    mask = index == members[0]
    for member in members[1:]:
        mask = mask | (index == member)
    return mask


def roll(tile, amount):
    amount %= 8
    return tile if amount == 0 else pltpu.roll(tile, amount, 0)


def mul_const(re, im, cr, ci):
    def axpy(a, x, b, y):
        terms = []
        for k, v in ((a, x), (b, y)):
            if abs(k) > 1e-12:
                terms.append((k, v))
        total = None
        for k, v in terms:
            if total is None:
                total = v if abs(k - 1) < 1e-12 else (-v if abs(k + 1) < 1e-12 else v * np.float32(k))
            elif abs(k - 1) < 1e-12:
                total = total + v
            elif abs(k + 1) < 1e-12:
                total = total - v
            else:
                total = total + v * np.float32(k)
        return total

    if abs(abs(cr) - abs(ci)) < 1e-12:
        root = np.float32(abs(cr))
        sr, si = math.copysign(1, cr), math.copysign(1, ci)
        return axpy(sr, re * root, -si, im * root), axpy(si, re * root, sr, im * root)
    return axpy(cr, re, -ci, im), axpy(ci, re, cr, im)


def rfft(x):
    n = len(x)
    if n == 2:
        return [(x[0] + x[1], None), (x[0] - x[1], None)]
    even, odd = rfft(x[0::2]), rfft(x[1::2])
    out = [None] * (n // 2 + 1)
    out[0] = (even[0][0] + odd[0][0], None)
    out[n // 2] = (even[0][0] - odd[0][0], None)
    out[n // 4] = (even[n // 4][0], -odd[n // 4][0])
    for k in range(1, n // 4):
        angle = -2 * math.pi * k / n
        tr, ti = mul_const(*odd[k], math.cos(angle), math.sin(angle))
        er, ei = even[k]
        out[k] = (er + tr, ei + ti)
        out[n // 2 - k] = (er - tr, ti - ei)
    return out


def irfft(spec):
    n = 2 * (len(spec) - 1)
    if n == 2:
        return [spec[0][0] + spec[1][0], spec[0][0] - spec[1][0]]
    q = n // 4
    even, odd = [None] * (q + 1), [None] * (q + 1)
    even[0] = (spec[0][0] + spec[2 * q][0], None)
    odd[0] = (spec[0][0] - spec[2 * q][0], None)
    even[q] = (2.0 * spec[q][0], None)
    odd[q] = (-2.0 * spec[q][1], None)
    for k in range(1, q):
        ar, ai = spec[k]
        br, bi = spec[2 * q - k]
        even[k] = (ar + br, ai - bi)
        angle = 2 * math.pi * k / n
        odd[k] = mul_const(ar - br, ai + bi, math.cos(angle), math.sin(angle))
    a, b = irfft(even), irfft(odd)
    return [v for two in zip(a, b) for v in two]


def split_kernel(src, out):
    upper = rows() < 4

    def body(i, _):
        f, t = i // 2, i % 2
        for pos in range(16):
            a = src[f, t, 0, pl.ds(8 * pos, 8), :]
            b = src[f, t, 1, pl.ds(8 * pos, 8), :]
            out[level_index(pos, 0), f, t] = jnp.where(upper, a, roll(b, 4))
            out[level_index(pos, 1), f, t] = jnp.where(upper, roll(a, 4), b)
        return 0

    lax.fori_loop(0, 8, body, 0)


def join_kernel(src, out):
    upper = rows() < 4

    def body(i, _):
        f, t = i // 2, i % 2
        for pos in range(16):
            a = src[level_index(pos, 0), f, t]
            b = src[level_index(pos, 1), f, t]
            out[f, t, 0, pl.ds(8 * pos, 8), :] = jnp.where(upper, a, roll(b, 4))
            out[f, t, 1, pl.ds(8 * pos, 8), :] = jnp.where(upper, roll(a, 4), b)
        return 0

    lax.fori_loop(0, 8, body, 0)


def spectrum_kernel(place, src, own, even, odd):
    r = rows()
    upper = r < 4
    on_even = (r * 0 + place[0]) == 0

    def body(f, _):
        for half in range(2):
            spec = rfft([src[(t // 2) * 2 + half, f, t % 2] for t in range(STEPS)])
            pairs = [(spec[0][0], spec[16][0])] + spec[1:16]
            for q in range(PAIRS):
                for c in range(2):
                    own[q, half, f, c] = pairs[q][c]
        return 0

    lax.fori_loop(0, FIELDS, body, 0)

    def messages(q, _):
        for f in range(FIELDS):
            low = [own[q, 0, f, c] for c in range(2)]
            high = [own[q, 1, f, c] for c in range(2)]
            up = high + [jnp.where(upper, roll(low[0], 4), low[1])]
            down = low + [jnp.where(upper, high[0], roll(high[1], 4))]
            for n in range(3):
                even[q, f, n] = jnp.where(on_even, up[n], down[n])
                odd[q, f, n] = jnp.where(on_even, down[n], up[n])
        return 0

    lax.fori_loop(0, PAIRS, messages, 0)


def corner_kernel(place, even, odd, inside, across):
    r = rows()
    on_even = (r * 0 + place[0]) == 0
    for_next = jnp.where(among(r, (3, 6, 7)), 1, 0)
    for_last = jnp.where(among(r, (0, 4, 5)), 1, 0)
    first_core = (r * 0 + place[1]) == 0
    for_inside = jnp.where(first_core, for_next, for_last) == 1
    for_across = jnp.where(first_core, for_last, for_next) == 1

    def body(q, _):
        for f in range(FIELDS):
            for c in range(2):
                a, b = even[q, f, c], odd[q, f, c]
                low = jnp.where(on_even, b, a)
                high = roll(jnp.where(on_even, a, b), 2)
                inside[q, f, c] = jnp.where(for_inside, low, high)
                across[q, f, c] = jnp.where(for_across, low, high)
        return 0

    lax.fori_loop(0, PAIRS, body, 0)


(A, AE, AW, AN, AS, AC, GE, GW, G, KE, KW, KN, KS, KZ, HKD, VALID) = range(16)


def coefficient_kernel(first_row, material, near, coef, edge):
    shape = (16, 128)
    line = first_row[0] - 4 + lax.broadcasted_iota(jnp.int32, shape, 0)
    column = lax.broadcasted_iota(jnp.int32, shape, 1)
    there = [column < 127, column > 0, line < 127, line > 0]
    has_e, has_w = [jnp.where(t, 1.0, 0.0).astype(jnp.float32) for t in there[:2]]
    valid = jnp.where((line >= 0) & (line <= 127), 1.0, 0.0).astype(jnp.float32)
    classes = near[...]

    def parts(row):
        value = jnp.zeros(shape, jnp.float32)
        for m in range(4):
            value = jnp.where(classes == m, material[row, m], value)
        moved = [pltpu.roll(value, 127, 1), pltpu.roll(value, 1, 1), pltpu.roll(value, 15, 0), pltpu.roll(value, 1, 0)]
        return value, [jnp.where(t, (value + v) * 0.5, value) for t, v in zip(there, moved)]

    shear, (se, sw, sn, ss) = parts(0)
    _, (ke, kw, kn, ks) = parts(1)
    axial, _ = parts(2)
    a = 0.8 * valid / (se + sw + sn + ss + 2.0 * shear)
    half = 0.5 * valid
    table = [
        a, a * se * has_e, a * sw * has_w, a * sn, a * ss, a * shear,
        0.3 * a * has_e, 0.3 * a * has_w, 0.3 * a,
        half * ke * has_e, half * kw * has_w, half * kn, half * ks, half * axial,
        0.5 * (ke + kw + kn + ks + 2.0 * axial), valid,
    ]
    for n, v in enumerate(table):
        turned = pltpu.roll(v, 14, 0)
        coef[n] = turned[:8]
        if n in (A, HKD, VALID):
            edge[(A, HKD, VALID).index(n)] = turned[8:]


def inverse_diagonal(lam, q, half_diag, valid):
    d0, d1, di = half_diag + 0.5 * lam[q, 0], half_diag + 0.5 * lam[q, 1], -0.5 * lam[q, 2]
    inv = 0.8 * valid / (d0 * d1 + di * di)
    return inv * d1, inv * d0, inv * di


def first_iterate(f, tiles, a, diagonal):
    re, im = tiles
    if f < 3:
        return a * re, a * im
    b00, b11, b01 = diagonal
    return b00 * re + b01 * im, b11 * im - b01 * re


def updater(lam, q, coef, diagonal):
    l = lanes()
    east = jnp.where(l == 127, 0.0, 0.3).astype(jnp.float32)
    west = jnp.where(l == 0, 0.0, 0.3).astype(jnp.float32)
    m00, m11, m01 = lam[q, 0], lam[q, 1], lam[q, 2]
    pa, pb, pc = diagonal

    def update(cur, up, dn, base, north=None, south=None):
        north, south = north or cur, south or cur
        new = [[None, None] for _ in range(FIELDS)]
        div, flow = [None, None], [None, None]
        for c in range(2):
            es = [pltpu.roll(cur[f][c], 127, 1) for f in range(FIELDS)]
            ws = [pltpu.roll(cur[f][c], 1, 1) for f in range(FIELDS)]
            ns = [roll(north[f][c], 7) for f in range(FIELDS)]
            ss = [roll(south[f][c], 1) for f in range(FIELDS)]
            grad = [
                coef[GE] * es[3] - coef[GW] * ws[3],
                coef[G] * (ns[3] - ss[3]),
                coef[G] * (up[3][c] - dn[3][c]),
            ]
            for f in range(3):
                v = base(f, c) + coef[AE] * es[f] + coef[AW] * ws[f]
                v = v + coef[AN] * ns[f] + coef[AS] * ss[f]
                new[f][c] = v + coef[AC] * (up[f][c] + dn[f][c]) - grad[f]
            flow[c] = (
                coef[KE] * es[3]
                + coef[KW] * ws[3]
                + coef[KN] * ns[3]
                + coef[KS] * ss[3]
                + coef[KZ] * (up[3][c] + dn[3][c])
            )
            div[c] = east * es[0] - west * ws[0] + 0.3 * ((ns[1] - ss[1]) + (up[2][c] - dn[2][c]))
        g0 = flow[0] - (m00 * div[0] + m01 * div[1])
        g1 = flow[1] - (m11 * div[1] - m01 * div[0])
        new[3][0] = base(3, 0) + pa * g0 + pc * g1
        new[3][1] = base(3, 1) + pb * g1 - pc * g0
        return new

    return update


def plane(ref, *index):
    return [[ref[(*index, f, c)] for c in range(2)] for f in range(FIELDS)]


def inner_kernel(place, lam, coef, edge, own, inside, across, x0, x1):
    r = rows()
    middle = among(r, (2, 3, 4, 5))
    first, last = r == 0, r == 7
    bit = (r ^ (2 * place[1])) & 2
    near_across, far_across = bit != 0, bit == 0

    def pair(q, _):
        diagonal = inverse_diagonal(lam, q, coef[HKD], coef[VALID])
        edge_diagonal = inverse_diagonal(lam, q, edge[1], edge[2])
        update = updater(lam, q, coef, diagonal)
        start = [[None] * FIELDS for _ in range(4)]
        edges = [[None] * FIELDS for _ in range(4)]
        for f in range(FIELDS):
            tiles = [[None, None] for _ in range(4)]
            far_tiles = [[None, None] for _ in range(4)]
            for c in range(2):
                for half in range(2):
                    centre = own[q, half, f, c]
                    a, b = across[q, half, f, c], inside[q, half, f, c]
                    near = jnp.where(near_across, a, b)
                    far = jnp.where(far_across, a, b)
                    for odd in range(2):
                        p = 2 * half + odd
                        inner, other = (6, 2) if odd else (2, 6)
                        tiles[p][c] = jnp.where(middle, roll(centre, inner), roll(near, other))
                        far_tiles[p][c] = roll(far, other)
            for p in range(4):
                start[p][f] = first_iterate(f, tiles[p], coef[A], diagonal)
                edges[p][f] = first_iterate(f, far_tiles[p], edge[0], edge_diagonal)
                for c in range(2):
                    x0[q, p, f, c] = start[p][f][c]
        none = [[0.0, 0.0]] * FIELDS
        for p in range(4):
            cur = plane(x0, q, p)
            up = plane(x0, q, p + 1) if p < 3 else none
            dn = plane(x0, q, p - 1) if p > 0 else none
            north = [[jnp.where(first, edges[p][f][c], cur[f][c]) for c in range(2)] for f in range(FIELDS)]
            south = [[jnp.where(last, edges[p][f][c], cur[f][c]) for c in range(2)] for f in range(FIELDS)]
            new = update(cur, up, dn, lambda f, c: 1.2 * cur[f][c], north, south)
            for f in range(FIELDS):
                for c in range(2):
                    x1[q, p, f, c] = new[f][c]
        return 0

    lax.fori_loop(0, PAIRS, pair, 0)


def solve_kernel(place, flags, lam, coef, even, odd, inside, across, start, second, out, xz, x1, x2, sol):
    r = rows()
    middle = among(r, (2, 3, 4, 5))
    upper = r < 4
    on_even = (r * 0 + place[0]) == 0
    core = r * 0 + place[1]
    pick_lo = (jnp.where(among(r, (3, 6, 7)), 1, 0) ^ core) == 1
    pick_hi = (jnp.where(among(r, (1, 4, 5)), 1, 0) ^ core) == 1

    def pair(q, _):
        m00, m11, m01 = lam[q, 0], lam[q, 1], lam[q, 2]
        diagonal = inverse_diagonal(lam, q, coef[HKD], coef[VALID])
        pa, pb, pc = diagonal
        update = updater(lam, q, coef, diagonal)
        for f in range(FIELDS):
            tiles = [[None, None] for _ in range(6)]
            for c in range(2):
                a, b = even[q, f, c], odd[q, f, c]
                lo, hi = jnp.where(on_even, b, a), jnp.where(on_even, a, b)
                a, b = across[q, f, c], inside[q, f, c]
                g1 = jnp.where(pick_lo, a, b)
                g2 = jnp.where(pick_hi, a, b)
                tiles[2][c] = jnp.where(middle, roll(lo, 6), roll(g1, 2))
                tiles[1][c] = jnp.where(middle, roll(lo, 2), roll(g1, 6))
                tiles[3][c] = jnp.where(middle, roll(hi, 2), roll(g2, 4))
                tiles[4][c] = jnp.where(middle, roll(hi, 6), g2)
            a, b = even[q, f, 2], odd[q, f, 2]
            lo, hi = jnp.where(on_even, b, a), jnp.where(on_even, a, b)
            tiles[0] = [roll(lo, 2), roll(lo, 6)]
            tiles[5] = [roll(hi, 2), roll(hi, 6)]
            for p in range(6):
                xz[p, f, 0], xz[p, f, 1] = first_iterate(f, tiles[p], coef[A], diagonal)

        def x0_at(p):
            if 0 <= p < 4:
                return plane(start, q, p)
            return plane(xz, p + 3 if p < 0 else p - 1)

        for p in (-2, -1, 4, 5):
            cur = x0_at(p)
            new = update(cur, x0_at(p + 1), x0_at(p - 1), lambda f, c: 1.2 * cur[f][c])
            keep = flags[0] if p < 0 else flags[1]
            for f in range(FIELDS):
                for c in range(2):
                    x1[p + 2, f, c] = keep * new[f][c]
        for p in (1, 2):
            for f in range(FIELDS):
                for c in range(2):
                    x1[p + 2, f, c] = second[q, p, f, c]
        for p, sign in ((0, -1.0), (3, 1.0)):
            side = x0_at(p + int(sign))
            for c in range(2):
                for f in range(3):
                    v = second[q, p, f, c] + coef[AC] * side[f][c]
                    if f == 2:
                        v = v - (sign * coef[G]) * side[3][c]
                    x1[p + 2, f, c] = v
            flow = [coef[KZ] * side[3][c] for c in range(2)]
            div = [(sign * 0.3) * side[2][c] for c in range(2)]
            g0 = flow[0] - (m00 * div[0] + m01 * div[1])
            g1 = flow[1] - (m11 * div[1] - m01 * div[0])
            x1[p + 2, 3, 0] = second[q, p, 3, 0] + pa * g0 + pc * g1
            x1[p + 2, 3, 1] = second[q, p, 3, 1] + pb * g1 - pc * g0

        for p in range(-1, 5):
            cur, base = plane(x1, p + 2), x0_at(p)
            new = update(cur, plane(x1, p + 3), plane(x1, p + 1), lambda f, c: base[f][c] + 0.2 * cur[f][c])
            for f in range(FIELDS):
                for c in range(2):
                    v = new[f][c]
                    if p < 0:
                        v = flags[0] * v
                    if p > 3:
                        v = flags[1] * v
                    x2[p + 1, f, c] = v
        for half in range(2):
            two = []
            for p in (2 * half, 2 * half + 1):
                cur, base = plane(x2, p + 1), x0_at(p)
                two.append(
                    update(cur, plane(x2, p + 2), plane(x2, p), lambda f, c: base[f][c] + 0.2 * cur[f][c])
                )
            for f in range(FIELDS):
                for c in range(2):
                    sol[q, half, f, c] = jnp.where(upper, roll(two[0][f][c], 6), roll(two[1][f][c], 2))
        return 0

    lax.fori_loop(0, PAIRS, pair, 0)

    scale32 = np.float32(1.0 / STEPS)

    def back(f, _):
        for half in range(2):
            tiles = [
                (sol[q, half, f, 0] * scale32, sol[q, half, f, 1] * scale32) for q in range(PAIRS)
            ]
            spec = [(tiles[0][0], None)] + tiles[1:] + [(tiles[0][1], None)]
            for t, v in enumerate(irfft(spec)):
                out[(t // 2) * 2 + half, f, t % 2] = v
        return 0

    lax.fori_loop(0, FIELDS, back, 0)


def call(kernel, outs, in_spaces, scratch=(), limit=4, micros=1):
    f32 = jnp.float32
    shapes = [jax.ShapeDtypeStruct(s, f32) for s in outs]
    specs = [pl.BlockSpec(memory_space=pltpu.VMEM) for _ in outs]
    single = len(outs) == 1
    return pl.pallas_call(
        kernel,
        out_shape=shapes[0] if single else shapes,
        in_specs=[pl.BlockSpec(memory_space=m) for m in in_spaces],
        out_specs=specs[0] if single else specs,
        scratch_shapes=[pltpu.VMEM(s, f32) for s in scratch],
        compiler_params=pltpu.CompilerParams(vmem_limit_bytes=limit * MIB),
        cost_estimate=pl.CostEstimate(flops=0, bytes_accessed=int(micros * 3.69e6), transcendentals=0),
    )


def lam_table():
    k = np.arange(1, PAIRS)
    real, imag = 1 - np.cos(2 * np.pi * k / STEPS), np.sin(2 * np.pi * k / STEPS)
    rest = np.stack([real, real, -imag], axis=1)
    return np.concatenate([[[0.0, 2.0, 0.0]], rest]).astype(np.float32)


def on_device(sources, regions, material):
    vmem, smem = pltpu.VMEM, pltpu.SMEM
    x = lax.axis_index("xh") * 2 + lax.axis_index("xl")
    y = lax.axis_index("y")
    z = lax.axis_index("z")
    pos = y * 4 + jnp.where(y % 2 == 1, 3 - x, x)
    block = 2 * pos + lax.axis_index("c")
    piece = (32, FIELDS, 2, 8, 128)

    def level(v):
        return lax.all_to_all(v, LEVEL, 0, 0, tiled=True)

    def swap(v, pairs):
        return lax.ppermute(v, AXES, pairs)

    arrived = level(call(split_kernel, [piece], [vmem])(sources))
    first_row = 4 * block
    wide = jnp.concatenate([regions[:8], regions, regions[:8]], axis=0)
    near = lax.dynamic_slice_in_dim(wide, first_row + 4, 16, axis=0)
    coef, edge = call(coefficient_kernel, [(16, 8, 128), (3, 8, 128)], [smem, smem, vmem])(
        first_row.astype(jnp.int32).reshape(1), material, near
    )
    place = jnp.stack([z % 2, lax.axis_index("c")]).astype(jnp.int32)
    flags = jnp.stack([(z > 0), (z < 7)]).astype(jnp.float32)
    arrived, coef, edge, place, flags = lax.optimization_barrier((arrived, coef, edge, place, flags))
    lam = jnp.asarray(lam_table())
    own, even, odd = call(
        spectrum_kernel,
        [(PAIRS, 2, FIELDS, 2, 8, 128)] + [(PAIRS, FIELDS, 3, 8, 128)] * 2,
        [smem, vmem],
        limit=8,
    )(place, arrived)
    even, odd = swap(even, level_swap(0)), swap(odd, level_swap(1))
    inside, across = swap(own, block_swap(0)), swap(own, block_swap(1))
    start, second = call(
        inner_kernel,
        [(PAIRS, 4, FIELDS, 2, 8, 128)] * 2,
        [smem, smem] + [vmem] * 5,
        limit=10,
        micros=5,
    )(place, lam, coef, edge, own, inside, across)
    corners = call(corner_kernel, [(PAIRS, FIELDS, 2, 8, 128)] * 2, [smem, vmem, vmem])(place, even, odd)
    inside, across = swap(corners[0], block_swap(0)), swap(corners[1], block_swap(1))
    answer = call(
        solve_kernel,
        [piece],
        [smem] * 3 + [vmem] * 7,
        scratch=[
            (6, FIELDS, 2, 8, 128),
            (8, FIELDS, 2, 8, 128),
            (6, FIELDS, 2, 8, 128),
            (PAIRS, 2, FIELDS, 2, 8, 128),
        ],
        limit=14,
    )(place, flags, lam, coef, even, odd, inside, across, start, second)
    return call(join_kernel, [(FIELDS, 2, 2, 128, 128)], [vmem])(level(answer))


def solution(mesh):
    fine = Mesh(mesh.devices.reshape([SIZES[a] for a in AXES]), AXES)
    spec = P(None, ("xl", "y", "c"), ("z", "xh"), None, None)
    return jax.shard_map(
        on_device, mesh=fine, in_specs=(spec, P(), P()), out_specs=spec, check_vma=False
    )
```

time: 103 us -> 93 us (0.903)
  other arithmetic: 13.9 us -> 0.18 us
  waiting for transfers between devices: 21 us -> 32.9 us
  starting transfers between devices: 22.5 us -> 15.2 us
    unnamed x15 -> x0, other arithmetic: 12.5 us -> none
    ppermute x6, starting transfers between devices: 15 us -> 7.74 us  [swap(): return lax.ppermute(v, AXES, pairs)]
    all_to_all x1, waiting for transfers between devices: 10.4 us -> 16.6 us  [level(): return lax.all_to_all(v, LEVEL, 0, 0, tiled=True)]
    ppermute x6, waiting for transfers between devices: 10.6 us -> 16.3 us  [swap(): return lax.ppermute(v, AXES, pairs)]
    pallas_call x3 -> x5, Pallas kernels: 12.6 us -> 13 us  [the longest x1 7.4 us: on_device(): call(solve_kernel, [piece], [smem] * 3 + [vmem] * 7, scratch=[(6, FIELDS,...]
  transfers between devices with their start and end apart: 7 -> 7, of which waited for: 4 -> 3; matrix products, arithmetic and copies ran while one was open for 14% -> 0% of each run, Pallas kernels for 1% -> 5%
where the time goes in v2:
time: 93 us; the launch traced here: 92.6 us
  waiting for transfers between devices  32.9 us (35%)
  blocking collectives  27.6 us (30%)
  Pallas kernels  15.3 us (16%)
  starting transfers between devices  15.2 us (16%)
  local copies, waits for them, and re-layouts  1.24 us (1%)
    all_to_all x1, blocking collectives, level(): return lax.all_to_all(v, LEVEL, 0, 0, tiled=True)  27.6 us
    all_to_all x1, waiting for transfers between devices, level(): return lax.all_to_all(v, LEVEL, 0, 0, tiled=True)  16.6 us
    ppermute x6, waiting for transfers between devices, swap(): return lax.ppermute(v, AXES, pairs)  16.3 us
    ppermute x6, starting transfers between devices, swap(): return lax.ppermute(v, AXES, pairs)  7.74 us
    all_to_all x1, starting transfers between devices, level(): return lax.all_to_all(v, LEVEL, 0, 0, tiled=True)  7.45 us
    pallas_call x1, Pallas kernels, on_device(): call(solve_kernel, [piece], [smem] * 3 + [vmem] * 7, scratch=[(6, FIELDS,...  7.4 us
    pallas_call x1, Pallas kernels, on_device(): call(inner_kernel, [(PAIRS, 4, FIELDS, 2, 8, 128)] * 2, [smem, smem] + [v...  3.24 us
  transfers between devices with their start and end apart: 7, of which 3 were waited for; matrix products, arithmetic and copies ran while one was open for 0% of the time, Pallas kernels for 5%

profile of v2, /device:TPU:96, one launch (start us, length us, event | category | flops | bytes accessed | tf_op | source)
XLA Modules:
  0.0 92.6 jit_solution(6618770795981318416)
XLA Ops:
  0.0 1.2 %copy-done = f32[4,2,2,128,128]{4,3,2,1,0:T(8,128)S(1)} copy-done((f32[4,2,2,128,128]{4,3,2,1,0:T(8,128)S(1)}, f32[4,2,2,128,128]{4,3,2,1,0:T(8,128)}, u32[]{:S(2)}) %copy-start) | copy-done | bytes 1048600
  1.2 1.1 %shard_map.46 = f32[32,4,2,8,128]{4,3,2,1,0:T(8,128)} custom-call(f32[4,2,2,128,128]{4,3,2,1,0:T(8,128)S(1)} %copy-done), custom_call_target="tpu_custom_call" | custom-call | bytes 3690000 | tf_op jit(solution)/shard_map/pallas_call | solution.py:501
  2.4 7.5 %all-to-all-start = ((f32[32,4,2,8,128]{4,3,2,1,0:T(8,128)}), f32[32,4,2,8,128]{4,3,2,1,0:T(8,128)S(1)}, u32[]{:S(2)}, u32[]{:S(2)}) async-start(f32[32,4,2,8,128]{4,3,2,1,0:T(8,128)} %shard_map.46), calls=%async_computation | async-start | bytes 2097152 | tf_op jit(solution)/shard_map/all_to_all | solution.py:496
  9.9 0.7 shard_map.47
  10.6 0.1 pad_add_fusion.place
  10.7 0.1 add_convert_fusion.flags
  10.7 16.6 %all-to-all-done.src = f32[32,4,2,8,128]{4,3,2,1,0:T(8,128)S(1)} async-done(((f32[32,4,2,8,128]{4,3,2,1,0:T(8,128)}), f32[32,4,2,8,128]{4,3,2,1,0:T(8,128)S(1)}, u32[]{:S(2)}, u32[]{:S(2)}) %all-to-all-start) | async-done | bytes 1048608 | tf_op jit(solution)/shard_map/all_to_all | solution.py:496
  27.3 1.0 %shard_map.48 = (f32[16,2,4,2,8,128]{5,4,3,2,1,0:T(8,128)S(1)}, f32[16,4,3,8,128]{4,3,2,1,0:T(8,128)S(1)}, f32[16,4,3,8,128]{4,3,2,1,0:T(8,128)S(1)}) custom-call(s32[2]{0:T(128)S(1)} %pad_add_fusion.place, f32[32,4,2,8,128]{4,3,2,1,0:T(8,128)S(1)} %all-to-all-done.src), custom_call_target="tpu_custom_call" | custom-call | bytes 3690000 | tf_op jit(solution)/shard_map/pallas_call | solution.py:512
  28.3 0.2 collective-permute-start
  28.5 5.9 %collective-permute-start.1 = (f32[16,4,3,8,128]{4,3,2,1,0:T(8,128)S(1)}, f32[16,4,3,8,128]{4,3,2,1,0:T(8,128)S(1)}, u32[]{:S(2)}, u32[]{:S(2)}) collective-permute-start(f32[16,4,3,8,128]{4,3,2,1,0:T(8,128)S(1)} %get-tuple-element.26), channel_id=1, source_target_pairs={{2,4},{18,20},{130,132},{146,148},{3,5},{19,21},{131,133},{147,149... | collective-permute-start | bytes 2359304 | tf_op jit(solution)/shard_map/ppermute | solution.py:499
  34.5 0.1 collective-permute-start.4
  34.6 0.7 collective-permute-start.5
  35.3 12.3 %collective-permute-done.even = f32[16,4,3,8,128]{4,3,2,1,0:T(8,128)S(1)} collective-permute-done((f32[16,4,3,8,128]{4,3,2,1,0:T(8,128)S(1)}, f32[16,4,3,8,128]{4,3,2,1,0:T(8,128)S(1)}, u32[]{:S(2)}, u32[]{:S(2)}) %collective-permute-start) | collective-permute-done | bytes 786464 | tf_op jit(solution)/shard_map/ppermute | solution.py:499
  47.6 4.0 %collective-permute-done.1.odd = f32[16,4,3,8,128]{4,3,2,1,0:T(8,128)S(1)} collective-permute-done((f32[16,4,3,8,128]{4,3,2,1,0:T(8,128)S(1)}, f32[16,4,3,8,128]{4,3,2,1,0:T(8,128)S(1)}, u32[]{:S(2)}, u32[]{:S(2)}) %collective-permute-start.1) | collective-permute-done | bytes 786464 | tf_op jit(solution)/shard_map/ppermute | solution.py:499
  51.6 0.7 shard_map.49
  52.3 0.1 collective-permute-start.2
  52.4 0.7 collective-permute-start.3
  53.1 0.0 collective-permute-done.4.inside
  53.1 0.0 collective-permute-done.5.across
  53.1 3.2 %shard_map.50 = (f32[16,4,4,2,8,128]{5,4,3,2,1,0:T(8,128)S(1)}, f32[16,4,4,2,8,128]{5,4,3,2,1,0:T(8,128)S(1)}) custom-call(s32[2]{0:T(128)S(1)} %pad_add_fusion.place, f32[16,3]{1,0:T(8,128)S(1)} %copy-done.1, f32[16,8,128]{2,1,0:T(8,128)S(1)} %get-tuple-element.23.coef, f32[3,8,128]{2,1,0:T(8,128)S(1)} %get-tuple-element.29.edge, ...), custom_call_target="tpu_custom_call" | custom-call | bytes 18450000 | tf_op jit(solution)/shard_map/pallas_call | solution.py:520
  56.4 0.0 collective-permute-done.2.inside
  56.4 7.4 %shard_map.51 = f32[32,4,2,8,128]{4,3,2,1,0:T(8,128)S(1)} custom-call(s32[2]{0:T(128)S(1)} %pad_add_fusion.place, f32[2]{0:T(128)S(1)} %add_convert_fusion.flags, f32[16,3]{1,0:T(8,128)S(1)} %copy-done.1, f32[16,8,128]{2,1,0:T(8,128)S(1)} %get-tuple-element.23.coef, f32[16,4,3,8,128]{4,3,2,1,0:T(8,128)S(1)} %collective-permute-done.even, ...), custom_call_target="tpu_custom_call" | custom-call | bytes 3690000 | tf_op jit(solution)/shard_map/pallas_call | solution.py:529
  63.8 27.6 %all_to_all.10.src = f32[32,4,2,8,128]{4,3,2,1,0:T(8,128)S(1)} all-to-all(f32[32,4,2,8,128]{4,3,2,1,0:T(8,128)S(1)} %shard_map.51), channel_id=1, replica_groups=mesh['xl'=2,'y'=4,'c'=2,'z'=8,'xh'=2] {'xl','y','c','xh'}, dimensions={0} | all-to-all | bytes 2097152 | tf_op jit(solution)/shard_map/all_to_all | solution.py:496
  91.4 1.2 %shard_map.52 = f32[4,2,2,128,128]{4,3,2,1,0:T(8,128)} custom-call(f32[32,4,2,8,128]{4,3,2,1,0:T(8,128)S(1)} %all_to_all.10.src), custom_call_target="tpu_custom_call" | custom-call | bytes 3690000 | tf_op jit(solution)/shard_map/pallas_call | solution.py:541
  (11 shorter events, 0.0 us)
Async XLA Ops:
  0.0 1.2 %copy-start = (f32[4,2,2,128,128]{4,3,2,1,0:T(8,128)S(1)}, f32[4,2,2,128,128]{4,3,2,1,0:T(8,128)}, u32[]{:S(2)}) copy-start(f32[4,2,2,128,128]{4,3,2,1,0:T(8,128)} %src.1) | copy-start | bytes 3145732
  1.2 8.6 %copy-start.3 = (s32[128,128]{1,0:T(8,128)S(1)}, s32[128,128]{1,0:T(8,128)}, u32[]{:S(2)}) copy-start(s32[128,128]{1,0:T(8,128)} %param.5) | copy-start | bytes 196612
  1.2 8.6 %slice-start = ((s32[128,128]{1,0:T(8,128)}), s32[8,128]{1,0:T(8,128)S(1)}, s32[]{:S(2)}) async-start(s32[128,128]{1,0:T(8,128)} %param.5), calls=%async_computation.2 | async-start | bytes 8192 | tf_op jit(solution)/shard_map/slice | solution.py:503
  1.2 8.7 %copy-start.2 = (f32[3,4]{1,0:T(4,128)S(1)}, f32[3,4]{1,0:T(4,128)}, u32[]{:S(2)}) copy-start(f32[3,4]{1,0:T(4,128)} %material.1) | copy-start | bytes 148
  2.4 50.8 %copy-start.1 = (f32[16,3]{1,0:T(8,128)S(1)}, f32[16,3]{1,0:T(8,128)}, u32[]{:S(2)}) copy-start(f32[16,3]{1,0:T(8,128)} %constant.51.clone.lam) | copy-start | bytes 580
  2.4 25.0 %all-to-all-start = ((f32[32,4,2,8,128]{4,3,2,1,0:T(8,128)}), f32[32,4,2,8,128]{4,3,2,1,0:T(8,128)S(1)}, u32[]{:S(2)}, u32[]{:S(2)}) async-start(f32[32,4,2,8,128]{4,3,2,1,0:T(8,128)} %shard_map.46), calls=%async_computation | async-start | bytes 2097152 | tf_op jit(solution)/shard_map/all_to_all | solution.py:496
  28.3 19.2 %collective-permute-start = (f32[16,4,3,8,128]{4,3,2,1,0:T(8,128)S(1)}, f32[16,4,3,8,128]{4,3,2,1,0:T(8,128)S(1)}, u32[]{:S(2)}, u32[]{:S(2)}) collective-permute-start(f32[16,4,3,8,128]{4,3,2,1,0:T(8,128)S(1)} %get-tuple-element.25), channel_id=1, source_target_pairs={{0,2},{16,18},{128,130},{144,146},{1,3},{17,19},{129,131},{145,147... | collective-permute-start | bytes 2359304 | tf_op jit(solution)/shard_map/ppermute | solution.py:499
  28.5 23.0 %collective-permute-start.1 = (f32[16,4,3,8,128]{4,3,2,1,0:T(8,128)S(1)}, f32[16,4,3,8,128]{4,3,2,1,0:T(8,128)S(1)}, u32[]{:S(2)}, u32[]{:S(2)}) collective-permute-start(f32[16,4,3,8,128]{4,3,2,1,0:T(8,128)S(1)} %get-tuple-element.26), channel_id=1, source_target_pairs={{2,4},{18,20},{130,132},{146,148},{3,5},{19,21},{131,133},{147,149... | collective-permute-start | bytes 2359304 | tf_op jit(solution)/shard_map/ppermute | solution.py:499
  34.5 18.6 %collective-permute-start.4 = (f32[16,2,4,2,8,128]{5,4,3,2,1,0:T(8,128)S(1)}, f32[16,2,4,2,8,128]{5,4,3,2,1,0:T(8,128)S(1)}, u32[]{:S(2)}, u32[]{:S(2)}) collective-permute-start(f32[16,2,4,2,8,128]{5,4,3,2,1,0:T(8,128)S(1)} %get-tuple-element.30.own), channel_id=1, source_target_pairs={{0,16},{128,144},{1,17},{129,145},{161,177},{33,49},{160,176},{32,... | collective-permute-start | bytes 3145736 | tf_op jit(solution)/shard_map/ppermute | solution.py:499
  34.6 18.5 %collective-permute-start.5 = (f32[16,2,4,2,8,128]{5,4,3,2,1,0:T(8,128)S(1)}, f32[16,2,4,2,8,128]{5,4,3,2,1,0:T(8,128)S(1)}, u32[]{:S(2)}, u32[]{:S(2)}) collective-permute-start(f32[16,2,4,2,8,128]{5,4,3,2,1,0:T(8,128)S(1)} %get-tuple-element.30.own), channel_id=1, source_target_pairs={{16,128},{144,1},{17,129},{145,161},{177,33},{49,160},{176,32},{48... | collective-permute-start | bytes 3145736 | tf_op jit(solution)/shard_map/ppermute | solution.py:499
  52.3 4.1 %collective-permute-start.2 = (f32[16,4,2,8,128]{4,3,2,1,0:T(8,128)S(1)}, f32[16,4,2,8,128]{4,3,2,1,0:T(8,128)S(1)}, u32[]{:S(2)}, u32[]{:S(2)}) collective-permute-start(f32[16,4,2,8,128]{4,3,2,1,0:T(8,128)S(1)} %get-tuple-element.27), channel_id=1, source_target_pairs={{0,16},{128,144},{1,17},{129,145},{161,177},{33,49},{160,176},{32,... | collective-permute-start | bytes 1572872 | tf_op jit(solution)/shard_map/ppermute | solution.py:499
  52.4 4.0 %collective-permute-start.3 = (f32[16,4,2,8,128]{4,3,2,1,0:T(8,128)S(1)}, f32[16,4,2,8,128]{4,3,2,1,0:T(8,128)S(1)}, u32[]{:S(2)}, u32[]{:S(2)}) collective-permute-start(f32[16,4,2,8,128]{4,3,2,1,0:T(8,128)S(1)} %get-tuple-element.28), channel_id=1, source_target_pairs={{16,128},{144,1},{17,129},{145,161},{177,33},{49,160},{176,32},{48... | collective-permute-start | bytes 1572872 | tf_op jit(solution)/shard_map/ppermute | solution.py:499

commit v3 on v1

v3 whole, which is shorter than its diff:
```python
import functools
import math

import jax
import jax.numpy as jnp
import numpy as np
from jax import lax
from jax.experimental import pallas as pl
from jax.experimental.pallas import tpu as pltpu
from jax.sharding import Mesh
from jax.sharding import PartitionSpec as P

AXES = ("xl", "y", "c", "z", "xh")
SIZES = dict(xl=2, y=4, c=2, z=8, xh=2)
LEVEL = ("xl", "y", "c", "xh")
STEPS = 32
PAIRS = 16
FIELDS = 4
MIB = 1 << 20
UNROLL = 4


def chip_at(pos):
    y, x = divmod(pos, 4)
    return (3 - x if y % 2 else x), y


def level_index(pos, core):
    x, y = chip_at(pos)
    return ((((x % 2) * 4 + y) * 2 + core) * 2) + x // 2


def device_index(z, pos, core):
    x, y = chip_at(pos)
    return ((((x % 2) * 4 + y) * 2 + core) * 8 + z) * 2 + x // 2


def both(pairs):
    return pairs + [(t, s) for s, t in pairs]


def sibling_swap():
    return both([(device_index(z, p, 0), device_index(z, p, 1)) for z in range(8) for p in range(16)])


def level_swap():
    return both([(device_index(z, p, 1), device_index(z + 1, p, 0)) for z in range(7) for p in range(16)])


def row_swap(parity):
    low = [p for p in range(15) if p % 2 == parity]
    return both([(device_index(z, p, c), device_index(z, p + 1, c)) for z in range(8) for p in low for c in range(2)])


def rows():
    return lax.broadcasted_iota(jnp.int32, (8, 128), 0)


def lanes():
    return lax.broadcasted_iota(jnp.int32, (8, 128), 1)


def among(index, members):
    mask = index == members[0]
    for member in members[1:]:
        mask = mask | (index == member)
    return mask


def roll(tile, amount):
    amount %= 8
    return tile if amount == 0 else pltpu.roll(tile, amount, 0)


def mul_const(re, im, cr, ci):
    def axpy(a, x, b, y):
        terms = []
        for k, v in ((a, x), (b, y)):
            if abs(k) > 1e-12:
                terms.append((k, v))
        total = None
        for k, v in terms:
            if total is None:
                total = v if abs(k - 1) < 1e-12 else (-v if abs(k + 1) < 1e-12 else v * np.float32(k))
            elif abs(k - 1) < 1e-12:
                total = total + v
            elif abs(k + 1) < 1e-12:
                total = total - v
            else:
                total = total + v * np.float32(k)
        return total

    if abs(abs(cr) - abs(ci)) < 1e-12:
        root = np.float32(abs(cr))
        sr, si = math.copysign(1, cr), math.copysign(1, ci)
        return axpy(sr, re * root, -si, im * root), axpy(si, re * root, sr, im * root)
    return axpy(cr, re, -ci, im), axpy(ci, re, cr, im)


def rfft(x):
    n = len(x)
    if n == 2:
        return [(x[0] + x[1], None), (x[0] - x[1], None)]
    even, odd = rfft(x[0::2]), rfft(x[1::2])
    out = [None] * (n // 2 + 1)
    out[0] = (even[0][0] + odd[0][0], None)
    out[n // 2] = (even[0][0] - odd[0][0], None)
    out[n // 4] = (even[n // 4][0], -odd[n // 4][0])
    for k in range(1, n // 4):
        angle = -2 * math.pi * k / n
        tr, ti = mul_const(*odd[k], math.cos(angle), math.sin(angle))
        er, ei = even[k]
        out[k] = (er + tr, ei + ti)
        out[n // 2 - k] = (er - tr, ti - ei)
    return out


def irfft(spec):
    n = 2 * (len(spec) - 1)
    if n == 2:
        return [spec[0][0] + spec[1][0], spec[0][0] - spec[1][0]]
    q = n // 4
    even, odd = [None] * (q + 1), [None] * (q + 1)
    even[0] = (spec[0][0] + spec[2 * q][0], None)
    odd[0] = (spec[0][0] - spec[2 * q][0], None)
    even[q] = (2.0 * spec[q][0], None)
    odd[q] = (-2.0 * spec[q][1], None)
    for k in range(1, q):
        ar, ai = spec[k]
        br, bi = spec[2 * q - k]
        even[k] = (ar + br, ai - bi)
        angle = 2 * math.pi * k / n
        odd[k] = mul_const(ar - br, ai + bi, math.cos(angle), math.sin(angle))
    a, b = irfft(even), irfft(odd)
    return [v for two in zip(a, b) for v in two]


def split_kernel(src, out, whole, pieces, in_sems, out_sems):
    arrivals = [pltpu.make_async_copy(src.at[f], whole.at[f], in_sems.at[f]) for f in range(FIELDS)]
    for copy in arrivals:
        copy.start()
    leaving = []
    for f in range(FIELDS):
        arrivals[f].wait()
        for t in range(2):
            for core in range(2):
                for pos in range(16):
                    pieces[level_index(pos, core), f, t] = whole[f, t, core, pl.ds(8 * pos, 8), :]
        leaving.append(pltpu.make_async_copy(pieces.at[:, f], out.at[:, f], out_sems.at[f]))
        leaving[-1].start()
    for copy in leaving:
        copy.wait()


def join_kernel(src, out, whole, sems):
    copies = []
    for f in range(FIELDS):
        for t in range(2):
            for core in range(2):
                for pos in range(16):
                    whole[f, t, core, pl.ds(8 * pos, 8), :] = src[level_index(pos, core), f, t]
        copies.append(pltpu.make_async_copy(whole.at[f], out.at[f], sems.at[f]))
        copies[-1].start()
    for copy in copies:
        copy.wait()


(A, AE, AW, AN, AS, AH, AC, GE, GW, GN, GS, GH, G, KE, KW, KN, KS, KH, KZ, HKD, DN, DS, DH) = range(23)


def coefficient_kernel(place, material, regions, coef):
    pos = place[1]
    r, l = rows(), lanes()
    there = [l < 127, l > 0, (r < 7) | (pos < 15), (r > 0) | (pos > 0)]
    has_e, has_w = [jnp.where(t, 1.0, 0.0).astype(jnp.float32) for t in there[:2]]
    here = regions[pl.ds(8 * pos, 8), :]
    after = regions[pl.ds(8 * jnp.minimum(pos + 1, 15), 8), :]
    before = regions[pl.ds(8 * jnp.maximum(pos - 1, 0), 8), :]

    def parts(row):
        def value_of(classes):
            value = jnp.zeros((8, 128), jnp.float32)
            for m in range(4):
                value = jnp.where(classes == m, material[row, m], value)
            return value

        value = value_of(here)
        moved = [
            pltpu.roll(value, 127, 1),
            pltpu.roll(value, 1, 1),
            roll(jnp.where(r == 0, value_of(after), value), 7),
            roll(jnp.where(r == 7, value_of(before), value), 1),
        ]
        return value, [jnp.where(t, (value + v) * 0.5, value) for t, v in zip(there, moved)]

    shear, (se, sw, sn, ss) = parts(0)
    _, (ke, kw, kn, ks) = parts(1)
    axial, _ = parts(2)
    a = 0.8 / (se + sw + sn + ss + 2.0 * shear)
    in_n, in_s = [jnp.where(t, 1.0, 0.0).astype(jnp.float32) for t in (r < 7, r > 0)]
    zero = jnp.zeros((8, 128), jnp.float32)

    def beside(south, north):
        return jnp.where(r == 0, south, jnp.where(r == 7, north, zero))

    g = 0.3 * a
    table = [
        a, a * se * has_e, a * sw * has_w, a * sn * in_n, a * ss * in_s, beside(a * ss, a * sn), a * shear,
        g * has_e, g * has_w, g * in_n, g * in_s, beside(-g, g), g,
        0.5 * ke * has_e, 0.5 * kw * has_w, 0.5 * kn * in_n, 0.5 * ks * in_s, beside(0.5 * ks, 0.5 * kn),
        0.5 * axial, 0.5 * (ke + kw + kn + ks + 2.0 * axial),
        0.3 * in_n, 0.3 * in_s, beside(zero - 0.3, zero + 0.3),
    ]
    for n, v in enumerate(table):
        coef[n] = v


def inverse_diagonal(lam, q, half_diag):
    d0, d1, di = half_diag + 0.5 * lam[q, 0], half_diag + 0.5 * lam[q, 1], -0.5 * lam[q, 2]
    inv = 0.8 / (d0 * d1 + di * di)
    return inv * d1, inv * d0, inv * di


def first_iterate(f, tiles, a, diagonal):
    re, im = tiles
    if f < 3:
        return a * re, a * im
    b00, b11, b01 = diagonal
    return b00 * re + b01 * im, b11 * im - b01 * re


def send(place, q, planes, row_a, row_b):
    r = rows()
    even = (r * 0 + place[1] % 2) == 0
    for p, tiles in planes:
        after = before = None
        for j in range(8):
            f, c = divmod(j, 2)
            seven, zero = roll(tiles[f][c], j + 1), roll(tiles[f][c], j - 1)
            after = seven if j == 0 else jnp.where(r == j, seven, after)
            before = zero if j == 0 else jnp.where(r == (j - 1) % 8, zero, before)
        row_a[q, p] = jnp.where(even, after, before)
        row_b[q, p] = jnp.where(even, before, after)


def spectrum_kernel(place, lam, coef, src, x0, outer, row_a, row_b, spec):
    def body(f, _):
        for p in range(2):
            got = rfft([src[(t // 2) * 2 + p, f, t % 2] for t in range(STEPS)])
            pairs = [(got[0][0], got[16][0])] + got[1:16]
            for q in range(PAIRS):
                for c in range(2):
                    spec[q, p, f, c] = pairs[q][c]
        return 0

    lax.fori_loop(0, FIELDS, body, 0)

    def pair(q, _):
        diagonal = inverse_diagonal(lam, q, coef[HKD])
        planes = [
            [first_iterate(f, (spec[q, p, f, 0], spec[q, p, f, 1]), coef[A], diagonal) for f in range(FIELDS)]
            for p in range(2)
        ]
        for p in range(2):
            for f in range(FIELDS):
                for c in range(2):
                    x0[q, p, f, c] = planes[p][f][c]
        for f in range(FIELDS):
            for c in range(2):
                outer[q, f, c] = x0[q, place[0], f, c]
        send(place, q, list(enumerate(planes)), row_a, row_b)
        return 0

    lax.fori_loop(0, PAIRS, pair, 0, unroll=UNROLL)


def own_kernel(place, lam, coef, x0, x, sib, part):
    l = lanes()
    east = jnp.where(l == 127, 0.0, 0.3).astype(jnp.float32)
    west = jnp.where(l == 0, 0.0, 0.3).astype(jnp.float32)
    core = place[0]
    sign = 1.0 - 2.0 * core.astype(jnp.float32)

    def pair(q, _):
        m00, m11, m01 = lam[q, 0], lam[q, 1], lam[q, 2]
        pa, pb, pc = inverse_diagonal(lam, q, coef[HKD])
        for p, edge in ((core, True), (1 - core, False)):
            new = [[None, None] for _ in range(FIELDS)]
            div, flow = [None, None], [None, None]
            for c in range(2):
                cur = [x[q, p, f, c] for f in range(FIELDS)]
                es = [pltpu.roll(v, 127, 1) for v in cur]
                ws = [pltpu.roll(v, 1, 1) for v in cur]
                ns = [roll(v, 7) for v in cur]
                ss = [roll(v, 1) for v in cur]
                if edge:
                    total = [sib[q, core, f, c] for f in range(FIELDS)]
                    drop_u, drop_p = sign * total[2], sign * total[3]
                else:
                    dn = [sib[q, 0, f, c] for f in range(FIELDS)]
                    up = [sib[q, 1, f, c] for f in range(FIELDS)]
                    total = [u + d for u, d in zip(up, dn)]
                    drop_u, drop_p = up[2] - dn[2], up[3] - dn[3]
                grad = [
                    coef[GE] * es[3] - coef[GW] * ws[3],
                    coef[GN] * ns[3] - coef[GS] * ss[3],
                    coef[G] * drop_p,
                ]
                for f in range(3):
                    v = (x0[q, p, f, c] + 0.2 * cur[f]) + coef[AE] * es[f] + coef[AW] * ws[f]
                    v = v + coef[AN] * ns[f] + coef[AS] * ss[f]
                    part[q, p, f, c] = v + coef[AC] * total[f] - grad[f]
                new[3][c] = x0[q, p, 3, c] + 0.2 * cur[3]
                flow[c] = (
                    coef[KE] * es[3]
                    + coef[KW] * ws[3]
                    + coef[KN] * ns[3]
                    + coef[KS] * ss[3]
                    + coef[KZ] * total[3]
                )
                div[c] = east * es[0] - west * ws[0] + coef[DN] * ns[1] - coef[DS] * ss[1] + 0.3 * drop_u
            g0 = flow[0] - (m00 * div[0] + m01 * div[1])
            g1 = flow[1] - (m11 * div[1] - m01 * div[0])
            part[q, p, 3, 0] = new[3][0] + pa * g0 + pc * g1
            part[q, p, 3, 1] = new[3][1] + pb * g1 - pc * g0
        return 0

    lax.fori_loop(0, PAIRS, pair, 0, unroll=UNROLL)


def finish(place, lam, q, coef, part, outer, row_a, row_b):
    r = rows()
    core = place[0]
    sign = 2.0 * core.astype(jnp.float32) - 1.0
    odd = r * 0 + place[1] % 2
    m00, m11, m01 = lam[q, 0], lam[q, 1], lam[q, 2]
    pa, pb, pc = inverse_diagonal(lam, q, coef[HKD])
    result = []
    for p, edge in ((core, True), (1 - core, False)):
        a, b = row_a[q, p], row_b[q, p]
        new = [[None, None] for _ in range(FIELDS)]
        div, flow = [None, None], [None, None]
        for c in range(2):
            beside = []
            for f in range(FIELDS):
                j = 2 * f + c
                low_is_b = (jnp.where(r == j, 1, 0) ^ odd) == 1
                beside.append(roll(jnp.where(low_is_b, b, a), -j))
            for f in range(3):
                new[f][c] = part[q, p, f, c] + coef[AH] * beside[f]
            new[1][c] = new[1][c] - coef[GH] * beside[3]
            flow[c] = coef[KH] * beside[3]
            div[c] = coef[DH] * beside[1]
            if edge:
                out = [outer[q, f, c] for f in range(FIELDS)]
                for f in range(3):
                    new[f][c] = new[f][c] + coef[AC] * out[f]
                new[2][c] = new[2][c] - (sign * coef[G]) * out[3]
                flow[c] = flow[c] + coef[KZ] * out[3]
                div[c] = div[c] + (0.3 * sign) * out[2]
        g0 = flow[0] - (m00 * div[0] + m01 * div[1])
        g1 = flow[1] - (m11 * div[1] - m01 * div[0])
        new[3][0] = part[q, p, 3, 0] + pa * g0 + pc * g1
        new[3][1] = part[q, p, 3, 1] + pb * g1 - pc * g0
        result.append((p, new))
    return result


def round_kernel(place, lam, coef, part, outer, row_a, row_b, y, next_outer, next_a, next_b):
    def pair(q, _):
        planes = finish(place, lam, q, coef, part, outer, row_a, row_b)
        for p, tiles in planes:
            for f in range(FIELDS):
                for c in range(2):
                    y[q, p, f, c] = tiles[f][c]
        for f in range(FIELDS):
            for c in range(2):
                next_outer[q, f, c] = planes[0][1][f][c]
        send(place, q, planes, next_a, next_b)
        return 0

    lax.fori_loop(0, PAIRS, pair, 0, unroll=UNROLL)


def last_kernel(place, lam, coef, part, outer, row_a, row_b, out, y):
    scale32 = np.float32(1.0 / STEPS)

    def pair(q, _):
        for p, tiles in finish(place, lam, q, coef, part, outer, row_a, row_b):
            for f in range(FIELDS):
                for c in range(2):
                    y[q, p, f, c] = tiles[f][c] * scale32
        return 0

    lax.fori_loop(0, PAIRS, pair, 0, unroll=UNROLL)

    def back(f, _):
        for p in range(2):
            spec = [(y[0, p, f, 0], None)]
            spec += [(y[q, p, f, 0], y[q, p, f, 1]) for q in range(1, PAIRS)]
            spec += [(y[0, p, f, 1], None)]
            for t, v in enumerate(irfft(spec)):
                out[(t // 2) * 2 + p, f, t % 2] = v
        return 0

    lax.fori_loop(0, FIELDS, back, 0)


def call(kernel, outs, in_spaces, scratch=(), limit=4, micros=1):
    f32 = jnp.float32
    shapes = [jax.ShapeDtypeStruct(s, f32) for s in outs]
    specs = [pl.BlockSpec(memory_space=pltpu.VMEM) for _ in outs]
    single = len(outs) == 1
    return pl.pallas_call(
        kernel,
        out_shape=shapes[0] if single else shapes,
        in_specs=[pl.BlockSpec(memory_space=m) for m in in_spaces],
        out_specs=specs[0] if single else specs,
        scratch_shapes=[pltpu.VMEM(s, f32) for s in scratch],
        compiler_params=pltpu.CompilerParams(vmem_limit_bytes=limit * MIB),
        cost_estimate=pl.CostEstimate(flops=0, bytes_accessed=int(micros * 3.69e6), transcendentals=0),
    )


def lam_table():
    k = np.arange(1, PAIRS)
    real, imag = 1 - np.cos(2 * np.pi * k / STEPS), np.sin(2 * np.pi * k / STEPS)
    rest = np.stack([real, real, -imag], axis=1)
    return np.concatenate([[[0.0, 2.0, 0.0]], rest]).astype(np.float32)


def on_device(sources, regions, material):
    vmem, smem = pltpu.VMEM, pltpu.SMEM
    x = lax.axis_index("xh") * 2 + lax.axis_index("xl")
    y = lax.axis_index("y")
    pos = y * 4 + jnp.where(y % 2 == 1, 3 - x, x)
    place = jnp.stack([lax.axis_index("c"), pos]).astype(jnp.int32)
    piece = (32, FIELDS, 2, 8, 128)
    block = (PAIRS, 2, FIELDS, 2, 8, 128)
    messages = [(PAIRS, FIELDS, 2, 8, 128), (PAIRS, 2, 8, 128), (PAIRS, 2, 8, 128)]

    def level(v):
        return lax.all_to_all(v, LEVEL, 0, 0, tiled=True)

    def exchange(v, outer, row_a, row_b):
        outer = lax.ppermute(outer, AXES, level_swap())
        sib = lax.ppermute(v, AXES, sibling_swap())
        row_a = lax.ppermute(row_a, AXES, row_swap(0))
        row_b = lax.ppermute(row_b, AXES, row_swap(1))
        part = call(own_kernel, [block], [smem, smem] + [vmem] * 4, limit=8, micros=2)(place, lam, coef, x0, v, sib)
        return part, outer, row_a, row_b

    whole = (FIELDS, 2, 2, 128, 128)
    pieces = pl.pallas_call(
        split_kernel,
        out_shape=jax.ShapeDtypeStruct(piece, jnp.float32),
        in_specs=[pl.BlockSpec(memory_space=pltpu.HBM)],
        out_specs=pl.BlockSpec(memory_space=pltpu.HBM),
        scratch_shapes=[
            pltpu.VMEM(whole, jnp.float32),
            pltpu.VMEM(piece, jnp.float32),
            pltpu.SemaphoreType.DMA((FIELDS,)),
            pltpu.SemaphoreType.DMA((FIELDS,)),
        ],
        compiler_params=pltpu.CompilerParams(vmem_limit_bytes=60 * MIB),
    )(sources)
    arrived = level(pieces)
    coef = call(coefficient_kernel, [(23, 8, 128)], [smem, smem, vmem])(place, material, regions)
    arrived, coef, place = lax.optimization_barrier((arrived, coef, place))
    lam = jnp.asarray(lam_table())
    x0, *out = call(spectrum_kernel, [block] + messages, [smem, smem, vmem, vmem], [block], 8)(
        place, lam, coef, arrived
    )
    x = x0
    for _ in range(2):
        x, *out = call(round_kernel, [block] + messages, [smem, smem] + [vmem] * 5, limit=8)(
            place, lam, coef, *exchange(x, *out)
        )
    answer = call(last_kernel, [piece], [smem, smem] + [vmem] * 5, [block], 8)(
        place, lam, coef, *exchange(x, *out)
    )
    return pl.pallas_call(
        join_kernel,
        out_shape=jax.ShapeDtypeStruct(whole, jnp.float32),
        in_specs=[pl.BlockSpec(memory_space=vmem)],
        out_specs=pl.BlockSpec(memory_space=pltpu.HBM),
        scratch_shapes=[pltpu.VMEM(whole, jnp.float32), pltpu.SemaphoreType.DMA((FIELDS,))],
        compiler_params=pltpu.CompilerParams(vmem_limit_bytes=4 * MIB),
    )(level(answer))


def solution(mesh):
    fine = Mesh(mesh.devices.reshape([SIZES[a] for a in AXES]), AXES)
    spec = P(None, ("xl", "y", "c"), ("z", "xh"), None, None)
    return jax.shard_map(
        on_device, mesh=fine, in_specs=(spec, P(), P()), out_specs=spec, check_vma=False
    )
```

time: 103 us -> 89.8 us (0.87)
  other arithmetic: 13.9 us -> 0.08 us
  waiting for transfers between devices: 21 us -> 33.4 us
  blocking collectives: 28.2 us -> 21.5 us
  starting transfers between devices: 22.5 us -> 19.9 us
  local copies, waits for them, and re-layouts: 2.04 us -> 0.61 us
  Pallas kernels: 14.9 us -> 13.6 us
    unnamed x15 -> x0, other arithmetic: 12.5 us -> none
    all_to_all x1, blocking collectives: 28.2 us -> 21.5 us  [level(): return lax.all_to_all(v, LEVEL, 0, 0, tiled=True)]
    ppermute x6 -> x12, waiting for transfers between devices: 10.6 us -> 17.2 us  [the longest x3 10.4 us: exchange(): outer = lax.ppermute(outer, AXES, level_swap())]
    all_to_all x1, waiting for transfers between devices: 10.4 us -> 16.2 us  [level(): return lax.all_to_all(v, LEVEL, 0, 0, tiled=True)]
    ppermute x6 -> x12, starting transfers between devices: 15 us -> 12.5 us  [the longest x3 5.92 us: exchange(): outer = lax.ppermute(outer, AXES, level_swap())]
    pallas_call x5 -> x10, Pallas kernels: 14.9 us -> 13.6 us  [the longest x3 4.86 us: exchange(): call(own_kernel, [block], [smem, smem] + [vmem] * 4, limit=8, micros=2)]
  transfers between devices with their start and end apart: 7 -> 13, of which waited for: 4 -> 7; matrix products, arithmetic and copies ran while one was open for 14% -> 0% of each run, Pallas kernels for 1% -> 6%
where the time goes in v3:
time: 89.8 us; the launch traced here: 89.3 us
  waiting for transfers between devices  33.4 us (37%)
  blocking collectives  21.5 us (24%)
  starting transfers between devices  19.9 us (22%)
  Pallas kernels  13.6 us (15%)
    all_to_all x1, blocking collectives, level(): return lax.all_to_all(v, LEVEL, 0, 0, tiled=True)  21.5 us
    all_to_all x1, waiting for transfers between devices, level(): return lax.all_to_all(v, LEVEL, 0, 0, tiled=True)  16.2 us
    ppermute x3, waiting for transfers between devices, exchange(): outer = lax.ppermute(outer, AXES, level_swap())  10.4 us
    all_to_all x1, starting transfers between devices, level(): return lax.all_to_all(v, LEVEL, 0, 0, tiled=True)  7.46 us
    ppermute x3, waiting for transfers between devices, exchange(): row_a = lax.ppermute(row_a, AXES, row_swap(0))  6.87 us
    ppermute x3, starting transfers between devices, exchange(): outer = lax.ppermute(outer, AXES, level_swap())  5.92 us
    pallas_call x3, Pallas kernels, exchange(): call(own_kernel, [block], [smem, smem] + [vmem] * 4, limit=8, micros=2)  4.86 us
    ppermute x3, starting transfers between devices, exchange(): sib = lax.ppermute(v, AXES, sibling_swap())  3.2 us
  transfers between devices with their start and end apart: 13, of which 7 were waited for; matrix products, arithmetic and copies ran while one was open for 0% of the time, Pallas kernels for 6%

profile of v3, /device:TPU:96, one launch (start us, length us, event | category | flops | bytes accessed | tf_op | source)
XLA Modules:
  0.0 89.3 jit_solution(10553659043753137314)
XLA Ops:
  0.0 2.0 %shard_map.46 = f32[32,4,2,8,128]{4,3,2,1,0:T(8,128)} custom-call(f32[4,2,2,128,128]{4,3,2,1,0:T(8,128)} %src.1), custom_call_target="tpu_custom_call" | custom-call | tf_op jit(solution)/shard_map/pallas_call | solution.py:454
  2.0 7.5 %all-to-all-start = ((f32[32,4,2,8,128]{4,3,2,1,0:T(8,128)}), f32[32,4,2,8,128]{4,3,2,1,0:T(8,128)S(1)}, u32[]{:S(2)}, u32[]{:S(2)}) async-start(f32[32,4,2,8,128]{4,3,2,1,0:T(8,128)} %shard_map.46), calls=%async_computation | async-start | bytes 2097152 | tf_op jit(solution)/shard_map/all_to_all | solution.py:443
  10.2 0.7 shard_map.47.coef
  10.9 16.2 %all-to-all-done.src = f32[32,4,2,8,128]{4,3,2,1,0:T(8,128)S(1)} async-done(((f32[32,4,2,8,128]{4,3,2,1,0:T(8,128)}), f32[32,4,2,8,128]{4,3,2,1,0:T(8,128)S(1)}, u32[]{:S(2)}, u32[]{:S(2)}) %all-to-all-start) | async-done | bytes 1048608 | tf_op jit(solution)/shard_map/all_to_all | solution.py:443
  27.0 1.2 %shard_map.48 = (f32[16,2,4,2,8,128]{5,4,3,2,1,0:T(8,128)S(1)}, f32[16,4,2,8,128]{4,3,2,1,0:T(8,128)S(1)}, f32[16,2,8,128]{3,2,1,0:T(8,128)S(1)}, f32[16,2,8,128]{3,2,1,0:T(8,128)S(1)}) custom-call(s32[2]{0:T(128)S(1)} %pad_add_fusion.place, f32[16,3]{1,0:T(8,128)S(1)} %copy-done, f32[23,8,128]{2,1,0:T(8,128)S(1)} %shard_map.47.coef, ...), custom_call_target="tpu_custom_call" | custom-call | bytes 3690000 | tf_op jit(solution)/shard_map/pallas_call | solution.py:471
  28.4 2.1 %collective-permute-start.1 = (f32[16,4,2,8,128]{4,3,2,1,0:T(8,128)S(1)}, f32[16,4,2,8,128]{4,3,2,1,0:T(8,128)S(1)}, u32[]{:S(2)}, u32[]{:S(2)}) collective-permute-start(f32[16,4,2,8,128]{4,3,2,1,0:T(8,128)S(1)} %get-tuple-element.24), channel_id=1, source_target_pairs={{16,2},{144,130},{17,3},{145,131},{177,163},{49,35},{176,162},{48,... | collective-permute-start | bytes 1572872 | tf_op jit(solution)/shard_map/ppermute | solution.py:446
  31.3 1.6 %shard_map.49.part = f32[16,2,4,2,8,128]{5,4,3,2,1,0:T(8,128)S(1)} custom-call(s32[2]{0:T(128)S(1)} %pad_add_fusion.place, f32[16,3]{1,0:T(8,128)S(1)} %copy-done, f32[23,8,128]{2,1,0:T(8,128)S(1)} %shard_map.47.coef, f32[16,2,4,2,8,128]{5,4,3,2,1,0:T(8,128)S(1)} %get-tuple-element.23.x0.x, f32[16,2,4,2,8,128]{5,4,3,2,1,0:T(8,128)S(1)} %get-tuple-element.23.x0.x, ...), custom_call_target="tpu_custom_call" | custom-call | bytes 7380000 | tf_op jit(solution)/shard_map/pallas_call | solution.py:450
  33.0 2.5 %collective-permute-done.2.row_a = f32[16,2,8,128]{3,2,1,0:T(8,128)S(1)} collective-permute-done((f32[16,2,8,128]{3,2,1,0:T(8,128)S(1)}, f32[16,2,8,128]{3,2,1,0:T(8,128)S(1)}, u32[]{:S(2)}, u32[]{:S(2)}) %collective-permute-start.2) | collective-permute-done | bytes 131104 | tf_op jit(solution)/shard_map/ppermute | solution.py:448
  35.5 3.3 %collective-permute-done.1.outer = f32[16,4,2,8,128]{4,3,2,1,0:T(8,128)S(1)} collective-permute-done((f32[16,4,2,8,128]{4,3,2,1,0:T(8,128)S(1)}, f32[16,4,2,8,128]{4,3,2,1,0:T(8,128)S(1)}, u32[]{:S(2)}, u32[]{:S(2)}) %collective-permute-start.1) | collective-permute-done | bytes 524320 | tf_op jit(solution)/shard_map/ppermute | solution.py:446
  38.9 1.2 %shard_map.50 = (f32[16,2,4,2,8,128]{5,4,3,2,1,0:T(8,128)S(1)}, f32[16,4,2,8,128]{4,3,2,1,0:T(8,128)S(1)}, f32[16,2,8,128]{3,2,1,0:T(8,128)S(1)}, f32[16,2,8,128]{3,2,1,0:T(8,128)S(1)}) custom-call(s32[2]{0:T(128)S(1)} %pad_add_fusion.place, f32[16,3]{1,0:T(8,128)S(1)} %copy-done, f32[23,8,128]{2,1,0:T(8,128)S(1)} %shard_map.47.coef, ...), custom_call_target="tpu_custom_call" | custom-call | bytes 3690000 | tf_op jit(solution)/shard_map/pallas_call | solution.py:476
  40.0 1.8 %collective-permute-start.4 = (f32[16,2,4,2,8,128]{5,4,3,2,1,0:T(8,128)S(1)}, f32[16,2,4,2,8,128]{5,4,3,2,1,0:T(8,128)S(1)}, u32[]{:S(2)}, u32[]{:S(2)}) collective-permute-start(f32[16,2,4,2,8,128]{5,4,3,2,1,0:T(8,128)S(1)} %get-tuple-element.27.x), channel_id=1, source_target_pairs={{0,16},{128,144},{1,17},{129,145},{161,177},{33,49},{160,176},{32,... | collective-permute-start | bytes 3145736 | tf_op jit(solution)/shard_map/ppermute | solution.py:447
  41.8 1.9 %collective-permute-start.5 = (f32[16,4,2,8,128]{4,3,2,1,0:T(8,128)S(1)}, f32[16,4,2,8,128]{4,3,2,1,0:T(8,128)S(1)}, u32[]{:S(2)}, u32[]{:S(2)}) collective-permute-start(f32[16,4,2,8,128]{4,3,2,1,0:T(8,128)S(1)} %get-tuple-element.28), channel_id=1, source_target_pairs={{16,2},{144,130},{17,3},{145,131},{177,163},{49,35},{176,162},{48,... | collective-permute-start | bytes 1572872 | tf_op jit(solution)/shard_map/ppermute | solution.py:446
  45.0 1.6 %shard_map.51.part = f32[16,2,4,2,8,128]{5,4,3,2,1,0:T(8,128)S(1)} custom-call(s32[2]{0:T(128)S(1)} %pad_add_fusion.place, f32[16,3]{1,0:T(8,128)S(1)} %copy-done, f32[23,8,128]{2,1,0:T(8,128)S(1)} %shard_map.47.coef, f32[16,2,4,2,8,128]{5,4,3,2,1,0:T(8,128)S(1)} %get-tuple-element.23.x0.x, f32[16,2,4,2,8,128]{5,4,3,2,1,0:T(8,128)S(1)} %get-tuple-element.27.x, ...), custom_call_target="tpu_custom_call" | custom-call | bytes 7380000 | tf_op jit(solution)/shard_map/pallas_call | solution.py:450
  46.6 2.2 %collective-permute-done.6.row_a = f32[16,2,8,128]{3,2,1,0:T(8,128)S(1)} collective-permute-done((f32[16,2,8,128]{3,2,1,0:T(8,128)S(1)}, f32[16,2,8,128]{3,2,1,0:T(8,128)S(1)}, u32[]{:S(2)}, u32[]{:S(2)}) %collective-permute-start.6) | collective-permute-done | bytes 131104 | tf_op jit(solution)/shard_map/ppermute | solution.py:448
  48.8 3.5 %collective-permute-done.5.outer = f32[16,4,2,8,128]{4,3,2,1,0:T(8,128)S(1)} collective-permute-done((f32[16,4,2,8,128]{4,3,2,1,0:T(8,128)S(1)}, f32[16,4,2,8,128]{4,3,2,1,0:T(8,128)S(1)}, u32[]{:S(2)}, u32[]{:S(2)}) %collective-permute-start.5) | collective-permute-done | bytes 524320 | tf_op jit(solution)/shard_map/ppermute | solution.py:446
  52.3 1.2 %shard_map.52 = (f32[16,2,4,2,8,128]{5,4,3,2,1,0:T(8,128)S(1)}, f32[16,4,2,8,128]{4,3,2,1,0:T(8,128)S(1)}, f32[16,2,8,128]{3,2,1,0:T(8,128)S(1)}, f32[16,2,8,128]{3,2,1,0:T(8,128)S(1)}) custom-call(s32[2]{0:T(128)S(1)} %pad_add_fusion.place, f32[16,3]{1,0:T(8,128)S(1)} %copy-done, f32[23,8,128]{2,1,0:T(8,128)S(1)} %shard_map.47.coef, ...), custom_call_target="tpu_custom_call" | custom-call | bytes 3690000 | tf_op jit(solution)/shard_map/pallas_call | solution.py:476
  53.5 1.3 %collective-permute-start.8 = (f32[16,2,4,2,8,128]{5,4,3,2,1,0:T(8,128)S(1)}, f32[16,2,4,2,8,128]{5,4,3,2,1,0:T(8,128)S(1)}, u32[]{:S(2)}, u32[]{:S(2)}) collective-permute-start(f32[16,2,4,2,8,128]{5,4,3,2,1,0:T(8,128)S(1)} %get-tuple-element.31.x), channel_id=1, source_target_pairs={{0,16},{128,144},{1,17},{129,145},{161,177},{33,49},{160,176},{32,... | collective-permute-start | bytes 3145736 | tf_op jit(solution)/shard_map/ppermute | solution.py:447
  54.8 1.9 %collective-permute-start.9 = (f32[16,4,2,8,128]{4,3,2,1,0:T(8,128)S(1)}, f32[16,4,2,8,128]{4,3,2,1,0:T(8,128)S(1)}, u32[]{:S(2)}, u32[]{:S(2)}) collective-permute-start(f32[16,4,2,8,128]{4,3,2,1,0:T(8,128)S(1)} %get-tuple-element.32), channel_id=1, source_target_pairs={{16,2},{144,130},{17,3},{145,131},{177,163},{49,35},{176,162},{48,... | collective-permute-start | bytes 1572872 | tf_op jit(solution)/shard_map/ppermute | solution.py:446
  58.0 1.6 %shard_map.53.part = f32[16,2,4,2,8,128]{5,4,3,2,1,0:T(8,128)S(1)} custom-call(s32[2]{0:T(128)S(1)} %pad_add_fusion.place, f32[16,3]{1,0:T(8,128)S(1)} %copy-done, f32[23,8,128]{2,1,0:T(8,128)S(1)} %shard_map.47.coef, f32[16,2,4,2,8,128]{5,4,3,2,1,0:T(8,128)S(1)} %get-tuple-element.23.x0.x, f32[16,2,4,2,8,128]{5,4,3,2,1,0:T(8,128)S(1)} %get-tuple-element.31.x, ...), custom_call_target="tpu_custom_call" | custom-call | bytes 7380000 | tf_op jit(solution)/shard_map/pallas_call | solution.py:450
  59.6 2.2 %collective-permute-done.10.row_a = f32[16,2,8,128]{3,2,1,0:T(8,128)S(1)} collective-permute-done((f32[16,2,8,128]{3,2,1,0:T(8,128)S(1)}, f32[16,2,8,128]{3,2,1,0:T(8,128)S(1)}, u32[]{:S(2)}, u32[]{:S(2)}) %collective-permute-start.10) | collective-permute-done | bytes 131104 | tf_op jit(solution)/shard_map/ppermute | solution.py:448
  61.8 3.5 %collective-permute-done.9.outer = f32[16,4,2,8,128]{4,3,2,1,0:T(8,128)S(1)} collective-permute-done((f32[16,4,2,8,128]{4,3,2,1,0:T(8,128)S(1)}, f32[16,4,2,8,128]{4,3,2,1,0:T(8,128)S(1)}, u32[]{:S(2)}, u32[]{:S(2)}) %collective-permute-start.9) | collective-permute-done | bytes 524320 | tf_op jit(solution)/shard_map/ppermute | solution.py:446
  65.3 1.4 %shard_map.54 = f32[32,4,2,8,128]{4,3,2,1,0:T(8,128)S(1)} custom-call(s32[2]{0:T(128)S(1)} %pad_add_fusion.place, f32[16,3]{1,0:T(8,128)S(1)} %copy-done, f32[23,8,128]{2,1,0:T(8,128)S(1)} %shard_map.47.coef, f32[16,2,4,2,8,128]{5,4,3,2,1,0:T(8,128)S(1)} %shard_map.53.part, f32[16,4,2,8,128]{4,3,2,1,0:T(8,128)S(1)} %collective-permute-done.9.outer, ...), custom_call_target="tpu_custom_call" | custom-call | bytes 3690000 | tf_op jit(solution)/shard_map/pallas_call | solution.py:479
  66.8 21.5 %all_to_all.10.src = f32[32,4,2,8,128]{4,3,2,1,0:T(8,128)S(1)} all-to-all(f32[32,4,2,8,128]{4,3,2,1,0:T(8,128)S(1)} %shard_map.54), channel_id=1, replica_groups=mesh['xl'=2,'y'=4,'c'=2,'z'=8,'xh'=2] {'xl','y','c','xh'}, dimensions={0} | all-to-all | bytes 2097152 | tf_op jit(solution)/shard_map/all_to_all | solution.py:443
  88.3 1.0 %shard_map.55 = f32[4,2,2,128,128]{4,3,2,1,0:T(8,128)} custom-call(f32[32,4,2,8,128]{4,3,2,1,0:T(8,128)S(1)} %all_to_all.10.src), custom_call_target="tpu_custom_call" | custom-call | tf_op jit(solution)/shard_map/pallas_call | solution.py:482
  (20 shorter events, 4.1 us)
Async XLA Ops:
  2.0 7.6 %copy-start.1 = (s32[128,128]{1,0:T(8,128)S(1)}, s32[128,128]{1,0:T(8,128)}, u32[]{:S(2)}) copy-start(s32[128,128]{1,0:T(8,128)} %regions.1) | copy-start | bytes 196612
  2.0 25.0 %all-to-all-start = ((f32[32,4,2,8,128]{4,3,2,1,0:T(8,128)}), f32[32,4,2,8,128]{4,3,2,1,0:T(8,128)S(1)}, u32[]{:S(2)}, u32[]{:S(2)}) async-start(f32[32,4,2,8,128]{4,3,2,1,0:T(8,128)} %shard_map.46), calls=%async_computation | async-start | bytes 2097152 | tf_op jit(solution)/shard_map/all_to_all | solution.py:443
  9.5 0.7 copy-start.2
  10.2 16.8 %copy-start = (f32[16,3]{1,0:T(8,128)S(1)}, f32[16,3]{1,0:T(8,128)}, u32[]{:S(2)}) copy-start(f32[16,3]{1,0:T(8,128)} %constant.38.clone.lam) | copy-start | bytes 580
  28.3 3.1 %collective-permute-start = (f32[16,2,4,2,8,128]{5,4,3,2,1,0:T(8,128)S(1)}, f32[16,2,4,2,8,128]{5,4,3,2,1,0:T(8,128)S(1)}, u32[]{:S(2)}, u32[]{:S(2)}) collective-permute-start(f32[16,2,4,2,8,128]{5,4,3,2,1,0:T(8,128)S(1)} %get-tuple-element.23.x0.x), channel_id=1, source_target_pairs={{0,16},{128,144},{1,17},{129,145},{161,177},{33,49},{160,176},{32,... | collective-permute-start | bytes 3145736 | tf_op jit(solution)/shard_map/ppermute | solution.py:447
  28.4 10.5 %collective-permute-start.1 = (f32[16,4,2,8,128]{4,3,2,1,0:T(8,128)S(1)}, f32[16,4,2,8,128]{4,3,2,1,0:T(8,128)S(1)}, u32[]{:S(2)}, u32[]{:S(2)}) collective-permute-start(f32[16,4,2,8,128]{4,3,2,1,0:T(8,128)S(1)} %get-tuple-element.24), channel_id=1, source_target_pairs={{16,2},{144,130},{17,3},{145,131},{177,163},{49,35},{176,162},{48,... | collective-permute-start | bytes 1572872 | tf_op jit(solution)/shard_map/ppermute | solution.py:446
  30.5 5.1 %collective-permute-start.2 = (f32[16,2,8,128]{3,2,1,0:T(8,128)S(1)}, f32[16,2,8,128]{3,2,1,0:T(8,128)S(1)}, u32[]{:S(2)}, u32[]{:S(2)}) collective-permute-start(f32[16,2,8,128]{3,2,1,0:T(8,128)S(1)} %get-tuple-element.25), channel_id=1, source_target_pairs={{0,128},{16,144},{1,129},{17,145},{161,33},{177,49},{160,32},{176,... | collective-permute-start | bytes 393224 | tf_op jit(solution)/shard_map/ppermute | solution.py:448
  30.7 4.8 %collective-permute-start.3 = (f32[16,2,8,128]{3,2,1,0:T(8,128)S(1)}, f32[16,2,8,128]{3,2,1,0:T(8,128)S(1)}, u32[]{:S(2)}, u32[]{:S(2)}) collective-permute-start(f32[16,2,8,128]{3,2,1,0:T(8,128)S(1)} %get-tuple-element.26), channel_id=1, source_target_pairs={{128,1},{144,17},{129,161},{145,177},{33,160},{49,176},{32,64},{48... | collective-permute-start | bytes 393224 | tf_op jit(solution)/shard_map/ppermute | solution.py:449
  40.0 5.0 %collective-permute-start.4 = (f32[16,2,4,2,8,128]{5,4,3,2,1,0:T(8,128)S(1)}, f32[16,2,4,2,8,128]{5,4,3,2,1,0:T(8,128)S(1)}, u32[]{:S(2)}, u32[]{:S(2)}) collective-permute-start(f32[16,2,4,2,8,128]{5,4,3,2,1,0:T(8,128)S(1)} %get-tuple-element.27.x), channel_id=1, source_target_pairs={{0,16},{128,144},{1,17},{129,145},{161,177},{33,49},{160,176},{32,... | collective-permute-start | bytes 3145736 | tf_op jit(solution)/shard_map/ppermute | solution.py:447
  41.8 10.5 %collective-permute-start.5 = (f32[16,4,2,8,128]{4,3,2,1,0:T(8,128)S(1)}, f32[16,4,2,8,128]{4,3,2,1,0:T(8,128)S(1)}, u32[]{:S(2)}, u32[]{:S(2)}) collective-permute-start(f32[16,4,2,8,128]{4,3,2,1,0:T(8,128)S(1)} %get-tuple-element.28), channel_id=1, source_target_pairs={{16,2},{144,130},{17,3},{145,131},{177,163},{49,35},{176,162},{48,... | collective-permute-start | bytes 1572872 | tf_op jit(solution)/shard_map/ppermute | solution.py:446
  43.7 5.1 %collective-permute-start.6 = (f32[16,2,8,128]{3,2,1,0:T(8,128)S(1)}, f32[16,2,8,128]{3,2,1,0:T(8,128)S(1)}, u32[]{:S(2)}, u32[]{:S(2)}) collective-permute-start(f32[16,2,8,128]{3,2,1,0:T(8,128)S(1)} %get-tuple-element.29), channel_id=1, source_target_pairs={{0,128},{16,144},{1,129},{17,145},{161,33},{177,49},{160,32},{176,... | collective-permute-start | bytes 393224 | tf_op jit(solution)/shard_map/ppermute | solution.py:448
  44.3 4.5 %collective-permute-start.7 = (f32[16,2,8,128]{3,2,1,0:T(8,128)S(1)}, f32[16,2,8,128]{3,2,1,0:T(8,128)S(1)}, u32[]{:S(2)}, u32[]{:S(2)}) collective-permute-start(f32[16,2,8,128]{3,2,1,0:T(8,128)S(1)} %get-tuple-element.30), channel_id=1, source_target_pairs={{128,1},{144,17},{129,161},{145,177},{33,160},{49,176},{32,64},{48... | collective-permute-start | bytes 393224 | tf_op jit(solution)/shard_map/ppermute | solution.py:449
  53.5 4.5 %collective-permute-start.8 = (f32[16,2,4,2,8,128]{5,4,3,2,1,0:T(8,128)S(1)}, f32[16,2,4,2,8,128]{5,4,3,2,1,0:T(8,128)S(1)}, u32[]{:S(2)}, u32[]{:S(2)}) collective-permute-start(f32[16,2,4,2,8,128]{5,4,3,2,1,0:T(8,128)S(1)} %get-tuple-element.31.x), channel_id=1, source_target_pairs={{0,16},{128,144},{1,17},{129,145},{161,177},{33,49},{160,176},{32,... | collective-permute-start | bytes 3145736 | tf_op jit(solution)/shard_map/ppermute | solution.py:447
  54.8 10.5 %collective-permute-start.9 = (f32[16,4,2,8,128]{4,3,2,1,0:T(8,128)S(1)}, f32[16,4,2,8,128]{4,3,2,1,0:T(8,128)S(1)}, u32[]{:S(2)}, u32[]{:S(2)}) collective-permute-start(f32[16,4,2,8,128]{4,3,2,1,0:T(8,128)S(1)} %get-tuple-element.32), channel_id=1, source_target_pairs={{16,2},{144,130},{17,3},{145,131},{177,163},{49,35},{176,162},{48,... | collective-permute-start | bytes 1572872 | tf_op jit(solution)/shard_map/ppermute | solution.py:446
  56.7 5.1 %collective-permute-start.10 = (f32[16,2,8,128]{3,2,1,0:T(8,128)S(1)}, f32[16,2,8,128]{3,2,1,0:T(8,128)S(1)}, u32[]{:S(2)}, u32[]{:S(2)}) collective-permute-start(f32[16,2,8,128]{3,2,1,0:T(8,128)S(1)} %get-tuple-element.33), channel_id=1, source_target_pairs={{0,128},{16,144},{1,129},{17,145},{161,33},{177,49},{160,32},{176,... | collective-permute-start | bytes 393224 | tf_op jit(solution)/shard_map/ppermute | solution.py:448
  57.3 4.5 %collective-permute-start.11 = (f32[16,2,8,128]{3,2,1,0:T(8,128)S(1)}, f32[16,2,8,128]{3,2,1,0:T(8,128)S(1)}, u32[]{:S(2)}, u32[]{:S(2)}) collective-permute-start(f32[16,2,8,128]{3,2,1,0:T(8,128)S(1)} %get-tuple-element.34), channel_id=1, source_target_pairs={{128,1},{144,17},{129,161},{145,177},{33,160},{49,176},{32,64},{48... | collective-permute-start | bytes 393224 | tf_op jit(solution)/shard_map/ppermute | solution.py:449

commit v4 on v3

--- a/solution.py
+++ b/solution.py
@@ -50,6 +50,15 @@
 def row_swap(parity):
     low = [p for p in range(15) if p % 2 == parity]
     return both([(device_index(z, p, c), device_index(z, p + 1, c)) for z in range(8) for p in low for c in range(2)])
+
+
+def core_index():
+    return lax.axis_index("c")
+
+
+def row_block():
+    x, y = lax.axis_index("xh") * 2 + lax.axis_index("xl"), lax.axis_index("y")
+    return y * 4 + jnp.where(y % 2 == 1, 3 - x, x)
 
 
 def rows():
@@ -165,11 +174,11 @@
         copy.wait()
 
 
-(A, AE, AW, AN, AS, AH, AC, GE, GW, GN, GS, GH, G, KE, KW, KN, KS, KH, KZ, HKD, DN, DS, DH) = range(23)
-
-
-def coefficient_kernel(place, material, regions, coef):
-    pos = place[1]
+(A, AE, AW, AN, AS, AH, AC, GE, GW, GN, GS, GH, G, KE, KW, KN, KS, KH, KZ, DN, DS, DH) = range(22)
+
+
+def coefficient_kernel(material, regions, coef, table):
+    pos = row_block()
     r, l = rows(), lanes()
     there = [l < 127, l > 0, (r < 7) | (pos < 15), (r > 0) | (pos > 0)]
     has_e, has_w = [jnp.where(t, 1.0, 0.0).astype(jnp.float32) for t in there[:2]]
@@ -204,21 +213,26 @@
         return jnp.where(r == 0, south, jnp.where(r == 7, north, zero))
 
     g = 0.3 * a
-    table = [
+    half_diag = 0.5 * (ke + kw + kn + ks + 2.0 * axial)
+    tiles = [
         a, a * se * has_e, a * sw * has_w, a * sn * in_n, a * ss * in_s, beside(a * ss, a * sn), a * shear,
         g * has_e, g * has_w, g * in_n, g * in_s, beside(-g, g), g,
         0.5 * ke * has_e, 0.5 * kw * has_w, 0.5 * kn * in_n, 0.5 * ks * in_s, beside(0.5 * ks, 0.5 * kn),
-        0.5 * axial, 0.5 * (ke + kw + kn + ks + 2.0 * axial),
+        0.5 * axial,
         0.3 * in_n, 0.3 * in_s, beside(zero - 0.3, zero + 0.3),
     ]
-    for n, v in enumerate(table):
+    for n, v in enumerate(tiles):
         coef[n] = v
-
-
-def inverse_diagonal(lam, q, half_diag):
-    d0, d1, di = half_diag + 0.5 * lam[q, 0], half_diag + 0.5 * lam[q, 1], -0.5 * lam[q, 2]
-    inv = 0.8 / (d0 * d1 + di * di)
-    return inv * d1, inv * d0, inv * di
+    for q in range(PAIRS):
+        m00, m11, m01 = 0.0, 2.0, 0.0
+        if q:
+            angle = 2 * math.pi * q / STEPS
+            m00 = m11 = 1 - math.cos(angle)
+            m01 = -math.sin(angle)
+        d0, d1, di = half_diag + 0.5 * m00, half_diag + 0.5 * m11, -0.5 * m01
+        inv = 0.8 / (d0 * d1 + di * di)
+        for n, v in enumerate((zero + m00, zero + m11, zero + m01, inv * d1, inv * d0, inv * di)):
+            table[q, n] = v
 
 
 def first_iterate(f, tiles, a, diagonal):
@@ -229,21 +243,26 @@
     return b00 * re + b01 * im, b11 * im - b01 * re
 
 
-def send(place, q, planes, row_a, row_b):
-    r = rows()
-    even = (r * 0 + place[1] % 2) == 0
-    for p, tiles in planes:
-        after = before = None
-        for j in range(8):
-            f, c = divmod(j, 2)
-            seven, zero = roll(tiles[f][c], j + 1), roll(tiles[f][c], j - 1)
-            after = seven if j == 0 else jnp.where(r == j, seven, after)
-            before = zero if j == 0 else jnp.where(r == (j - 1) % 8, zero, before)
+TALL = 8 * 2 * FIELDS
+
+
+def tile(j):
+    return pl.ds(8 * j, 8)
+
+
+def every(row):
+    return pl.ds(row, 8, stride=8)
+
+
+def send(q, block, row_a, row_b):
+    even = (rows() * 0 + row_block() % 2) == 0
+    for p in range(2):
+        after, before = block[q, p, every(7), :], block[q, p, every(0), :]
         row_a[q, p] = jnp.where(even, after, before)
         row_b[q, p] = jnp.where(even, before, after)
 
 
-def spectrum_kernel(place, lam, coef, src, x0, outer, row_a, row_b, spec):
+def spectrum_kernel(coef, table, src, x0, outer, row_a, row_b, spec):
     def body(f, _):
         for p in range(2):
             got = rfft([src[(t // 2) * 2 + p, f, t % 2] for t in range(STEPS)])
@@ -256,49 +275,44 @@
     lax.fori_loop(0, FIELDS, body, 0)
 
     def pair(q, _):
-        diagonal = inverse_diagonal(lam, q, coef[HKD])
-        planes = [
-            [first_iterate(f, (spec[q, p, f, 0], spec[q, p, f, 1]), coef[A], diagonal) for f in range(FIELDS)]
-            for p in range(2)
-        ]
+        diagonal = table[q, 3], table[q, 4], table[q, 5]
         for p in range(2):
             for f in range(FIELDS):
+                got = first_iterate(f, (spec[q, p, f, 0], spec[q, p, f, 1]), coef[A], diagonal)
                 for c in range(2):
-                    x0[q, p, f, c] = planes[p][f][c]
-        for f in range(FIELDS):
-            for c in range(2):
-                outer[q, f, c] = x0[q, place[0], f, c]
-        send(place, q, list(enumerate(planes)), row_a, row_b)
+                    x0[q, p, tile(2 * f + c), :] = got[c]
+        outer[q] = x0[q, core_index()]
+        send(q, x0, row_a, row_b)
         return 0
 
     lax.fori_loop(0, PAIRS, pair, 0, unroll=UNROLL)
 
 
-def own_kernel(place, lam, coef, x0, x, sib, part):
+def own_kernel(coef, table, x0, x, sib, part):
     l = lanes()
     east = jnp.where(l == 127, 0.0, 0.3).astype(jnp.float32)
     west = jnp.where(l == 0, 0.0, 0.3).astype(jnp.float32)
-    core = place[0]
+    core = core_index()
     sign = 1.0 - 2.0 * core.astype(jnp.float32)
 
     def pair(q, _):
-        m00, m11, m01 = lam[q, 0], lam[q, 1], lam[q, 2]
-        pa, pb, pc = inverse_diagonal(lam, q, coef[HKD])
+        m00, m11, m01 = table[q, 0], table[q, 1], table[q, 2]
+        pa, pb, pc = table[q, 3], table[q, 4], table[q, 5]
         for p, edge in ((core, True), (1 - core, False)):
             new = [[None, None] for _ in range(FIELDS)]
             div, flow = [None, None], [None, None]
             for c in range(2):
-                cur = [x[q, p, f, c] for f in range(FIELDS)]
+                cur = [x[q, p, tile(2 * f + c), :] for f in range(FIELDS)]
                 es = [pltpu.roll(v, 127, 1) for v in cur]
                 ws = [pltpu.roll(v, 1, 1) for v in cur]
                 ns = [roll(v, 7) for v in cur]
                 ss = [roll(v, 1) for v in cur]
                 if edge:
-                    total = [sib[q, core, f, c] for f in range(FIELDS)]
+                    total = [sib[q, core, tile(2 * f + c), :] for f in range(FIELDS)]
                     drop_u, drop_p = sign * total[2], sign * total[3]
                 else:
-                    dn = [sib[q, 0, f, c] for f in range(FIELDS)]
-                    up = [sib[q, 1, f, c] for f in range(FIELDS)]
+                    dn = [sib[q, 0, tile(2 * f + c), :] for f in range(FIELDS)]
+                    up = [sib[q, 1, tile(2 * f + c), :] for f in range(FIELDS)]
                     total = [u + d for u, d in zip(up, dn)]
                     drop_u, drop_p = up[2] - dn[2], up[3] - dn[3]
                 grad = [
@@ -307,10 +321,10 @@
                     coef[G] * drop_p,
                 ]
                 for f in range(3):
-                    v = (x0[q, p, f, c] + 0.2 * cur[f]) + coef[AE] * es[f] + coef[AW] * ws[f]
+                    v = (x0[q, p, tile(2 * f + c), :] + 0.2 * cur[f]) + coef[AE] * es[f] + coef[AW] * ws[f]
                     v = v + coef[AN] * ns[f] + coef[AS] * ss[f]
-                    part[q, p, f, c] = v + coef[AC] * total[f] - grad[f]
-                new[3][c] = x0[q, p, 3, c] + 0.2 * cur[3]
+                    part[q, p, tile(2 * f + c), :] = v + coef[AC] * total[f] - grad[f]
+                new[3][c] = x0[q, p, tile(6 + c), :] + 0.2 * cur[3]
                 flow[c] = (
                     coef[KE] * es[3]
                     + coef[KW] * ws[3]
@@ -321,38 +335,36 @@
                 div[c] = east * es[0] - west * ws[0] + coef[DN] * ns[1] - coef[DS] * ss[1] + 0.3 * drop_u
             g0 = flow[0] - (m00 * div[0] + m01 * div[1])
             g1 = flow[1] - (m11 * div[1] - m01 * div[0])
-            part[q, p, 3, 0] = new[3][0] + pa * g0 + pc * g1
-            part[q, p, 3, 1] = new[3][1] + pb * g1 - pc * g0
+            part[q, p, tile(6), :] = new[3][0] + pa * g0 + pc * g1
+            part[q, p, tile(7), :] = new[3][1] + pb * g1 - pc * g0
         return 0
 
     lax.fori_loop(0, PAIRS, pair, 0, unroll=UNROLL)
 
 
-def finish(place, lam, q, coef, part, outer, row_a, row_b):
+def finish(q, coef, table, part, outer, row_a, row_b, edges):
     r = rows()
-    core = place[0]
+    core = core_index()
     sign = 2.0 * core.astype(jnp.float32) - 1.0
-    odd = r * 0 + place[1] % 2
-    m00, m11, m01 = lam[q, 0], lam[q, 1], lam[q, 2]
-    pa, pb, pc = inverse_diagonal(lam, q, coef[HKD])
+    even = (r * 0 + row_block() % 2) == 0
+    m00, m11, m01 = table[q, 0], table[q, 1], table[q, 2]
+    pa, pb, pc = table[q, 3], table[q, 4], table[q, 5]
     result = []
-    for p, edge in ((core, True), (1 - core, False)):
+    for n, p, edge in ((0, core, True), (1, 1 - core, False)):
         a, b = row_a[q, p], row_b[q, p]
+        edges[q % UNROLL, n, every(0), :] = jnp.where(even, b, a)
+        edges[q % UNROLL, n, every(7), :] = jnp.where(even, a, b)
         new = [[None, None] for _ in range(FIELDS)]
         div, flow = [None, None], [None, None]
         for c in range(2):
-            beside = []
-            for f in range(FIELDS):
-                j = 2 * f + c
-                low_is_b = (jnp.where(r == j, 1, 0) ^ odd) == 1
-                beside.append(roll(jnp.where(low_is_b, b, a), -j))
+            beside = [edges[q % UNROLL, n, tile(2 * f + c), :] for f in range(FIELDS)]
             for f in range(3):
-                new[f][c] = part[q, p, f, c] + coef[AH] * beside[f]
+                new[f][c] = part[q, p, tile(2 * f + c), :] + coef[AH] * beside[f]
             new[1][c] = new[1][c] - coef[GH] * beside[3]
             flow[c] = coef[KH] * beside[3]
             div[c] = coef[DH] * beside[1]
             if edge:
-                out = [outer[q, f, c] for f in range(FIELDS)]
+                out = [outer[q, tile(2 * f + c), :] for f in range(FIELDS)]
                 for f in range(3):
                     new[f][c] = new[f][c] + coef[AC] * out[f]
                 new[2][c] = new[2][c] - (sign * coef[G]) * out[3]
@@ -360,36 +372,38 @@
                 div[c] = div[c] + (0.3 * sign) * out[2]
         g0 = flow[0] - (m00 * div[0] + m01 * div[1])
         g1 = flow[1] - (m11 * div[1] - m01 * div[0])
-        new[3][0] = part[q, p, 3, 0] + pa * g0 + pc * g1
-        new[3][1] = part[q, p, 3, 1] + pb * g1 - pc * g0
+        new[3][0] = part[q, p, tile(6), :] + pa * g0 + pc * g1
+        new[3][1] = part[q, p, tile(7), :] + pb * g1 - pc * g0
         result.append((p, new))
     return result
 
 
-def round_kernel(place, lam, coef, part, outer, row_a, row_b, y, next_outer, next_a, next_b):
+def clear(edges):
+    edges[...] = jnp.zeros(edges.shape, jnp.float32)
+
+
+def round_kernel(coef, table, part, outer, row_a, row_b, y, next_outer, next_a, next_b, edges):
+    clear(edges)
+
     def pair(q, _):
-        planes = finish(place, lam, q, coef, part, outer, row_a, row_b)
-        for p, tiles in planes:
-            for f in range(FIELDS):
-                for c in range(2):
-                    y[q, p, f, c] = tiles[f][c]
-        for f in range(FIELDS):
-            for c in range(2):
-                next_outer[q, f, c] = planes[0][1][f][c]
-        send(place, q, planes, next_a, next_b)
+        for p, tiles in finish(q, coef, table, part, outer, row_a, row_b, edges):
+            for j in range(2 * FIELDS):
+                y[q, p, tile(j), :] = tiles[j // 2][j % 2]
+        next_outer[q] = y[q, core_index()]
+        send(q, y, next_a, next_b)
         return 0
 
     lax.fori_loop(0, PAIRS, pair, 0, unroll=UNROLL)
 
 
-def last_kernel(place, lam, coef, part, outer, row_a, row_b, out, y):
+def last_kernel(coef, table, part, outer, row_a, row_b, out, y, edges):
+    clear(edges)
     scale32 = np.float32(1.0 / STEPS)
 
     def pair(q, _):
-        for p, tiles in finish(place, lam, q, coef, part, outer, row_a, row_b):
-            for f in range(FIELDS):
-                for c in range(2):
-                    y[q, p, f, c] = tiles[f][c] * scale32
+        for p, tiles in finish(q, coef, table, part, outer, row_a, row_b, edges):
+            for j in range(2 * FIELDS):
+                y[q, p, j // 2, j % 2] = tiles[j // 2][j % 2] * scale32
         return 0
 
     lax.fori_loop(0, PAIRS, pair, 0, unroll=UNROLL)
@@ -422,22 +436,13 @@
     )
 
 
-def lam_table():
-    k = np.arange(1, PAIRS)
-    real, imag = 1 - np.cos(2 * np.pi * k / STEPS), np.sin(2 * np.pi * k / STEPS)
-    rest = np.stack([real, real, -imag], axis=1)
-    return np.concatenate([[[0.0, 2.0, 0.0]], rest]).astype(np.float32)
-
-
 def on_device(sources, regions, material):
     vmem, smem = pltpu.VMEM, pltpu.SMEM
-    x = lax.axis_index("xh") * 2 + lax.axis_index("xl")
-    y = lax.axis_index("y")
-    pos = y * 4 + jnp.where(y % 2 == 1, 3 - x, x)
-    place = jnp.stack([lax.axis_index("c"), pos]).astype(jnp.int32)
     piece = (32, FIELDS, 2, 8, 128)
-    block = (PAIRS, 2, FIELDS, 2, 8, 128)
-    messages = [(PAIRS, FIELDS, 2, 8, 128), (PAIRS, 2, 8, 128), (PAIRS, 2, 8, 128)]
+    block = (PAIRS, 2, TALL, 128)
+    apart = (PAIRS, 2, FIELDS, 2, 8, 128)
+    messages = [(PAIRS, TALL, 128), (PAIRS, 2, 8, 128), (PAIRS, 2, 8, 128)]
+    edges = (UNROLL, 2, TALL, 128)
 
     def level(v):
         return lax.all_to_all(v, LEVEL, 0, 0, tiled=True)
@@ -447,7 +452,7 @@
         sib = lax.ppermute(v, AXES, sibling_swap())
         row_a = lax.ppermute(row_a, AXES, row_swap(0))
         row_b = lax.ppermute(row_b, AXES, row_swap(1))
-        part = call(own_kernel, [block], [smem, smem] + [vmem] * 4, limit=8, micros=2)(place, lam, coef, x0, v, sib)
+        part = call(own_kernel, [block], [vmem] * 5, limit=8, micros=2)(coef, table, x0, v, sib)
         return part, outer, row_a, row_b
 
     whole = (FIELDS, 2, 2, 128, 128)
@@ -465,19 +470,18 @@
         compiler_params=pltpu.CompilerParams(vmem_limit_bytes=60 * MIB),
     )(sources)
     arrived = level(pieces)
-    coef = call(coefficient_kernel, [(23, 8, 128)], [smem, smem, vmem])(place, material, regions)
-    arrived, coef, place = lax.optimization_barrier((arrived, coef, place))
-    lam = jnp.asarray(lam_table())
-    x0, *out = call(spectrum_kernel, [block] + messages, [smem, smem, vmem, vmem], [block], 8)(
-        place, lam, coef, arrived
+    coef, table = call(coefficient_kernel, [(22, 8, 128), (PAIRS, 6, 8, 128)], [smem, vmem])(material, regions)
+    arrived, coef, table = lax.optimization_barrier((arrived, coef, table))
+    x0, *out = call(spectrum_kernel, [block] + messages, [vmem] * 3, [apart], 8)(
+        coef, table, arrived
     )
     x = x0
     for _ in range(2):
-        x, *out = call(round_kernel, [block] + messages, [smem, smem] + [vmem] * 5, limit=8)(
-            place, lam, coef, *exchange(x, *out)
+        x, *out = call(round_kernel, [block] + messages, [vmem] * 6, [edges], 8)(
+            coef, table, *exchange(x, *out)
         )
-    answer = call(last_kernel, [piece], [smem, smem] + [vmem] * 5, [block], 8)(
-        place, lam, coef, *exchange(x, *out)
+    answer = call(last_kernel, [piece], [vmem] * 6, [apart, edges], 8)(
+        coef, table, *exchange(x, *out)
     )
     return pl.pallas_call(
         join_kernel,

time: 89.8 us -> 86.8 us (0.967)
  Pallas kernels: 13.6 us -> 8.51 us
  waiting for transfers between devices: 33.4 us -> 36.2 us
    pallas_call x8, Pallas kernels: 10.5 us -> 5.48 us  [the longest x3 2.7 us: exchange(): call(own_kernel, [block], [vmem] * 5, limit=8, micros=2)]
    ppermute x3, waiting for transfers between devices: 6.87 us -> 9.03 us  [exchange(): row_a = lax.ppermute(row_a, AXES, row_swap(0))]
  transfers between devices with their start and end apart: 13 -> 13, of which waited for: 7 -> 7; matrix products, arithmetic and copies ran while one was open for 0% -> 0% of each run, Pallas kernels for 6% -> 4%
where the time goes in v4:
time: 86.8 us; the launch traced here: 86.4 us
  waiting for transfers between devices  36.2 us (42%)
  blocking collectives  21.6 us (25%)
  starting transfers between devices  19.9 us (23%)
  Pallas kernels  8.51 us (10%)
    all_to_all x1, blocking collectives, level(): return lax.all_to_all(v, LEVEL, 0, 0, tiled=True)  21.6 us
    all_to_all x1, waiting for transfers between devices, level(): return lax.all_to_all(v, LEVEL, 0, 0, tiled=True)  16.8 us
    ppermute x3, waiting for transfers between devices, exchange(): outer = lax.ppermute(outer, AXES, level_swap())  10.4 us
    ppermute x3, waiting for transfers between devices, exchange(): row_a = lax.ppermute(row_a, AXES, row_swap(0))  9.03 us
    all_to_all x1, starting transfers between devices, level(): return lax.all_to_all(v, LEVEL, 0, 0, tiled=True)  7.46 us
    ppermute x3, starting transfers between devices, exchange(): outer = lax.ppermute(outer, AXES, level_swap())  5.92 us
    ppermute x3, starting transfers between devices, exchange(): sib = lax.ppermute(v, AXES, sibling_swap())  3.2 us
    pallas_call x3, Pallas kernels, exchange(): call(own_kernel, [block], [vmem] * 5, limit=8, micros=2)  2.7 us
  transfers between devices with their start and end apart: 13, of which 7 were waited for; matrix products, arithmetic and copies ran while one was open for 0% of the time, Pallas kernels for 4%

profile of v4, /device:TPU:96, one launch (start us, length us, event | category | flops | bytes accessed | tf_op | source)
XLA Modules:
  0.0 86.4 jit_solution(13742286433996529507)
XLA Ops:
  0.0 2.0 %shard_map.37 = f32[32,4,2,8,128]{4,3,2,1,0:T(8,128)} custom-call(f32[4,2,2,128,128]{4,3,2,1,0:T(8,128)} %src.1), custom_call_target="tpu_custom_call" | custom-call | tf_op jit(solution)/shard_map/pallas_call | solution.py:459
  2.0 7.5 %all-to-all-start = ((f32[32,4,2,8,128]{4,3,2,1,0:T(8,128)}), f32[32,4,2,8,128]{4,3,2,1,0:T(8,128)S(1)}, u32[]{:S(2)}, u32[]{:S(2)}) async-start(f32[32,4,2,8,128]{4,3,2,1,0:T(8,128)} %shard_map.37), calls=%async_computation | async-start | bytes 2097152 | tf_op jit(solution)/shard_map/all_to_all | solution.py:448
  9.5 0.7 shard_map.38
  10.2 16.8 %all-to-all-done.src = f32[32,4,2,8,128]{4,3,2,1,0:T(8,128)S(1)} async-done(((f32[32,4,2,8,128]{4,3,2,1,0:T(8,128)}), f32[32,4,2,8,128]{4,3,2,1,0:T(8,128)S(1)}, u32[]{:S(2)}, u32[]{:S(2)}) %all-to-all-start) | async-done | bytes 1048608 | tf_op jit(solution)/shard_map/all_to_all | solution.py:448
  27.6 2.1 %collective-permute-start.1 = (f32[16,64,128]{2,1,0:T(8,128)S(1)}, f32[16,64,128]{2,1,0:T(8,128)S(1)}, u32[]{:S(2)}, u32[]{:S(2)}) collective-permute-start(f32[16,64,128]{2,1,0:T(8,128)S(1)} %get-tuple-element.28), channel_id=1, source_target_pairs={{16,2},{144,130},{17,3},{145,131},{177,163},{49,35},{176,162},{48,... | collective-permute-start | bytes 1572872 | tf_op jit(solution)/shard_map/ppermute | solution.py:451
  30.0 0.7 collective-permute-start.3
  30.6 0.9 %shard_map.40.part = f32[16,2,64,128]{3,2,1,0:T(8,128)S(1)} custom-call(f32[22,8,128]{2,1,0:T(8,128)S(1)} %get-tuple-element.24.coef, f32[16,6,8,128]{3,2,1,0:T(8,128)S(1)} %get-tuple-element.25.table, f32[16,2,64,128]{3,2,1,0:T(8,128)S(1)} %get-tuple-element.27.x0.x, f32[16,2,64,128]{3,2,1,0:T(8,128)S(1)} %get-tuple-element.27.x0.x, ...), custom_call_target="tpu_custom_call" | custom-call | bytes 7380000 | tf_op jit(solution)/shard_map/pallas_call | solution.py:455
  31.5 3.3 %collective-permute-done.2.row_a = f32[16,2,8,128]{3,2,1,0:T(8,128)S(1)} collective-permute-done((f32[16,2,8,128]{3,2,1,0:T(8,128)S(1)}, f32[16,2,8,128]{3,2,1,0:T(8,128)S(1)}, u32[]{:S(2)}, u32[]{:S(2)}) %collective-permute-start.2) | collective-permute-done | bytes 131104 | tf_op jit(solution)/shard_map/ppermute | solution.py:453
  34.8 3.3 %collective-permute-done.1.outer = f32[16,64,128]{2,1,0:T(8,128)S(1)} collective-permute-done((f32[16,64,128]{2,1,0:T(8,128)S(1)}, f32[16,64,128]{2,1,0:T(8,128)S(1)}, u32[]{:S(2)}, u32[]{:S(2)}) %collective-permute-start.1) | collective-permute-done | bytes 524320 | tf_op jit(solution)/shard_map/ppermute | solution.py:451
  38.6 1.8 %collective-permute-start.4 = (f32[16,2,64,128]{3,2,1,0:T(8,128)S(1)}, f32[16,2,64,128]{3,2,1,0:T(8,128)S(1)}, u32[]{:S(2)}, u32[]{:S(2)}) collective-permute-start(f32[16,2,64,128]{3,2,1,0:T(8,128)S(1)} %get-tuple-element.31.x), channel_id=1, source_target_pairs={{0,16},{128,144},{1,17},{129,145},{161,177},{33,49},{160,176},{32,... | collective-permute-start | bytes 3145736 | tf_op jit(solution)/shard_map/ppermute | solution.py:452
  40.4 1.9 %collective-permute-start.5 = (f32[16,64,128]{2,1,0:T(8,128)S(1)}, f32[16,64,128]{2,1,0:T(8,128)S(1)}, u32[]{:S(2)}, u32[]{:S(2)}) collective-permute-start(f32[16,64,128]{2,1,0:T(8,128)S(1)} %get-tuple-element.32), channel_id=1, source_target_pairs={{16,2},{144,130},{17,3},{145,131},{177,163},{49,35},{176,162},{48,... | collective-permute-start | bytes 1572872 | tf_op jit(solution)/shard_map/ppermute | solution.py:451
  42.9 0.7 collective-permute-start.7
  43.5 0.9 %shard_map.42.part = f32[16,2,64,128]{3,2,1,0:T(8,128)S(1)} custom-call(f32[22,8,128]{2,1,0:T(8,128)S(1)} %get-tuple-element.24.coef, f32[16,6,8,128]{3,2,1,0:T(8,128)S(1)} %get-tuple-element.25.table, f32[16,2,64,128]{3,2,1,0:T(8,128)S(1)} %get-tuple-element.27.x0.x, f32[16,2,64,128]{3,2,1,0:T(8,128)S(1)} %get-tuple-element.31.x, ...), custom_call_target="tpu_custom_call" | custom-call | bytes 7380000 | tf_op jit(solution)/shard_map/pallas_call | solution.py:455
  44.4 2.9 %collective-permute-done.6.row_a = f32[16,2,8,128]{3,2,1,0:T(8,128)S(1)} collective-permute-done((f32[16,2,8,128]{3,2,1,0:T(8,128)S(1)}, f32[16,2,8,128]{3,2,1,0:T(8,128)S(1)}, u32[]{:S(2)}, u32[]{:S(2)}) %collective-permute-start.6) | collective-permute-done | bytes 131104 | tf_op jit(solution)/shard_map/ppermute | solution.py:453
  47.3 3.5 %collective-permute-done.5.outer = f32[16,64,128]{2,1,0:T(8,128)S(1)} collective-permute-done((f32[16,64,128]{2,1,0:T(8,128)S(1)}, f32[16,64,128]{2,1,0:T(8,128)S(1)}, u32[]{:S(2)}, u32[]{:S(2)}) %collective-permute-start.5) | collective-permute-done | bytes 524320 | tf_op jit(solution)/shard_map/ppermute | solution.py:451
  51.3 1.3 %collective-permute-start.8 = (f32[16,2,64,128]{3,2,1,0:T(8,128)S(1)}, f32[16,2,64,128]{3,2,1,0:T(8,128)S(1)}, u32[]{:S(2)}, u32[]{:S(2)}) collective-permute-start(f32[16,2,64,128]{3,2,1,0:T(8,128)S(1)} %get-tuple-element.35.x), channel_id=1, source_target_pairs={{0,16},{128,144},{1,17},{129,145},{161,177},{33,49},{160,176},{32,... | collective-permute-start | bytes 3145736 | tf_op jit(solution)/shard_map/ppermute | solution.py:452
  52.6 1.9 %collective-permute-start.9 = (f32[16,64,128]{2,1,0:T(8,128)S(1)}, f32[16,64,128]{2,1,0:T(8,128)S(1)}, u32[]{:S(2)}, u32[]{:S(2)}) collective-permute-start(f32[16,64,128]{2,1,0:T(8,128)S(1)} %get-tuple-element.36), channel_id=1, source_target_pairs={{16,2},{144,130},{17,3},{145,131},{177,163},{49,35},{176,162},{48,... | collective-permute-start | bytes 1572872 | tf_op jit(solution)/shard_map/ppermute | solution.py:451
  55.1 0.7 collective-permute-start.11
  55.8 0.9 %shard_map.44.part = f32[16,2,64,128]{3,2,1,0:T(8,128)S(1)} custom-call(f32[22,8,128]{2,1,0:T(8,128)S(1)} %get-tuple-element.24.coef, f32[16,6,8,128]{3,2,1,0:T(8,128)S(1)} %get-tuple-element.25.table, f32[16,2,64,128]{3,2,1,0:T(8,128)S(1)} %get-tuple-element.27.x0.x, f32[16,2,64,128]{3,2,1,0:T(8,128)S(1)} %get-tuple-element.35.x, ...), custom_call_target="tpu_custom_call" | custom-call | bytes 7380000 | tf_op jit(solution)/shard_map/pallas_call | solution.py:455
  56.7 2.9 %collective-permute-done.10.row_a = f32[16,2,8,128]{3,2,1,0:T(8,128)S(1)} collective-permute-done((f32[16,2,8,128]{3,2,1,0:T(8,128)S(1)}, f32[16,2,8,128]{3,2,1,0:T(8,128)S(1)}, u32[]{:S(2)}, u32[]{:S(2)}) %collective-permute-start.10) | collective-permute-done | bytes 131104 | tf_op jit(solution)/shard_map/ppermute | solution.py:453
  59.6 3.5 %collective-permute-done.9.outer = f32[16,64,128]{2,1,0:T(8,128)S(1)} collective-permute-done((f32[16,64,128]{2,1,0:T(8,128)S(1)}, f32[16,64,128]{2,1,0:T(8,128)S(1)}, u32[]{:S(2)}, u32[]{:S(2)}) %collective-permute-start.9) | collective-permute-done | bytes 524320 | tf_op jit(solution)/shard_map/ppermute | solution.py:451
  63.1 0.7 shard_map.45
  63.8 21.6 %all_to_all.10.src = f32[32,4,2,8,128]{4,3,2,1,0:T(8,128)S(1)} all-to-all(f32[32,4,2,8,128]{4,3,2,1,0:T(8,128)S(1)} %shard_map.45), channel_id=1, replica_groups=mesh['xl'=2,'y'=4,'c'=2,'z'=8,'xh'=2] {'xl','y','c','xh'}, dimensions={0} | all-to-all | bytes 2097152 | tf_op jit(solution)/shard_map/all_to_all | solution.py:448
  85.4 1.0 %shard_map.46 = f32[4,2,2,128,128]{4,3,2,1,0:T(8,128)} custom-call(f32[32,4,2,8,128]{4,3,2,1,0:T(8,128)S(1)} %all_to_all.10.src), custom_call_target="tpu_custom_call" | custom-call | tf_op jit(solution)/shard_map/pallas_call | solution.py:486
  (17 shorter events, 2.9 us)
Async XLA Ops:
  2.0 7.5 %copy-start = (s32[128,128]{1,0:T(8,128)S(1)}, s32[128,128]{1,0:T(8,128)}, u32[]{:S(2)}) copy-start(s32[128,128]{1,0:T(8,128)} %regions.1) | copy-start | bytes 196612
  2.0 7.5 %copy-start.1 = (f32[3,4]{1,0:T(4,128)S(1)}, f32[3,4]{1,0:T(4,128)}, u32[]{:S(2)}) copy-start(f32[3,4]{1,0:T(4,128)} %material.1) | copy-start | bytes 148
  2.0 25.0 %all-to-all-start = ((f32[32,4,2,8,128]{4,3,2,1,0:T(8,128)}), f32[32,4,2,8,128]{4,3,2,1,0:T(8,128)S(1)}, u32[]{:S(2)}, u32[]{:S(2)}) async-start(f32[32,4,2,8,128]{4,3,2,1,0:T(8,128)} %shard_map.37), calls=%async_computation | async-start | bytes 2097152 | tf_op jit(solution)/shard_map/all_to_all | solution.py:448
  27.5 3.1 %collective-permute-start = (f32[16,2,64,128]{3,2,1,0:T(8,128)S(1)}, f32[16,2,64,128]{3,2,1,0:T(8,128)S(1)}, u32[]{:S(2)}, u32[]{:S(2)}) collective-permute-start(f32[16,2,64,128]{3,2,1,0:T(8,128)S(1)} %get-tuple-element.27.x0.x), channel_id=1, source_target_pairs={{0,16},{128,144},{1,17},{129,145},{161,177},{33,49},{160,176},{32,... | collective-permute-start | bytes 3145736 | tf_op jit(solution)/shard_map/ppermute | solution.py:452
  27.6 10.5 %collective-permute-start.1 = (f32[16,64,128]{2,1,0:T(8,128)S(1)}, f32[16,64,128]{2,1,0:T(8,128)S(1)}, u32[]{:S(2)}, u32[]{:S(2)}) collective-permute-start(f32[16,64,128]{2,1,0:T(8,128)S(1)} %get-tuple-element.28), channel_id=1, source_target_pairs={{16,2},{144,130},{17,3},{145,131},{177,163},{49,35},{176,162},{48,... | collective-permute-start | bytes 1572872 | tf_op jit(solution)/shard_map/ppermute | solution.py:451
  29.7 5.1 %collective-permute-start.2 = (f32[16,2,8,128]{3,2,1,0:T(8,128)S(1)}, f32[16,2,8,128]{3,2,1,0:T(8,128)S(1)}, u32[]{:S(2)}, u32[]{:S(2)}) collective-permute-start(f32[16,2,8,128]{3,2,1,0:T(8,128)S(1)} %get-tuple-element.29), channel_id=1, source_target_pairs={{0,128},{16,144},{1,129},{17,145},{161,33},{177,49},{160,32},{176,... | collective-permute-start | bytes 393224 | tf_op jit(solution)/shard_map/ppermute | solution.py:453
  30.0 4.8 %collective-permute-start.3 = (f32[16,2,8,128]{3,2,1,0:T(8,128)S(1)}, f32[16,2,8,128]{3,2,1,0:T(8,128)S(1)}, u32[]{:S(2)}, u32[]{:S(2)}) collective-permute-start(f32[16,2,8,128]{3,2,1,0:T(8,128)S(1)} %get-tuple-element.30), channel_id=1, source_target_pairs={{128,1},{144,17},{129,161},{145,177},{33,160},{49,176},{32,64},{48... | collective-permute-start | bytes 393224 | tf_op jit(solution)/shard_map/ppermute | solution.py:454
  38.6 5.0 %collective-permute-start.4 = (f32[16,2,64,128]{3,2,1,0:T(8,128)S(1)}, f32[16,2,64,128]{3,2,1,0:T(8,128)S(1)}, u32[]{:S(2)}, u32[]{:S(2)}) collective-permute-start(f32[16,2,64,128]{3,2,1,0:T(8,128)S(1)} %get-tuple-element.31.x), channel_id=1, source_target_pairs={{0,16},{128,144},{1,17},{129,145},{161,177},{33,49},{160,176},{32,... | collective-permute-start | bytes 3145736 | tf_op jit(solution)/shard_map/ppermute | solution.py:452
  40.4 10.5 %collective-permute-start.5 = (f32[16,64,128]{2,1,0:T(8,128)S(1)}, f32[16,64,128]{2,1,0:T(8,128)S(1)}, u32[]{:S(2)}, u32[]{:S(2)}) collective-permute-start(f32[16,64,128]{2,1,0:T(8,128)S(1)} %get-tuple-element.32), channel_id=1, source_target_pairs={{16,2},{144,130},{17,3},{145,131},{177,163},{49,35},{176,162},{48,... | collective-permute-start | bytes 1572872 | tf_op jit(solution)/shard_map/ppermute | solution.py:451
  42.3 5.1 %collective-permute-start.6 = (f32[16,2,8,128]{3,2,1,0:T(8,128)S(1)}, f32[16,2,8,128]{3,2,1,0:T(8,128)S(1)}, u32[]{:S(2)}, u32[]{:S(2)}) collective-permute-start(f32[16,2,8,128]{3,2,1,0:T(8,128)S(1)} %get-tuple-element.33), channel_id=1, source_target_pairs={{0,128},{16,144},{1,129},{17,145},{161,33},{177,49},{160,32},{176,... | collective-permute-start | bytes 393224 | tf_op jit(solution)/shard_map/ppermute | solution.py:453
  42.9 4.5 %collective-permute-start.7 = (f32[16,2,8,128]{3,2,1,0:T(8,128)S(1)}, f32[16,2,8,128]{3,2,1,0:T(8,128)S(1)}, u32[]{:S(2)}, u32[]{:S(2)}) collective-permute-start(f32[16,2,8,128]{3,2,1,0:T(8,128)S(1)} %get-tuple-element.34), channel_id=1, source_target_pairs={{128,1},{144,17},{129,161},{145,177},{33,160},{49,176},{32,64},{48... | collective-permute-start | bytes 393224 | tf_op jit(solution)/shard_map/ppermute | solution.py:454
  51.3 4.5 %collective-permute-start.8 = (f32[16,2,64,128]{3,2,1,0:T(8,128)S(1)}, f32[16,2,64,128]{3,2,1,0:T(8,128)S(1)}, u32[]{:S(2)}, u32[]{:S(2)}) collective-permute-start(f32[16,2,64,128]{3,2,1,0:T(8,128)S(1)} %get-tuple-element.35.x), channel_id=1, source_target_pairs={{0,16},{128,144},{1,17},{129,145},{161,177},{33,49},{160,176},{32,... | collective-permute-start | bytes 3145736 | tf_op jit(solution)/shard_map/ppermute | solution.py:452
  52.6 10.5 %collective-permute-start.9 = (f32[16,64,128]{2,1,0:T(8,128)S(1)}, f32[16,64,128]{2,1,0:T(8,128)S(1)}, u32[]{:S(2)}, u32[]{:S(2)}) collective-permute-start(f32[16,64,128]{2,1,0:T(8,128)S(1)} %get-tuple-element.36), channel_id=1, source_target_pairs={{16,2},{144,130},{17,3},{145,131},{177,163},{49,35},{176,162},{48,... | collective-permute-start | bytes 1572872 | tf_op jit(solution)/shard_map/ppermute | solution.py:451
  54.5 5.1 %collective-permute-start.10 = (f32[16,2,8,128]{3,2,1,0:T(8,128)S(1)}, f32[16,2,8,128]{3,2,1,0:T(8,128)S(1)}, u32[]{:S(2)}, u32[]{:S(2)}) collective-permute-start(f32[16,2,8,128]{3,2,1,0:T(8,128)S(1)} %get-tuple-element.37), channel_id=1, source_target_pairs={{0,128},{16,144},{1,129},{17,145},{161,33},{177,49},{160,32},{176,... | collective-permute-start | bytes 393224 | tf_op jit(solution)/shard_map/ppermute | solution.py:453
  55.1 4.5 %collective-permute-start.11 = (f32[16,2,8,128]{3,2,1,0:T(8,128)S(1)}, f32[16,2,8,128]{3,2,1,0:T(8,128)S(1)}, u32[]{:S(2)}, u32[]{:S(2)}) collective-permute-start(f32[16,2,8,128]{3,2,1,0:T(8,128)S(1)} %get-tuple-element.38), channel_id=1, source_target_pairs={{128,1},{144,17},{129,161},{145,177},{33,160},{49,176},{32,64},{48... | collective-permute-start | bytes 393224 | tf_op jit(solution)/shard_map/ppermute | solution.py:454

commit v5 on v4

--- a/solution.py
+++ b/solution.py
@@ -144,21 +144,12 @@
     return [v for two in zip(a, b) for v in two]
 
 
-def split_kernel(src, out, whole, pieces, in_sems, out_sems):
-    arrivals = [pltpu.make_async_copy(src.at[f], whole.at[f], in_sems.at[f]) for f in range(FIELDS)]
-    for copy in arrivals:
-        copy.start()
-    leaving = []
+def split_kernel(src, out):
     for f in range(FIELDS):
-        arrivals[f].wait()
         for t in range(2):
             for core in range(2):
                 for pos in range(16):
-                    pieces[level_index(pos, core), f, t] = whole[f, t, core, pl.ds(8 * pos, 8), :]
-        leaving.append(pltpu.make_async_copy(pieces.at[:, f], out.at[:, f], out_sems.at[f]))
-        leaving[-1].start()
-    for copy in leaving:
-        copy.wait()
+                    out[level_index(pos, core), f, t] = src[f, t, core, pl.ds(8 * pos, 8), :]
 
 
 def join_kernel(src, out, whole, sems):
@@ -177,7 +168,7 @@
 (A, AE, AW, AN, AS, AH, AC, GE, GW, GN, GS, GH, G, KE, KW, KN, KS, KH, KZ, DN, DS, DH) = range(22)
 
 
-def coefficient_kernel(material, regions, coef, table):
+def coefficient_kernel(material, regions, coef, table, beside_table):
     pos = row_block()
     r, l = rows(), lanes()
     there = [l < 127, l > 0, (r < 7) | (pos < 15), (r > 0) | (pos > 0)]
@@ -186,25 +177,28 @@
     after = regions[pl.ds(8 * jnp.minimum(pos + 1, 15), 8), :]
     before = regions[pl.ds(8 * jnp.maximum(pos - 1, 0), 8), :]
 
+    def value_of(row, classes):
+        value = jnp.zeros((8, 128), jnp.float32)
+        for m in range(4):
+            value = jnp.where(classes == m, material[row, m], value)
+        return value
+
+    def faces(value, after, before, there):
+        moved = [pltpu.roll(value, 127, 1), pltpu.roll(value, 1, 1), after, before]
+        return [jnp.where(t, (value + v) * 0.5, value) for t, v in zip(there, moved)]
+
     def parts(row):
-        def value_of(classes):
-            value = jnp.zeros((8, 128), jnp.float32)
-            for m in range(4):
-                value = jnp.where(classes == m, material[row, m], value)
-            return value
-
-        value = value_of(here)
-        moved = [
-            pltpu.roll(value, 127, 1),
-            pltpu.roll(value, 1, 1),
-            roll(jnp.where(r == 0, value_of(after), value), 7),
-            roll(jnp.where(r == 7, value_of(before), value), 1),
-        ]
-        return value, [jnp.where(t, (value + v) * 0.5, value) for t, v in zip(there, moved)]
-
-    shear, (se, sw, sn, ss) = parts(0)
-    _, (ke, kw, kn, ks) = parts(1)
-    axial, _ = parts(2)
+        v, va, vb = value_of(row, here), value_of(row, after), value_of(row, before)
+        own = faces(v, roll(jnp.where(r == 0, va, v), 7), roll(jnp.where(r == 7, vb, v), 1), there)
+        side = jnp.where(r == 0, roll(vb, 1), roll(va, 7))
+        north = jnp.where(r == 0, v, roll(va, 6))
+        south = jnp.where(r == 0, roll(vb, 2), v)
+        always = l >= 0
+        return v, own, side, faces(side, north, south, there[:2] + [always, always])
+
+    shear, (se, sw, sn, ss), side_shear, side_shear_faces = parts(0)
+    _, (ke, kw, kn, ks), _, side_kappa_faces = parts(1)
+    axial, _, side_axial, _ = parts(2)
     a = 0.8 / (se + sw + sn + ss + 2.0 * shear)
     in_n, in_s = [jnp.where(t, 1.0, 0.0).astype(jnp.float32) for t in (r < 7, r > 0)]
     zero = jnp.zeros((8, 128), jnp.float32)
@@ -214,6 +208,10 @@
 
     g = 0.3 * a
     half_diag = 0.5 * (ke + kw + kn + ks + 2.0 * axial)
+    total = side_shear_faces[0] + side_shear_faces[1] + side_shear_faces[2] + side_shear_faces[3]
+    side_a = 0.8 / (total + 2.0 * side_shear)
+    total = side_kappa_faces[0] + side_kappa_faces[1] + side_kappa_faces[2] + side_kappa_faces[3]
+    side_half_diag = 0.5 * (total + 2.0 * side_axial)
     tiles = [
         a, a * se * has_e, a * sw * has_w, a * sn * in_n, a * ss * in_s, beside(a * ss, a * sn), a * shear,
         g * has_e, g * has_w, g * in_n, g * in_s, beside(-g, g), g,
@@ -233,6 +231,10 @@
         inv = 0.8 / (d0 * d1 + di * di)
         for n, v in enumerate((zero + m00, zero + m11, zero + m01, inv * d1, inv * d0, inv * di)):
             table[q, n] = v
+        d0, d1 = side_half_diag + 0.5 * m00, side_half_diag + 0.5 * m11
+        inv = 0.8 / (d0 * d1 + di * di)
+        for n, v in enumerate((side_a, inv * d1, inv * d0, inv * di)):
+            beside_table[q, n] = v
 
 
 def first_iterate(f, tiles, a, diagonal):
@@ -262,57 +264,73 @@
         row_b[q, p] = jnp.where(even, before, after)
 
 
-def spectrum_kernel(coef, table, src, x0, outer, row_a, row_b, spec):
+def load(block, *place):
+    return [[block[(*place, tile(2 * f + c), slice(None))] for c in range(2)] for f in range(FIELDS)]
+
+
+def scaled(tiles, a, diagonal):
+    return [first_iterate(f, tiles[f], a, diagonal) for f in range(FIELDS)]
+
+
+def spectrum_kernel(src, x, outer, row_a, row_b):
     def body(f, _):
         for p in range(2):
             got = rfft([src[(t // 2) * 2 + p, f, t % 2] for t in range(STEPS)])
             pairs = [(got[0][0], got[16][0])] + got[1:16]
             for q in range(PAIRS):
                 for c in range(2):
-                    spec[q, p, f, c] = pairs[q][c]
+                    x[q, p, pl.ds(pl.multiple_of(16 * f, 16) + 8 * c, 8), :] = pairs[q][c]
         return 0
 
     lax.fori_loop(0, FIELDS, body, 0)
 
     def pair(q, _):
-        diagonal = table[q, 3], table[q, 4], table[q, 5]
-        for p in range(2):
-            for f in range(FIELDS):
-                got = first_iterate(f, (spec[q, p, f, 0], spec[q, p, f, 1]), coef[A], diagonal)
-                for c in range(2):
-                    x0[q, p, tile(2 * f + c), :] = got[c]
-        outer[q] = x0[q, core_index()]
-        send(q, x0, row_a, row_b)
+        outer[q] = x[q, core_index()]
+        send(q, x, row_a, row_b)
         return 0
 
     lax.fori_loop(0, PAIRS, pair, 0, unroll=UNROLL)
 
 
-def own_kernel(coef, table, x0, x, sib, part):
+def own_kernel(first, coef, table, x0, x, sib, part, start=None):
     l = lanes()
     east = jnp.where(l == 127, 0.0, 0.3).astype(jnp.float32)
     west = jnp.where(l == 0, 0.0, 0.3).astype(jnp.float32)
     core = core_index()
+    first_core = (rows() * 0 + core) == 0
     sign = 1.0 - 2.0 * core.astype(jnp.float32)
 
     def pair(q, _):
         m00, m11, m01 = table[q, 0], table[q, 1], table[q, 2]
         pa, pb, pc = table[q, 3], table[q, 4], table[q, 5]
+        beside = [load(sib, q, 0), load(sib, q, 1)]
+        if first:
+            beside = [scaled(tiles, coef[A], (pa, pb, pc)) for tiles in beside]
         for p, edge in ((core, True), (1 - core, False)):
             new = [[None, None] for _ in range(FIELDS)]
             div, flow = [None, None], [None, None]
+            here = load(x, q, p)
+            if first:
+                here = scaled(here, coef[A], (pa, pb, pc))
+                base = [[1.2 * here[f][c] for c in range(2)] for f in range(FIELDS)]
+                for f in range(FIELDS):
+                    for c in range(2):
+                        start[q, p, tile(2 * f + c), :] = here[f][c]
+            else:
+                base = load(x0, q, p)
+                base = [[base[f][c] + 0.2 * here[f][c] for c in range(2)] for f in range(FIELDS)]
             for c in range(2):
-                cur = [x[q, p, tile(2 * f + c), :] for f in range(FIELDS)]
+                cur = [here[f][c] for f in range(FIELDS)]
                 es = [pltpu.roll(v, 127, 1) for v in cur]
                 ws = [pltpu.roll(v, 1, 1) for v in cur]
                 ns = [roll(v, 7) for v in cur]
                 ss = [roll(v, 1) for v in cur]
                 if edge:
-                    total = [sib[q, core, tile(2 * f + c), :] for f in range(FIELDS)]
+                    total = [jnp.where(first_core, beside[0][f][c], beside[1][f][c]) for f in range(FIELDS)]
                     drop_u, drop_p = sign * total[2], sign * total[3]
                 else:
-                    dn = [sib[q, 0, tile(2 * f + c), :] for f in range(FIELDS)]
-                    up = [sib[q, 1, tile(2 * f + c), :] for f in range(FIELDS)]
+                    dn = [beside[0][f][c] for f in range(FIELDS)]
+                    up = [beside[1][f][c] for f in range(FIELDS)]
                     total = [u + d for u, d in zip(up, dn)]
                     drop_u, drop_p = up[2] - dn[2], up[3] - dn[3]
                 grad = [
@@ -321,10 +339,10 @@
                     coef[G] * drop_p,
                 ]
                 for f in range(3):
-                    v = (x0[q, p, tile(2 * f + c), :] + 0.2 * cur[f]) + coef[AE] * es[f] + coef[AW] * ws[f]
+                    v = base[f][c] + coef[AE] * es[f] + coef[AW] * ws[f]
                     v = v + coef[AN] * ns[f] + coef[AS] * ss[f]
                     part[q, p, tile(2 * f + c), :] = v + coef[AC] * total[f] - grad[f]
-                new[3][c] = x0[q, p, tile(6 + c), :] + 0.2 * cur[3]
+                new[3][c] = base[3][c]
                 flow[c] = (
                     coef[KE] * es[3]
                     + coef[KW] * ws[3]
@@ -342,7 +360,11 @@
     lax.fori_loop(0, PAIRS, pair, 0, unroll=UNROLL)
 
 
-def finish(q, coef, table, part, outer, row_a, row_b, edges):
+def own_first_kernel(coef, table, x, sib, part, start):
+    own_kernel(True, coef, table, None, x, sib, part, start)
+
+
+def finish(first, q, coef, table, beside_table, part, outer, row_a, row_b, edges):
     r = rows()
     core = core_index()
     sign = 2.0 * core.astype(jnp.float32) - 1.0
@@ -356,15 +378,22 @@
         edges[q % UNROLL, n, every(7), :] = jnp.where(even, a, b)
         new = [[None, None] for _ in range(FIELDS)]
         div, flow = [None, None], [None, None]
+        side = load(edges, q % UNROLL, n)
+        if first:
+            side = scaled(side, beside_table[q, 0], [beside_table[q, m] for m in (1, 2, 3)])
+        if edge:
+            away = load(outer, q)
+            if first:
+                away = scaled(away, coef[A], (pa, pb, pc))
         for c in range(2):
-            beside = [edges[q % UNROLL, n, tile(2 * f + c), :] for f in range(FIELDS)]
+            beside = [side[f][c] for f in range(FIELDS)]
             for f in range(3):
                 new[f][c] = part[q, p, tile(2 * f + c), :] + coef[AH] * beside[f]
             new[1][c] = new[1][c] - coef[GH] * beside[3]
             flow[c] = coef[KH] * beside[3]
             div[c] = coef[DH] * beside[1]
             if edge:
-                out = [outer[q, tile(2 * f + c), :] for f in range(FIELDS)]
+                out = [away[f][c] for f in range(FIELDS)]
                 for f in range(3):
                     new[f][c] = new[f][c] + coef[AC] * out[f]
                 new[2][c] = new[2][c] - (sign * coef[G]) * out[3]
@@ -382,11 +411,11 @@
     edges[...] = jnp.zeros(edges.shape, jnp.float32)
 
 
-def round_kernel(coef, table, part, outer, row_a, row_b, y, next_outer, next_a, next_b, edges):
+def round_kernel(first, coef, table, beside_table, part, outer, row_a, row_b, y, next_outer, next_a, next_b, edges):
     clear(edges)
 
     def pair(q, _):
-        for p, tiles in finish(q, coef, table, part, outer, row_a, row_b, edges):
+        for p, tiles in finish(first, q, coef, table, beside_table, part, outer, row_a, row_b, edges):
             for j in range(2 * FIELDS):
                 y[q, p, tile(j), :] = tiles[j // 2][j % 2]
         next_outer[q] = y[q, core_index()]
@@ -396,12 +425,12 @@
     lax.fori_loop(0, PAIRS, pair, 0, unroll=UNROLL)
 
 
-def last_kernel(coef, table, part, outer, row_a, row_b, out, y, edges):
+def last_kernel(coef, table, beside_table, part, outer, row_a, row_b, out, y, edges):
     clear(edges)
     scale32 = np.float32(1.0 / STEPS)
 
     def pair(q, _):
-        for p, tiles in finish(q, coef, table, part, outer, row_a, row_b, edges):
+        for p, tiles in finish(False, q, coef, table, beside_table, part, outer, row_a, row_b, edges):
             for j in range(2 * FIELDS):
                 y[q, p, j // 2, j % 2] = tiles[j // 2][j % 2] * scale32
         return 0
@@ -452,37 +481,29 @@
         sib = lax.ppermute(v, AXES, sibling_swap())
         row_a = lax.ppermute(row_a, AXES, row_swap(0))
         row_b = lax.ppermute(row_b, AXES, row_swap(1))
-        part = call(own_kernel, [block], [vmem] * 5, limit=8, micros=2)(coef, table, x0, v, sib)
-        return part, outer, row_a, row_b
+        return sib, outer, row_a, row_b
 
     whole = (FIELDS, 2, 2, 128, 128)
-    pieces = pl.pallas_call(
-        split_kernel,
-        out_shape=jax.ShapeDtypeStruct(piece, jnp.float32),
-        in_specs=[pl.BlockSpec(memory_space=pltpu.HBM)],
-        out_specs=pl.BlockSpec(memory_space=pltpu.HBM),
-        scratch_shapes=[
-            pltpu.VMEM(whole, jnp.float32),
-            pltpu.VMEM(piece, jnp.float32),
-            pltpu.SemaphoreType.DMA((FIELDS,)),
-            pltpu.SemaphoreType.DMA((FIELDS,)),
-        ],
-        compiler_params=pltpu.CompilerParams(vmem_limit_bytes=60 * MIB),
-    )(sources)
-    arrived = level(pieces)
-    coef, table = call(coefficient_kernel, [(22, 8, 128), (PAIRS, 6, 8, 128)], [smem, vmem])(material, regions)
-    arrived, coef, table = lax.optimization_barrier((arrived, coef, table))
-    x0, *out = call(spectrum_kernel, [block] + messages, [vmem] * 3, [apart], 8)(
-        coef, table, arrived
+    arrived = level(call(split_kernel, [piece], [vmem])(sources))
+    x, *out = call(spectrum_kernel, [block] + messages, [vmem], limit=8)(arrived)
+    sib, *out = exchange(x, *out)
+    x, regions, material = lax.optimization_barrier((x, regions, material))
+    factors = call(coefficient_kernel, [(22, 8, 128), (PAIRS, 6, 8, 128), (PAIRS, 4, 8, 128)], [smem, vmem])(
+        material, regions
     )
-    x = x0
-    for _ in range(2):
-        x, *out = call(round_kernel, [block] + messages, [vmem] * 6, [edges], 8)(
-            coef, table, *exchange(x, *out)
+    coef, table, _ = factors
+    part, x0 = call(own_first_kernel, [block] * 2, [vmem] * 4, limit=8, micros=2)(
+        coef, table, x, sib
+    )
+    for n in range(2):
+        x, *out = call(functools.partial(round_kernel, n == 0), [block] + messages, [vmem] * 7, [edges], 8)(
+            *factors, part, *out
         )
-    answer = call(last_kernel, [piece], [vmem] * 6, [apart, edges], 8)(
-        coef, table, *exchange(x, *out)
-    )
+        sib, *out = exchange(x, *out)
+        part = call(functools.partial(own_kernel, False), [block], [vmem] * 5, limit=8, micros=2)(
+            coef, table, x0, x, sib
+        )
+    answer = call(last_kernel, [piece], [vmem] * 7, [apart, edges], 8)(*factors, part, *out)
     return pl.pallas_call(
         join_kernel,
         out_shape=jax.ShapeDtypeStruct(whole, jnp.float32),

time: 86.8 us -> 85.9 us (0.990)
  blocking collectives: 21.6 us -> 46.2 us
  waiting for transfers between devices: 36.2 us -> 18.5 us
  starting transfers between devices: 19.9 us -> 12.5 us
  Pallas kernels: 8.51 us -> 7 us
  local copies, waits for them, and re-layouts: 0.01 us -> 1.23 us
    all_to_all x1 -> x2, blocking collectives: 21.6 us -> 46.2 us  [level(): return lax.all_to_all(v, LEVEL, 0, 0, tiled=True)]
    all_to_all x1 -> x0, waiting for transfers between devices: 16.8 us -> none  [level(): return lax.all_to_all(v, LEVEL, 0, 0, tiled=True)]
    all_to_all x1 -> x0, starting transfers between devices: 7.46 us -> none  [level(): return lax.all_to_all(v, LEVEL, 0, 0, tiled=True)]
    pallas_call x9, Pallas kernels: 7.49 us -> 5.99 us  [the longest x2 2 us: on_device(): call(functools.partial(own_kernel, False), [block], [vmem] * 5, limit=8,...]
    unnamed x4 -> x6, local copies, waits for them, and re-layouts: 0.01 us -> 1.23 us
  transfers between devices with their start and end apart: 13 -> 12, of which waited for: 7 -> 6; matrix products, arithmetic and copies ran while one was open for 0% -> 0% of each run, Pallas kernels for 4% -> 4%
where the time goes in v5:
time: 85.9 us; the launch traced here: 85.5 us
  blocking collectives  46.2 us (54%)
  waiting for transfers between devices  18.5 us (22%)
  starting transfers between devices  12.5 us (15%)
  Pallas kernels  7 us (8%)
  local copies, waits for them, and re-layouts  1.23 us (1%)
    all_to_all x2, blocking collectives, level(): return lax.all_to_all(v, LEVEL, 0, 0, tiled=True)  46.2 us
    ppermute x3, waiting for transfers between devices, exchange(): outer = lax.ppermute(outer, AXES, level_swap())  10.2 us
    ppermute x3, waiting for transfers between devices, exchange(): row_a = lax.ppermute(row_a, AXES, row_swap(0))  8.23 us
    ppermute x3, starting transfers between devices, exchange(): outer = lax.ppermute(outer, AXES, level_swap())  6.05 us
    ppermute x3, starting transfers between devices, exchange(): sib = lax.ppermute(v, AXES, sibling_swap())  3.32 us
    pallas_call x2, Pallas kernels, on_device(): call(functools.partial(own_kernel, False), [block], [vmem] * 5, limit=8,...  2 us
    ppermute x3, starting transfers between devices, exchange(): row_b = lax.ppermute(row_b, AXES, row_swap(1))  1.97 us
  transfers between devices with their start and end apart: 12, of which 6 were waited for; matrix products, arithmetic and copies ran while one was open for 0% of the time, Pallas kernels for 4%

profile of v5, /device:TPU:96, one launch (start us, length us, event | category | flops | bytes accessed | tf_op | source)
XLA Modules:
  0.0 85.5 jit_solution(4525602541829716348)
XLA Ops:
  0.0 1.2 %copy-done = f32[4,2,2,128,128]{4,3,2,1,0:T(8,128)S(1)} copy-done((f32[4,2,2,128,128]{4,3,2,1,0:T(8,128)S(1)}, f32[4,2,2,128,128]{4,3,2,1,0:T(8,128)}, u32[]{:S(2)}) %copy-start) | copy-done | bytes 1048600
  1.4 24.6 %all_to_all.10.src = f32[32,4,2,8,128]{4,3,2,1,0:T(8,128)S(1)} all-to-all(f32[32,4,2,8,128]{4,3,2,1,0:T(8,128)S(1)} %shard_map.37), channel_id=1, replica_groups=mesh['xl'=2,'y'=4,'c'=2,'z'=8,'xh'=2] {'xl','y','c','xh'}, dimensions={0} | all-to-all | bytes 2097152 | tf_op jit(solution)/shard_map/all_to_all | solution.py:477
  26.5 2.2 %collective-permute-start.1 = (f32[16,64,128]{2,1,0:T(8,128)S(1)}, f32[16,64,128]{2,1,0:T(8,128)S(1)}, u32[]{:S(2)}, u32[]{:S(2)}) collective-permute-start(f32[16,64,128]{2,1,0:T(8,128)S(1)} %get-tuple-element.34), channel_id=1, source_target_pairs={{16,2},{144,130},{17,3},{145,131},{177,163},{49,35},{176,162},{48,... | collective-permute-start | bytes 1572872 | tf_op jit(solution)/shard_map/ppermute | solution.py:480
  29.0 0.7 collective-permute-start.3
  29.6 0.7 shard_map.39
  30.4 1.0 %shard_map.40 = (f32[16,2,64,128]{3,2,1,0:T(8,128)S(1)}, f32[16,2,64,128]{3,2,1,0:T(8,128)S(1)}) custom-call(f32[22,8,128]{2,1,0:T(8,128)S(1)} %get-tuple-element.28.coef, f32[16,6,8,128]{3,2,1,0:T(8,128)S(1)} %get-tuple-element.29.table, f32[16,2,64,128]{3,2,1,0:T(8,128)S(1)} %get-tuple-element.31.x, f32[16,2,64,128]{3,2,1,0:T(8,128)S(1)} %collective-permute-done.sib), custom_call_target="tpu_custom_call" | custom-call | bytes 7380000 | tf_op jit(solution)/shard_map/pallas_call | solution.py:495
  31.4 2.4 %collective-permute-done.2.row_a = f32[16,2,8,128]{3,2,1,0:T(8,128)S(1)} collective-permute-done((f32[16,2,8,128]{3,2,1,0:T(8,128)S(1)}, f32[16,2,8,128]{3,2,1,0:T(8,128)S(1)}, u32[]{:S(2)}, u32[]{:S(2)}) %collective-permute-start.2) | collective-permute-done | bytes 131104 | tf_op jit(solution)/shard_map/ppermute | solution.py:482
  33.8 3.2 %collective-permute-done.1.outer = f32[16,64,128]{2,1,0:T(8,128)S(1)} collective-permute-done((f32[16,64,128]{2,1,0:T(8,128)S(1)}, f32[16,64,128]{2,1,0:T(8,128)S(1)}, u32[]{:S(2)}, u32[]{:S(2)}) %collective-permute-start.1) | collective-permute-done | bytes 524320 | tf_op jit(solution)/shard_map/ppermute | solution.py:480
  37.0 0.5 shard_map.41
  37.6 1.9 %collective-permute-start.4 = (f32[16,2,64,128]{3,2,1,0:T(8,128)S(1)}, f32[16,2,64,128]{3,2,1,0:T(8,128)S(1)}, u32[]{:S(2)}, u32[]{:S(2)}) collective-permute-start(f32[16,2,64,128]{3,2,1,0:T(8,128)S(1)} %get-tuple-element.37.x), channel_id=1, source_target_pairs={{0,16},{128,144},{1,17},{129,145},{161,177},{33,49},{160,176},{32,... | collective-permute-start | bytes 3145736 | tf_op jit(solution)/shard_map/ppermute | solution.py:481
  39.5 1.9 %collective-permute-start.5 = (f32[16,64,128]{2,1,0:T(8,128)S(1)}, f32[16,64,128]{2,1,0:T(8,128)S(1)}, u32[]{:S(2)}, u32[]{:S(2)}) collective-permute-start(f32[16,64,128]{2,1,0:T(8,128)S(1)} %get-tuple-element.38), channel_id=1, source_target_pairs={{16,2},{144,130},{17,3},{145,131},{177,163},{49,35},{176,162},{48,... | collective-permute-start | bytes 1572872 | tf_op jit(solution)/shard_map/ppermute | solution.py:480
  41.8 0.7 collective-permute-start.7
  42.5 1.0 %shard_map.42.part = f32[16,2,64,128]{3,2,1,0:T(8,128)S(1)} custom-call(f32[22,8,128]{2,1,0:T(8,128)S(1)} %get-tuple-element.28.coef, f32[16,6,8,128]{3,2,1,0:T(8,128)S(1)} %get-tuple-element.29.table, f32[16,2,64,128]{3,2,1,0:T(8,128)S(1)} %get-tuple-element.32.x0, f32[16,2,64,128]{3,2,1,0:T(8,128)S(1)} %get-tuple-element.37.x, ...), custom_call_target="tpu_custom_call" | custom-call | bytes 7380000 | tf_op jit(solution)/shard_map/pallas_call | solution.py:503
  43.5 2.9 %collective-permute-done.6.row_a = f32[16,2,8,128]{3,2,1,0:T(8,128)S(1)} collective-permute-done((f32[16,2,8,128]{3,2,1,0:T(8,128)S(1)}, f32[16,2,8,128]{3,2,1,0:T(8,128)S(1)}, u32[]{:S(2)}, u32[]{:S(2)}) %collective-permute-start.6) | collective-permute-done | bytes 131104 | tf_op jit(solution)/shard_map/ppermute | solution.py:482
  46.4 3.5 %collective-permute-done.5.outer = f32[16,64,128]{2,1,0:T(8,128)S(1)} collective-permute-done((f32[16,64,128]{2,1,0:T(8,128)S(1)}, f32[16,64,128]{2,1,0:T(8,128)S(1)}, u32[]{:S(2)}, u32[]{:S(2)}) %collective-permute-start.5) | collective-permute-done | bytes 524320 | tf_op jit(solution)/shard_map/ppermute | solution.py:480
  50.4 1.3 %collective-permute-start.8 = (f32[16,2,64,128]{3,2,1,0:T(8,128)S(1)}, f32[16,2,64,128]{3,2,1,0:T(8,128)S(1)}, u32[]{:S(2)}, u32[]{:S(2)}) collective-permute-start(f32[16,2,64,128]{3,2,1,0:T(8,128)S(1)} %get-tuple-element.41.x), channel_id=1, source_target_pairs={{0,16},{128,144},{1,17},{129,145},{161,177},{33,49},{160,176},{32,... | collective-permute-start | bytes 3145736 | tf_op jit(solution)/shard_map/ppermute | solution.py:481
  51.7 1.9 %collective-permute-start.9 = (f32[16,64,128]{2,1,0:T(8,128)S(1)}, f32[16,64,128]{2,1,0:T(8,128)S(1)}, u32[]{:S(2)}, u32[]{:S(2)}) collective-permute-start(f32[16,64,128]{2,1,0:T(8,128)S(1)} %get-tuple-element.42), channel_id=1, source_target_pairs={{16,2},{144,130},{17,3},{145,131},{177,163},{49,35},{176,162},{48,... | collective-permute-start | bytes 1572872 | tf_op jit(solution)/shard_map/ppermute | solution.py:480
  54.1 0.7 collective-permute-start.11
  54.8 1.0 %shard_map.44.part = f32[16,2,64,128]{3,2,1,0:T(8,128)S(1)} custom-call(f32[22,8,128]{2,1,0:T(8,128)S(1)} %get-tuple-element.28.coef, f32[16,6,8,128]{3,2,1,0:T(8,128)S(1)} %get-tuple-element.29.table, f32[16,2,64,128]{3,2,1,0:T(8,128)S(1)} %get-tuple-element.32.x0, f32[16,2,64,128]{3,2,1,0:T(8,128)S(1)} %get-tuple-element.41.x, ...), custom_call_target="tpu_custom_call" | custom-call | bytes 7380000 | tf_op jit(solution)/shard_map/pallas_call | solution.py:503
  55.8 2.9 %collective-permute-done.10.row_a = f32[16,2,8,128]{3,2,1,0:T(8,128)S(1)} collective-permute-done((f32[16,2,8,128]{3,2,1,0:T(8,128)S(1)}, f32[16,2,8,128]{3,2,1,0:T(8,128)S(1)}, u32[]{:S(2)}, u32[]{:S(2)}) %collective-permute-start.10) | collective-permute-done | bytes 131104 | tf_op jit(solution)/shard_map/ppermute | solution.py:482
  58.7 3.5 %collective-permute-done.9.outer = f32[16,64,128]{2,1,0:T(8,128)S(1)} collective-permute-done((f32[16,64,128]{2,1,0:T(8,128)S(1)}, f32[16,64,128]{2,1,0:T(8,128)S(1)}, u32[]{:S(2)}, u32[]{:S(2)}) %collective-permute-start.9) | collective-permute-done | bytes 524320 | tf_op jit(solution)/shard_map/ppermute | solution.py:480
  62.2 0.7 shard_map.45
  63.0 21.6 %all_to_all.11.src = f32[32,4,2,8,128]{4,3,2,1,0:T(8,128)S(1)} all-to-all(f32[32,4,2,8,128]{4,3,2,1,0:T(8,128)S(1)} %shard_map.45), channel_id=1, replica_groups=mesh['xl'=2,'y'=4,'c'=2,'z'=8,'xh'=2] {'xl','y','c','xh'}, dimensions={0} | all-to-all | bytes 2097152 | tf_op jit(solution)/shard_map/all_to_all | solution.py:477
  84.5 1.0 %shard_map.46 = f32[4,2,2,128,128]{4,3,2,1,0:T(8,128)} custom-call(f32[32,4,2,8,128]{4,3,2,1,0:T(8,128)S(1)} %all_to_all.11.src), custom_call_target="tpu_custom_call" | custom-call | tf_op jit(solution)/shard_map/pallas_call | solution.py:507
  (18 shorter events, 2.3 us)
Async XLA Ops:
  0.0 1.2 %copy-start = (f32[4,2,2,128,128]{4,3,2,1,0:T(8,128)S(1)}, f32[4,2,2,128,128]{4,3,2,1,0:T(8,128)}, u32[]{:S(2)}) copy-start(f32[4,2,2,128,128]{4,3,2,1,0:T(8,128)} %src.1) | copy-start | bytes 3145732
  26.0 3.6 %copy-start.1 = (s32[128,128]{1,0:T(8,128)S(1)}, s32[128,128]{1,0:T(8,128)}, u32[]{:S(2)}) copy-start(s32[128,128]{1,0:T(8,128)} %regions) | copy-start | bytes 196612
  26.4 4.0 %collective-permute-start = (f32[16,2,64,128]{3,2,1,0:T(8,128)S(1)}, f32[16,2,64,128]{3,2,1,0:T(8,128)S(1)}, u32[]{:S(2)}, u32[]{:S(2)}) collective-permute-start(f32[16,2,64,128]{3,2,1,0:T(8,128)S(1)} %get-tuple-element.31.x), channel_id=1, source_target_pairs={{0,16},{128,144},{1,17},{129,145},{161,177},{33,49},{160,176},{32,... | collective-permute-start | bytes 3145736 | tf_op jit(solution)/shard_map/ppermute | solution.py:481
  26.5 3.1 %copy-start.2 = (f32[3,4]{1,0:T(4,128)S(1)}, f32[3,4]{1,0:T(4,128)}, u32[]{:S(2)}) copy-start(f32[3,4]{1,0:T(4,128)} %material) | copy-start | bytes 148
  26.5 10.5 %collective-permute-start.1 = (f32[16,64,128]{2,1,0:T(8,128)S(1)}, f32[16,64,128]{2,1,0:T(8,128)S(1)}, u32[]{:S(2)}, u32[]{:S(2)}) collective-permute-start(f32[16,64,128]{2,1,0:T(8,128)S(1)} %get-tuple-element.34), channel_id=1, source_target_pairs={{16,2},{144,130},{17,3},{145,131},{177,163},{49,35},{176,162},{48,... | collective-permute-start | bytes 1572872 | tf_op jit(solution)/shard_map/ppermute | solution.py:480
  28.8 5.1 %collective-permute-start.2 = (f32[16,2,8,128]{3,2,1,0:T(8,128)S(1)}, f32[16,2,8,128]{3,2,1,0:T(8,128)S(1)}, u32[]{:S(2)}, u32[]{:S(2)}) collective-permute-start(f32[16,2,8,128]{3,2,1,0:T(8,128)S(1)} %get-tuple-element.35), channel_id=1, source_target_pairs={{0,128},{16,144},{1,129},{17,145},{161,33},{177,49},{160,32},{176,... | collective-permute-start | bytes 393224 | tf_op jit(solution)/shard_map/ppermute | solution.py:482
  29.0 4.9 %collective-permute-start.3 = (f32[16,2,8,128]{3,2,1,0:T(8,128)S(1)}, f32[16,2,8,128]{3,2,1,0:T(8,128)S(1)}, u32[]{:S(2)}, u32[]{:S(2)}) collective-permute-start(f32[16,2,8,128]{3,2,1,0:T(8,128)S(1)} %get-tuple-element.36), channel_id=1, source_target_pairs={{128,1},{144,17},{129,161},{145,177},{33,160},{49,176},{32,64},{48... | collective-permute-start | bytes 393224 | tf_op jit(solution)/shard_map/ppermute | solution.py:483
  37.6 5.0 %collective-permute-start.4 = (f32[16,2,64,128]{3,2,1,0:T(8,128)S(1)}, f32[16,2,64,128]{3,2,1,0:T(8,128)S(1)}, u32[]{:S(2)}, u32[]{:S(2)}) collective-permute-start(f32[16,2,64,128]{3,2,1,0:T(8,128)S(1)} %get-tuple-element.37.x), channel_id=1, source_target_pairs={{0,16},{128,144},{1,17},{129,145},{161,177},{33,49},{160,176},{32,... | collective-permute-start | bytes 3145736 | tf_op jit(solution)/shard_map/ppermute | solution.py:481
  39.5 10.5 %collective-permute-start.5 = (f32[16,64,128]{2,1,0:T(8,128)S(1)}, f32[16,64,128]{2,1,0:T(8,128)S(1)}, u32[]{:S(2)}, u32[]{:S(2)}) collective-permute-start(f32[16,64,128]{2,1,0:T(8,128)S(1)} %get-tuple-element.38), channel_id=1, source_target_pairs={{16,2},{144,130},{17,3},{145,131},{177,163},{49,35},{176,162},{48,... | collective-permute-start | bytes 1572872 | tf_op jit(solution)/shard_map/ppermute | solution.py:480
  41.4 5.1 %collective-permute-start.6 = (f32[16,2,8,128]{3,2,1,0:T(8,128)S(1)}, f32[16,2,8,128]{3,2,1,0:T(8,128)S(1)}, u32[]{:S(2)}, u32[]{:S(2)}) collective-permute-start(f32[16,2,8,128]{3,2,1,0:T(8,128)S(1)} %get-tuple-element.39), channel_id=1, source_target_pairs={{0,128},{16,144},{1,129},{17,145},{161,33},{177,49},{160,32},{176,... | collective-permute-start | bytes 393224 | tf_op jit(solution)/shard_map/ppermute | solution.py:482
  41.8 4.6 %collective-permute-start.7 = (f32[16,2,8,128]{3,2,1,0:T(8,128)S(1)}, f32[16,2,8,128]{3,2,1,0:T(8,128)S(1)}, u32[]{:S(2)}, u32[]{:S(2)}) collective-permute-start(f32[16,2,8,128]{3,2,1,0:T(8,128)S(1)} %get-tuple-element.40), channel_id=1, source_target_pairs={{128,1},{144,17},{129,161},{145,177},{33,160},{49,176},{32,64},{48... | collective-permute-start | bytes 393224 | tf_op jit(solution)/shard_map/ppermute | solution.py:483
  50.4 4.4 %collective-permute-start.8 = (f32[16,2,64,128]{3,2,1,0:T(8,128)S(1)}, f32[16,2,64,128]{3,2,1,0:T(8,128)S(1)}, u32[]{:S(2)}, u32[]{:S(2)}) collective-permute-start(f32[16,2,64,128]{3,2,1,0:T(8,128)S(1)} %get-tuple-element.41.x), channel_id=1, source_target_pairs={{0,16},{128,144},{1,17},{129,145},{161,177},{33,49},{160,176},{32,... | collective-permute-start | bytes 3145736 | tf_op jit(solution)/shard_map/ppermute | solution.py:481
  51.7 10.5 %collective-permute-start.9 = (f32[16,64,128]{2,1,0:T(8,128)S(1)}, f32[16,64,128]{2,1,0:T(8,128)S(1)}, u32[]{:S(2)}, u32[]{:S(2)}) collective-permute-start(f32[16,64,128]{2,1,0:T(8,128)S(1)} %get-tuple-element.42), channel_id=1, source_target_pairs={{16,2},{144,130},{17,3},{145,131},{177,163},{49,35},{176,162},{48,... | collective-permute-start | bytes 1572872 | tf_op jit(solution)/shard_map/ppermute | solution.py:480
  53.7 5.1 %collective-permute-start.10 = (f32[16,2,8,128]{3,2,1,0:T(8,128)S(1)}, f32[16,2,8,128]{3,2,1,0:T(8,128)S(1)}, u32[]{:S(2)}, u32[]{:S(2)}) collective-permute-start(f32[16,2,8,128]{3,2,1,0:T(8,128)S(1)} %get-tuple-element.43), channel_id=1, source_target_pairs={{0,128},{16,144},{1,129},{17,145},{161,33},{177,49},{160,32},{176,... | collective-permute-start | bytes 393224 | tf_op jit(solution)/shard_map/ppermute | solution.py:482
  54.1 4.6 %collective-permute-start.11 = (f32[16,2,8,128]{3,2,1,0:T(8,128)S(1)}, f32[16,2,8,128]{3,2,1,0:T(8,128)S(1)}, u32[]{:S(2)}, u32[]{:S(2)}) collective-permute-start(f32[16,2,8,128]{3,2,1,0:T(8,128)S(1)} %get-tuple-element.44), channel_id=1, source_target_pairs={{128,1},{144,17},{129,161},{145,177},{33,160},{49,176},{32,64},{48... | collective-permute-start | bytes 393224 | tf_op jit(solution)/shard_map/ppermute | solution.py:483

commit v6 on v5

--- a/solution.py
+++ b/solution.py
@@ -44,12 +44,14 @@
 
 
 def level_swap():
-    return both([(device_index(z, p, 1), device_index(z + 1, p, 0)) for z in range(7) for p in range(16)])
+    return both([(device_index(z, p, 1), device_index((z + 1) % 8, p, 0)) for z in range(8) for p in range(16)])
 
 
 def row_swap(parity):
-    low = [p for p in range(15) if p % 2 == parity]
-    return both([(device_index(z, p, c), device_index(z, p + 1, c)) for z in range(8) for p in low for c in range(2)])
+    low = range(parity, 16, 2)
+    return both(
+        [(device_index(z, p, c), device_index(z, (p + 1) % 16, c)) for z in range(8) for p in low for c in range(2)]
+    )
 
 
 def core_index():
@@ -204,7 +206,7 @@
     zero = jnp.zeros((8, 128), jnp.float32)
 
     def beside(south, north):
-        return jnp.where(r == 0, south, jnp.where(r == 7, north, zero))
+        return jnp.where((r == 0) & (pos > 0), south, jnp.where((r == 7) & (pos < 15), north, zero))
 
     g = 0.3 * a
     half_diag = 0.5 * (ke + kw + kn + ks + 2.0 * axial)
@@ -368,6 +370,8 @@
     r = rows()
     core = core_index()
     sign = 2.0 * core.astype(jnp.float32) - 1.0
+    here = jnp.where(lax.axis_index("z") == 7 * core, 0.0, 1.0).astype(jnp.float32)
+    axial_u, axial_p, axial_g = here * coef[AC], here * coef[KZ], (here * sign) * coef[G]
     even = (r * 0 + row_block() % 2) == 0
     m00, m11, m01 = table[q, 0], table[q, 1], table[q, 2]
     pa, pb, pc = table[q, 3], table[q, 4], table[q, 5]
@@ -395,10 +399,10 @@
             if edge:
                 out = [away[f][c] for f in range(FIELDS)]
                 for f in range(3):
-                    new[f][c] = new[f][c] + coef[AC] * out[f]
-                new[2][c] = new[2][c] - (sign * coef[G]) * out[3]
-                flow[c] = flow[c] + coef[KZ] * out[3]
-                div[c] = div[c] + (0.3 * sign) * out[2]
+                    new[f][c] = new[f][c] + axial_u * out[f]
+                new[2][c] = new[2][c] - axial_g * out[3]
+                flow[c] = flow[c] + axial_p * out[3]
+                div[c] = div[c] + (0.3 * here * sign) * out[2]
         g0 = flow[0] - (m00 * div[0] + m01 * div[1])
         g1 = flow[1] - (m11 * div[1] - m01 * div[0])
         new[3][0] = part[q, p, tile(6), :] + pa * g0 + pc * g1

time: 85.9 us -> 83.7 us (0.974)
  the two profiles are of different devices: /device:TPU:96 before, /device:TPU:1 now
where the time goes in v6:
time: 83.7 us; the launch traced here: 83.6 us
  blocking collectives  46.2 us (55%)
  waiting for transfers between devices  19 us (23%)
  starting transfers between devices  9.99 us (12%)
  Pallas kernels  7.03 us (8%)
  local copies, waits for them, and re-layouts  1.23 us (1%)
    all_to_all x2, blocking collectives, level(): return lax.all_to_all(v, LEVEL, 0, 0, tiled=True)  46.2 us
    ppermute x3, waiting for transfers between devices, exchange(): outer = lax.ppermute(outer, AXES, level_swap())  9.08 us
    ppermute x3, starting transfers between devices, exchange(): sib = lax.ppermute(v, AXES, sibling_swap())  6.03 us
    ppermute x3, waiting for transfers between devices, exchange(): row_b = lax.ppermute(row_b, AXES, row_swap(1))  3.94 us
    ppermute x3, waiting for transfers between devices, exchange(): sib = lax.ppermute(v, AXES, sibling_swap())  3.02 us
    ppermute x3, waiting for transfers between devices, exchange(): row_a = lax.ppermute(row_a, AXES, row_swap(0))  2.96 us
    ppermute x3, starting transfers between devices, exchange(): row_b = lax.ppermute(row_b, AXES, row_swap(1))  2.32 us
    pallas_call x2, Pallas kernels, on_device(): call(functools.partial(own_kernel, False), [block], [vmem] * 5, limit=8,...  1.98 us
  transfers between devices with their start and end apart: 12, of which 11 were waited for; matrix products, arithmetic and copies ran while one was open for 0% of the time, Pallas kernels for 4%

profile of v6, /device:TPU:1, one launch (start us, length us, event | category | flops | bytes accessed | tf_op | source)
XLA Modules:
  0.0 83.6 jit_solution(17865810422779752670)
XLA Ops:
  0.0 1.2 %copy-done = f32[4,2,2,128,128]{4,3,2,1,0:T(8,128)S(1)} copy-done((f32[4,2,2,128,128]{4,3,2,1,0:T(8,128)S(1)}, f32[4,2,2,128,128]{4,3,2,1,0:T(8,128)}, u32[]{:S(2)}) %copy-start) | copy-done | bytes 1048600
  1.4 25.3 %all_to_all.10.src = f32[32,4,2,8,128]{4,3,2,1,0:T(8,128)S(1)} all-to-all(f32[32,4,2,8,128]{4,3,2,1,0:T(8,128)S(1)} %shard_map.37), channel_id=1, replica_groups=mesh['xl'=2,'y'=4,'c'=2,'z'=8,'xh'=2] {'xl','y','c','xh'}, dimensions={0} | all-to-all | bytes 2097152 | tf_op jit(solution)/shard_map/all_to_all | solution.py:481
  27.1 0.9 %collective-permute-start = (f32[16,2,64,128]{3,2,1,0:T(8,128)S(1)}, f32[16,2,64,128]{3,2,1,0:T(8,128)S(1)}, u32[]{:S(2)}, u32[]{:S(2)}) collective-permute-start(f32[16,2,64,128]{3,2,1,0:T(8,128)S(1)} %get-tuple-element.31.x), channel_id=1, source_target_pairs={{0,16},{128,144},{1,17},{129,145},{161,177},{33,49},{160,176},{32,... | collective-permute-start | bytes 3145736 | tf_op jit(solution)/shard_map/ppermute | solution.py:485
  28.0 1.6 %collective-permute-start.1 = (f32[16,64,128]{2,1,0:T(8,128)S(1)}, f32[16,64,128]{2,1,0:T(8,128)S(1)}, u32[]{:S(2)}, u32[]{:S(2)}) collective-permute-start(f32[16,64,128]{2,1,0:T(8,128)S(1)} %get-tuple-element.34), channel_id=1, source_target_pairs={{16,2},{144,130},{17,3},{145,131},{177,163},{49,35},{176,162},{48,... | collective-permute-start | bytes 1572872 | tf_op jit(solution)/shard_map/ppermute | solution.py:484
  29.6 0.8 collective-permute-start.3
  31.1 1.0 %shard_map.40 = (f32[16,2,64,128]{3,2,1,0:T(8,128)S(1)}, f32[16,2,64,128]{3,2,1,0:T(8,128)S(1)}) custom-call(f32[22,8,128]{2,1,0:T(8,128)S(1)} %get-tuple-element.28.coef, f32[16,6,8,128]{3,2,1,0:T(8,128)S(1)} %get-tuple-element.29.table, f32[16,2,64,128]{3,2,1,0:T(8,128)S(1)} %get-tuple-element.31.x, f32[16,2,64,128]{3,2,1,0:T(8,128)S(1)} %collective-permute-done.sib), custom_call_target="tpu_custom_call" | custom-call | bytes 7380000 | tf_op jit(solution)/shard_map/pallas_call | solution.py:499
  32.2 1.3 %collective-permute-done.2.row_a = f32[16,2,8,128]{3,2,1,0:T(8,128)S(1)} collective-permute-done((f32[16,2,8,128]{3,2,1,0:T(8,128)S(1)}, f32[16,2,8,128]{3,2,1,0:T(8,128)S(1)}, u32[]{:S(2)}, u32[]{:S(2)}) %collective-permute-start.2) | collective-permute-done | bytes 131104 | tf_op jit(solution)/shard_map/ppermute | solution.py:486
  33.5 1.5 %collective-permute-done.3.row_b = f32[16,2,8,128]{3,2,1,0:T(8,128)S(1)} collective-permute-done((f32[16,2,8,128]{3,2,1,0:T(8,128)S(1)}, f32[16,2,8,128]{3,2,1,0:T(8,128)S(1)}, u32[]{:S(2)}, u32[]{:S(2)}) %collective-permute-start.3) | collective-permute-done | bytes 131104 | tf_op jit(solution)/shard_map/ppermute | solution.py:487
  35.0 1.9 %collective-permute-done.1.outer = f32[16,64,128]{2,1,0:T(8,128)S(1)} collective-permute-done((f32[16,64,128]{2,1,0:T(8,128)S(1)}, f32[16,64,128]{2,1,0:T(8,128)S(1)}, u32[]{:S(2)}, u32[]{:S(2)}) %collective-permute-start.1) | collective-permute-done | bytes 524320 | tf_op jit(solution)/shard_map/ppermute | solution.py:484
  37.4 4.0 %collective-permute-start.4 = (f32[16,2,64,128]{3,2,1,0:T(8,128)S(1)}, f32[16,2,64,128]{3,2,1,0:T(8,128)S(1)}, u32[]{:S(2)}, u32[]{:S(2)}) collective-permute-start(f32[16,2,64,128]{3,2,1,0:T(8,128)S(1)} %get-tuple-element.37.x), channel_id=1, source_target_pairs={{0,16},{128,144},{1,17},{129,145},{161,177},{33,49},{160,176},{32,... | collective-permute-start | bytes 3145736 | tf_op jit(solution)/shard_map/ppermute | solution.py:485
  41.5 0.8 collective-permute-start.7
  42.2 1.5 %collective-permute-done.4.sib = f32[16,2,64,128]{3,2,1,0:T(8,128)S(1)} collective-permute-done((f32[16,2,64,128]{3,2,1,0:T(8,128)S(1)}, f32[16,2,64,128]{3,2,1,0:T(8,128)S(1)}, u32[]{:S(2)}, u32[]{:S(2)}) %collective-permute-start.4) | collective-permute-done | bytes 1048608 | tf_op jit(solution)/shard_map/ppermute | solution.py:485
  43.8 1.0 %shard_map.42.part = f32[16,2,64,128]{3,2,1,0:T(8,128)S(1)} custom-call(f32[22,8,128]{2,1,0:T(8,128)S(1)} %get-tuple-element.28.coef, f32[16,6,8,128]{3,2,1,0:T(8,128)S(1)} %get-tuple-element.29.table, f32[16,2,64,128]{3,2,1,0:T(8,128)S(1)} %get-tuple-element.32.x0, f32[16,2,64,128]{3,2,1,0:T(8,128)S(1)} %get-tuple-element.37.x, ...), custom_call_target="tpu_custom_call" | custom-call | bytes 7380000 | tf_op jit(solution)/shard_map/pallas_call | solution.py:507
  44.8 0.8 collective-permute-done.6.row_a
  45.6 1.2 %collective-permute-done.7.row_b = f32[16,2,8,128]{3,2,1,0:T(8,128)S(1)} collective-permute-done((f32[16,2,8,128]{3,2,1,0:T(8,128)S(1)}, f32[16,2,8,128]{3,2,1,0:T(8,128)S(1)}, u32[]{:S(2)}, u32[]{:S(2)}) %collective-permute-start.7) | collective-permute-done | bytes 131104 | tf_op jit(solution)/shard_map/ppermute | solution.py:487
  46.8 3.6 %collective-permute-done.5.outer = f32[16,64,128]{2,1,0:T(8,128)S(1)} collective-permute-done((f32[16,64,128]{2,1,0:T(8,128)S(1)}, f32[16,64,128]{2,1,0:T(8,128)S(1)}, u32[]{:S(2)}, u32[]{:S(2)}) %collective-permute-start.5) | collective-permute-done | bytes 524320 | tf_op jit(solution)/shard_map/ppermute | solution.py:484
  50.9 1.1 %collective-permute-start.8 = (f32[16,2,64,128]{3,2,1,0:T(8,128)S(1)}, f32[16,2,64,128]{3,2,1,0:T(8,128)S(1)}, u32[]{:S(2)}, u32[]{:S(2)}) collective-permute-start(f32[16,2,64,128]{3,2,1,0:T(8,128)S(1)} %get-tuple-element.41.x), channel_id=1, source_target_pairs={{0,16},{128,144},{1,17},{129,145},{161,177},{33,49},{160,176},{32,... | collective-permute-start | bytes 3145736 | tf_op jit(solution)/shard_map/ppermute | solution.py:485
  52.7 1.5 %collective-permute-done.8.sib = f32[16,2,64,128]{3,2,1,0:T(8,128)S(1)} collective-permute-done((f32[16,2,64,128]{3,2,1,0:T(8,128)S(1)}, f32[16,2,64,128]{3,2,1,0:T(8,128)S(1)}, u32[]{:S(2)}, u32[]{:S(2)}) %collective-permute-start.8) | collective-permute-done | bytes 1048608 | tf_op jit(solution)/shard_map/ppermute | solution.py:485
  54.3 1.0 %shard_map.44.part = f32[16,2,64,128]{3,2,1,0:T(8,128)S(1)} custom-call(f32[22,8,128]{2,1,0:T(8,128)S(1)} %get-tuple-element.28.coef, f32[16,6,8,128]{3,2,1,0:T(8,128)S(1)} %get-tuple-element.29.table, f32[16,2,64,128]{3,2,1,0:T(8,128)S(1)} %get-tuple-element.32.x0, f32[16,2,64,128]{3,2,1,0:T(8,128)S(1)} %get-tuple-element.41.x, ...), custom_call_target="tpu_custom_call" | custom-call | bytes 7380000 | tf_op jit(solution)/shard_map/pallas_call | solution.py:507
  55.2 0.8 collective-permute-done.10.row_a
  56.1 1.2 %collective-permute-done.11.row_b = f32[16,2,8,128]{3,2,1,0:T(8,128)S(1)} collective-permute-done((f32[16,2,8,128]{3,2,1,0:T(8,128)S(1)}, f32[16,2,8,128]{3,2,1,0:T(8,128)S(1)}, u32[]{:S(2)}, u32[]{:S(2)}) %collective-permute-start.11) | collective-permute-done | bytes 131104 | tf_op jit(solution)/shard_map/ppermute | solution.py:487
  57.3 3.6 %collective-permute-done.9.outer = f32[16,64,128]{2,1,0:T(8,128)S(1)} collective-permute-done((f32[16,64,128]{2,1,0:T(8,128)S(1)}, f32[16,64,128]{2,1,0:T(8,128)S(1)}, u32[]{:S(2)}, u32[]{:S(2)}) %collective-permute-start.9) | collective-permute-done | bytes 524320 | tf_op jit(solution)/shard_map/ppermute | solution.py:484
  61.6 20.9 %all_to_all.11.src = f32[32,4,2,8,128]{4,3,2,1,0:T(8,128)S(1)} all-to-all(f32[32,4,2,8,128]{4,3,2,1,0:T(8,128)S(1)} %shard_map.45), channel_id=1, replica_groups=mesh['xl'=2,'y'=4,'c'=2,'z'=8,'xh'=2] {'xl','y','c','xh'}, dimensions={0} | all-to-all | bytes 2097152 | tf_op jit(solution)/shard_map/all_to_all | solution.py:481
  82.6 1.0 %shard_map.46 = f32[4,2,2,128,128]{4,3,2,1,0:T(8,128)} custom-call(f32[32,4,2,8,128]{4,3,2,1,0:T(8,128)S(1)} %all_to_all.11.src), custom_call_target="tpu_custom_call" | custom-call | tf_op jit(solution)/shard_map/pallas_call | solution.py:511
  (18 shorter events, 3.8 us)
Async XLA Ops:
  0.0 1.2 %copy-start = (f32[4,2,2,128,128]{4,3,2,1,0:T(8,128)S(1)}, f32[4,2,2,128,128]{4,3,2,1,0:T(8,128)}, u32[]{:S(2)}) copy-start(f32[4,2,2,128,128]{4,3,2,1,0:T(8,128)} %src.1) | copy-start | bytes 3145732
  26.7 3.7 %copy-start.1 = (s32[128,128]{1,0:T(8,128)S(1)}, s32[128,128]{1,0:T(8,128)}, u32[]{:S(2)}) copy-start(s32[128,128]{1,0:T(8,128)} %regions) | copy-start | bytes 196612
  27.1 4.0 %collective-permute-start = (f32[16,2,64,128]{3,2,1,0:T(8,128)S(1)}, f32[16,2,64,128]{3,2,1,0:T(8,128)S(1)}, u32[]{:S(2)}, u32[]{:S(2)}) collective-permute-start(f32[16,2,64,128]{3,2,1,0:T(8,128)S(1)} %get-tuple-element.31.x), channel_id=1, source_target_pairs={{0,16},{128,144},{1,17},{129,145},{161,177},{33,49},{160,176},{32,... | collective-permute-start | bytes 3145736 | tf_op jit(solution)/shard_map/ppermute | solution.py:485
  28.0 2.4 %copy-start.2 = (f32[3,4]{1,0:T(4,128)S(1)}, f32[3,4]{1,0:T(4,128)}, u32[]{:S(2)}) copy-start(f32[3,4]{1,0:T(4,128)} %material) | copy-start | bytes 148
  28.0 8.9 %collective-permute-start.1 = (f32[16,64,128]{2,1,0:T(8,128)S(1)}, f32[16,64,128]{2,1,0:T(8,128)S(1)}, u32[]{:S(2)}, u32[]{:S(2)}) collective-permute-start(f32[16,64,128]{2,1,0:T(8,128)S(1)} %get-tuple-element.34), channel_id=1, source_target_pairs={{16,2},{144,130},{17,3},{145,131},{177,163},{49,35},{176,162},{48,... | collective-permute-start | bytes 1572872 | tf_op jit(solution)/shard_map/ppermute | solution.py:484
  29.6 3.8 %collective-permute-start.2 = (f32[16,2,8,128]{3,2,1,0:T(8,128)S(1)}, f32[16,2,8,128]{3,2,1,0:T(8,128)S(1)}, u32[]{:S(2)}, u32[]{:S(2)}) collective-permute-start(f32[16,2,8,128]{3,2,1,0:T(8,128)S(1)} %get-tuple-element.35), channel_id=1, source_target_pairs={{0,128},{16,144},{1,129},{17,145},{161,33},{177,49},{160,32},{176,... | collective-permute-start | bytes 393224 | tf_op jit(solution)/shard_map/ppermute | solution.py:486
  29.6 5.3 %collective-permute-start.3 = (f32[16,2,8,128]{3,2,1,0:T(8,128)S(1)}, f32[16,2,8,128]{3,2,1,0:T(8,128)S(1)}, u32[]{:S(2)}, u32[]{:S(2)}) collective-permute-start(f32[16,2,8,128]{3,2,1,0:T(8,128)S(1)} %get-tuple-element.36), channel_id=1, source_target_pairs={{128,1},{144,17},{129,161},{145,177},{33,160},{49,176},{32,64},{48... | collective-permute-start | bytes 393224 | tf_op jit(solution)/shard_map/ppermute | solution.py:487
  37.4 6.3 %collective-permute-start.4 = (f32[16,2,64,128]{3,2,1,0:T(8,128)S(1)}, f32[16,2,64,128]{3,2,1,0:T(8,128)S(1)}, u32[]{:S(2)}, u32[]{:S(2)}) collective-permute-start(f32[16,2,64,128]{3,2,1,0:T(8,128)S(1)} %get-tuple-element.37.x), channel_id=1, source_target_pairs={{0,16},{128,144},{1,17},{129,145},{161,177},{33,49},{160,176},{32,... | collective-permute-start | bytes 3145736 | tf_op jit(solution)/shard_map/ppermute | solution.py:485
  41.5 8.9 %collective-permute-start.5 = (f32[16,64,128]{2,1,0:T(8,128)S(1)}, f32[16,64,128]{2,1,0:T(8,128)S(1)}, u32[]{:S(2)}, u32[]{:S(2)}) collective-permute-start(f32[16,64,128]{2,1,0:T(8,128)S(1)} %get-tuple-element.38), channel_id=1, source_target_pairs={{16,2},{144,130},{17,3},{145,131},{177,163},{49,35},{176,162},{48,... | collective-permute-start | bytes 1572872 | tf_op jit(solution)/shard_map/ppermute | solution.py:484
  41.5 4.1 %collective-permute-start.6 = (f32[16,2,8,128]{3,2,1,0:T(8,128)S(1)}, f32[16,2,8,128]{3,2,1,0:T(8,128)S(1)}, u32[]{:S(2)}, u32[]{:S(2)}) collective-permute-start(f32[16,2,8,128]{3,2,1,0:T(8,128)S(1)} %get-tuple-element.39), channel_id=1, source_target_pairs={{0,128},{16,144},{1,129},{17,145},{161,33},{177,49},{160,32},{176,... | collective-permute-start | bytes 393224 | tf_op jit(solution)/shard_map/ppermute | solution.py:486
  41.5 5.3 %collective-permute-start.7 = (f32[16,2,8,128]{3,2,1,0:T(8,128)S(1)}, f32[16,2,8,128]{3,2,1,0:T(8,128)S(1)}, u32[]{:S(2)}, u32[]{:S(2)}) collective-permute-start(f32[16,2,8,128]{3,2,1,0:T(8,128)S(1)} %get-tuple-element.40), channel_id=1, source_target_pairs={{128,1},{144,17},{129,161},{145,177},{33,160},{49,176},{32,64},{48... | collective-permute-start | bytes 393224 | tf_op jit(solution)/shard_map/ppermute | solution.py:487
  50.9 3.4 %collective-permute-start.8 = (f32[16,2,64,128]{3,2,1,0:T(8,128)S(1)}, f32[16,2,64,128]{3,2,1,0:T(8,128)S(1)}, u32[]{:S(2)}, u32[]{:S(2)}) collective-permute-start(f32[16,2,64,128]{3,2,1,0:T(8,128)S(1)} %get-tuple-element.41.x), channel_id=1, source_target_pairs={{0,16},{128,144},{1,17},{129,145},{161,177},{33,49},{160,176},{32,... | collective-permute-start | bytes 3145736 | tf_op jit(solution)/shard_map/ppermute | solution.py:485
  52.0 8.9 %collective-permute-start.9 = (f32[16,64,128]{2,1,0:T(8,128)S(1)}, f32[16,64,128]{2,1,0:T(8,128)S(1)}, u32[]{:S(2)}, u32[]{:S(2)}) collective-permute-start(f32[16,64,128]{2,1,0:T(8,128)S(1)} %get-tuple-element.42), channel_id=1, source_target_pairs={{16,2},{144,130},{17,3},{145,131},{177,163},{49,35},{176,162},{48,... | collective-permute-start | bytes 1572872 | tf_op jit(solution)/shard_map/ppermute | solution.py:484
  52.0 4.1 %collective-permute-start.10 = (f32[16,2,8,128]{3,2,1,0:T(8,128)S(1)}, f32[16,2,8,128]{3,2,1,0:T(8,128)S(1)}, u32[]{:S(2)}, u32[]{:S(2)}) collective-permute-start(f32[16,2,8,128]{3,2,1,0:T(8,128)S(1)} %get-tuple-element.43), channel_id=1, source_target_pairs={{0,128},{16,144},{1,129},{17,145},{161,33},{177,49},{160,32},{176,... | collective-permute-start | bytes 393224 | tf_op jit(solution)/shard_map/ppermute | solution.py:486
  52.0 5.3 %collective-permute-start.11 = (f32[16,2,8,128]{3,2,1,0:T(8,128)S(1)}, f32[16,2,8,128]{3,2,1,0:T(8,128)S(1)}, u32[]{:S(2)}, u32[]{:S(2)}) collective-permute-start(f32[16,2,8,128]{3,2,1,0:T(8,128)S(1)} %get-tuple-element.44), channel_id=1, source_target_pairs={{128,1},{144,17},{129,161},{145,177},{33,160},{49,176},{32,64},{48... | collective-permute-start | bytes 393224 | tf_op jit(solution)/shard_map/ppermute | solution.py:487

commit v7 on v6

--- a/solution.py
+++ b/solution.py
@@ -366,88 +366,114 @@
     own_kernel(True, coef, table, None, x, sib, part, start)
 
 
-def finish(first, q, coef, table, beside_table, part, outer, row_a, row_b, edges):
-    r = rows()
+def finish(first, edge, q, coef, table, beside_table, part, row_a, row_b, sides, outer=None):
     core = core_index()
-    sign = 2.0 * core.astype(jnp.float32) - 1.0
+    p = core if edge else 1 - core
     here = jnp.where(lax.axis_index("z") == 7 * core, 0.0, 1.0).astype(jnp.float32)
-    axial_u, axial_p, axial_g = here * coef[AC], here * coef[KZ], (here * sign) * coef[G]
-    even = (r * 0 + row_block() % 2) == 0
+    sign = here * (2.0 * core.astype(jnp.float32) - 1.0)
+    even = (rows() * 0 + row_block() % 2) == 0
     m00, m11, m01 = table[q, 0], table[q, 1], table[q, 2]
     pa, pb, pc = table[q, 3], table[q, 4], table[q, 5]
-    result = []
-    for n, p, edge in ((0, core, True), (1, 1 - core, False)):
-        a, b = row_a[q, p], row_b[q, p]
-        edges[q % UNROLL, n, every(0), :] = jnp.where(even, b, a)
-        edges[q % UNROLL, n, every(7), :] = jnp.where(even, a, b)
-        new = [[None, None] for _ in range(FIELDS)]
-        div, flow = [None, None], [None, None]
-        side = load(edges, q % UNROLL, n)
+    a, b = row_a[q, p], row_b[q, p]
+    sides[q % UNROLL, every(0), :] = jnp.where(even, b, a)
+    sides[q % UNROLL, every(7), :] = jnp.where(even, a, b)
+    side = load(sides, q % UNROLL)
+    if first:
+        side = scaled(side, beside_table[q, 0], [beside_table[q, m] for m in (1, 2, 3)])
+    if edge:
+        away = load(outer, q)
         if first:
-            side = scaled(side, beside_table[q, 0], [beside_table[q, m] for m in (1, 2, 3)])
+            away = scaled(away, coef[A], (pa, pb, pc))
+    old = load(part, q, p)
+    new = [[None, None] for _ in range(FIELDS)]
+    div, flow = [None, None], [None, None]
+    for c in range(2):
+        for f in range(3):
+            new[f][c] = old[f][c] + coef[AH] * side[f][c]
+        new[1][c] = new[1][c] - coef[GH] * side[3][c]
+        flow[c] = coef[KH] * side[3][c]
+        div[c] = coef[DH] * side[1][c]
         if edge:
-            away = load(outer, q)
-            if first:
-                away = scaled(away, coef[A], (pa, pb, pc))
-        for c in range(2):
-            beside = [side[f][c] for f in range(FIELDS)]
             for f in range(3):
-                new[f][c] = part[q, p, tile(2 * f + c), :] + coef[AH] * beside[f]
-            new[1][c] = new[1][c] - coef[GH] * beside[3]
-            flow[c] = coef[KH] * beside[3]
-            div[c] = coef[DH] * beside[1]
-            if edge:
-                out = [away[f][c] for f in range(FIELDS)]
-                for f in range(3):
-                    new[f][c] = new[f][c] + axial_u * out[f]
-                new[2][c] = new[2][c] - axial_g * out[3]
-                flow[c] = flow[c] + axial_p * out[3]
-                div[c] = div[c] + (0.3 * here * sign) * out[2]
-        g0 = flow[0] - (m00 * div[0] + m01 * div[1])
-        g1 = flow[1] - (m11 * div[1] - m01 * div[0])
-        new[3][0] = part[q, p, tile(6), :] + pa * g0 + pc * g1
-        new[3][1] = part[q, p, tile(7), :] + pb * g1 - pc * g0
-        result.append((p, new))
-    return result
-
-
-def clear(edges):
-    edges[...] = jnp.zeros(edges.shape, jnp.float32)
-
-
-def round_kernel(first, coef, table, beside_table, part, outer, row_a, row_b, y, next_outer, next_a, next_b, edges):
-    clear(edges)
+                new[f][c] = new[f][c] + (here * coef[AC]) * away[f][c]
+            new[2][c] = new[2][c] - (sign * coef[G]) * away[3][c]
+            flow[c] = flow[c] + (here * coef[KZ]) * away[3][c]
+            div[c] = div[c] + (0.3 * sign) * away[2][c]
+    g0 = flow[0] - (m00 * div[0] + m01 * div[1])
+    g1 = flow[1] - (m11 * div[1] - m01 * div[0])
+    new[3][0] = old[3][0] + pa * g0 + pc * g1
+    new[3][1] = old[3][1] + pb * g1 - pc * g0
+    return new
+
+
+def clear(sides):
+    sides[...] = jnp.zeros(sides.shape, jnp.float32)
+
+
+def other_kernel(first, coef, table, beside_table, part, row_a, row_b, y, sides):
+    clear(sides)
 
     def pair(q, _):
-        for p, tiles in finish(first, q, coef, table, beside_table, part, outer, row_a, row_b, edges):
-            for j in range(2 * FIELDS):
-                y[q, p, tile(j), :] = tiles[j // 2][j % 2]
-        next_outer[q] = y[q, core_index()]
+        new = finish(first, False, q, coef, table, beside_table, part, row_a, row_b, sides)
+        for j in range(2 * FIELDS):
+            y[q, tile(j), :] = new[j // 2][j % 2]
+        return 0
+
+    lax.fori_loop(0, PAIRS, pair, 0, unroll=UNROLL)
+
+
+def edge_kernel(first, coef, table, beside_table, part, outer, row_a, row_b, other, y, next_outer, next_a, next_b, sides):
+    clear(sides)
+    core = core_index()
+
+    def pair(q, _):
+        new = finish(first, True, q, coef, table, beside_table, part, row_a, row_b, sides, outer)
+        for j in range(2 * FIELDS):
+            y[q, core, tile(j), :] = new[j // 2][j % 2]
+            next_outer[q, tile(j), :] = new[j // 2][j % 2]
+        y[q, 1 - core] = other[q]
         send(q, y, next_a, next_b)
         return 0
 
     lax.fori_loop(0, PAIRS, pair, 0, unroll=UNROLL)
 
 
-def last_kernel(coef, table, beside_table, part, outer, row_a, row_b, out, y, edges):
-    clear(edges)
+def to_steps(y, f):
     scale32 = np.float32(1.0 / STEPS)
 
+    def at(q, c):
+        return y[q, pl.ds(pl.multiple_of(16 * f, 16) + 8 * c, 8), :] * scale32
+
+    return irfft([(at(0, 0), None)] + [(at(q, 0), at(q, 1)) for q in range(1, PAIRS)] + [(at(0, 1), None)])
+
+
+def last_other_kernel(coef, table, beside_table, part, row_a, row_b, steps, y, sides):
+    other_kernel(False, coef, table, beside_table, part, row_a, row_b, y, sides)
+
+    def back(f, _):
+        for t, v in enumerate(to_steps(y, f)):
+            steps[f, t] = v
+        return 0
+
+    lax.fori_loop(0, FIELDS, back, 0)
+
+
+def last_edge_kernel(coef, table, beside_table, part, outer, row_a, row_b, other, out, y, sides):
+    clear(sides)
+    core = core_index()
+
     def pair(q, _):
-        for p, tiles in finish(False, q, coef, table, beside_table, part, outer, row_a, row_b, edges):
-            for j in range(2 * FIELDS):
-                y[q, p, j // 2, j % 2] = tiles[j // 2][j % 2] * scale32
+        new = finish(False, True, q, coef, table, beside_table, part, row_a, row_b, sides, outer)
+        for j in range(2 * FIELDS):
+            y[q, tile(j), :] = new[j // 2][j % 2]
         return 0
 
     lax.fori_loop(0, PAIRS, pair, 0, unroll=UNROLL)
 
     def back(f, _):
-        for p in range(2):
-            spec = [(y[0, p, f, 0], None)]
-            spec += [(y[q, p, f, 0], y[q, p, f, 1]) for q in range(1, PAIRS)]
-            spec += [(y[0, p, f, 1], None)]
-            for t, v in enumerate(irfft(spec)):
-                out[(t // 2) * 2 + p, f, t % 2] = v
+        for t, v in enumerate(to_steps(y, f)):
+            out[(t // 2) * 2 + core, f, t % 2] = v
+            out[(t // 2) * 2 + 1 - core, f, t % 2] = other[f, t]
         return 0
 
     lax.fori_loop(0, FIELDS, back, 0)
@@ -473,9 +499,9 @@
     vmem, smem = pltpu.VMEM, pltpu.SMEM
     piece = (32, FIELDS, 2, 8, 128)
     block = (PAIRS, 2, TALL, 128)
-    apart = (PAIRS, 2, FIELDS, 2, 8, 128)
+    plane = (PAIRS, TALL, 128)
     messages = [(PAIRS, TALL, 128), (PAIRS, 2, 8, 128), (PAIRS, 2, 8, 128)]
-    edges = (UNROLL, 2, TALL, 128)
+    sides = (UNROLL, TALL, 128)
 
     def level(v):
         return lax.all_to_all(v, LEVEL, 0, 0, tiled=True)
@@ -500,14 +526,18 @@
         coef, table, x, sib
     )
     for n in range(2):
-        x, *out = call(functools.partial(round_kernel, n == 0), [block] + messages, [vmem] * 7, [edges], 8)(
-            *factors, part, *out
+        outer, *beside = out
+        other = call(functools.partial(other_kernel, n == 0), [plane], [vmem] * 6, [sides], 8)(*factors, part, *beside)
+        x, *out = call(functools.partial(edge_kernel, n == 0), [block] + messages, [vmem] * 8, [sides], 8)(
+            *factors, part, outer, *beside, other
         )
         sib, *out = exchange(x, *out)
         part = call(functools.partial(own_kernel, False), [block], [vmem] * 5, limit=8, micros=2)(
             coef, table, x0, x, sib
         )
-    answer = call(last_kernel, [piece], [vmem] * 7, [apart, edges], 8)(*factors, part, *out)
+    outer, *beside = out
+    other = call(last_other_kernel, [(FIELDS, STEPS, 8, 128)], [vmem] * 6, [plane, sides], 8)(*factors, part, *beside)
+    answer = call(last_edge_kernel, [piece], [vmem] * 8, [plane, sides], 8)(*factors, part, outer, *beside, other)
     return pl.pallas_call(
         join_kernel,
         out_shape=jax.ShapeDtypeStruct(whole, jnp.float32),

time: 83.7 us -> 83.3 us (level)
  waiting for transfers between devices: 19 us -> 18 us
    ppermute x3, waiting for transfers between devices: 9.08 us -> 7.81 us  [exchange(): outer = lax.ppermute(outer, AXES, level_swap())]
    pallas_call x3 -> x6, Pallas kernels: 1.79 us -> 2.34 us  [the longest x2 0.81 us: on_device(): call(functools.partial(edge_kernel, n == 0), [block] + messages, [vmem] *...]
  transfers between devices with their start and end apart: 12 -> 12, of which waited for: 11 -> 11; matrix products, arithmetic and copies ran while one was open for 0% -> 0% of each run, Pallas kernels for 4% -> 6%
where the time goes in v7:
time: 83.3 us; the launch traced here: 83.1 us
  blocking collectives  46.2 us (55%)
  waiting for transfers between devices  18 us (22%)
  starting transfers between devices  9.98 us (12%)
  Pallas kernels  7.57 us (9%)
  local copies, waits for them, and re-layouts  1.23 us (1%)
    all_to_all x2, blocking collectives, level(): return lax.all_to_all(v, LEVEL, 0, 0, tiled=True)  46.2 us
    ppermute x3, waiting for transfers between devices, exchange(): outer = lax.ppermute(outer, AXES, level_swap())  7.81 us
    ppermute x3, starting transfers between devices, exchange(): sib = lax.ppermute(v, AXES, sibling_swap())  6.02 us
    ppermute x3, waiting for transfers between devices, exchange(): row_b = lax.ppermute(row_b, AXES, row_swap(1))  4.22 us
    ppermute x3, waiting for transfers between devices, exchange(): sib = lax.ppermute(v, AXES, sibling_swap())  3.02 us
    ppermute x3, waiting for transfers between devices, exchange(): row_a = lax.ppermute(row_a, AXES, row_swap(0))  2.98 us
    ppermute x3, starting transfers between devices, exchange(): row_b = lax.ppermute(row_b, AXES, row_swap(1))  2.04 us
    pallas_call x2, Pallas kernels, on_device(): call(functools.partial(own_kernel, False), [block], [vmem] * 5, limit=8,...  1.96 us
  transfers between devices with their start and end apart: 12, of which 11 were waited for; matrix products, arithmetic and copies ran while one was open for 0% of the time, Pallas kernels for 6%

profile of v7, /device:TPU:1, one launch (start us, length us, event | category | flops | bytes accessed | tf_op | source)
XLA Modules:
  0.0 83.1 jit_solution(15232392332921207069)
XLA Ops:
  0.0 1.2 %copy-done = f32[4,2,2,128,128]{4,3,2,1,0:T(8,128)S(1)} copy-done((f32[4,2,2,128,128]{4,3,2,1,0:T(8,128)S(1)}, f32[4,2,2,128,128]{4,3,2,1,0:T(8,128)}, u32[]{:S(2)}) %copy-start) | copy-done | bytes 1048600
  1.4 25.3 %all_to_all.10.src = f32[32,4,2,8,128]{4,3,2,1,0:T(8,128)S(1)} all-to-all(f32[32,4,2,8,128]{4,3,2,1,0:T(8,128)S(1)} %shard_map.37), channel_id=1, replica_groups=mesh['xl'=2,'y'=4,'c'=2,'z'=8,'xh'=2] {'xl','y','c','xh'}, dimensions={0} | all-to-all | bytes 2097152 | tf_op jit(solution)/shard_map/all_to_all | solution.py:507
  27.1 0.9 %collective-permute-start = (f32[16,2,64,128]{3,2,1,0:T(8,128)S(1)}, f32[16,2,64,128]{3,2,1,0:T(8,128)S(1)}, u32[]{:S(2)}, u32[]{:S(2)}) collective-permute-start(f32[16,2,64,128]{3,2,1,0:T(8,128)S(1)} %get-tuple-element.31.x), channel_id=1, source_target_pairs={{0,16},{128,144},{1,17},{129,145},{161,177},{33,49},{160,176},{32,... | collective-permute-start | bytes 3145736 | tf_op jit(solution)/shard_map/ppermute | solution.py:511
  28.0 1.6 %collective-permute-start.1 = (f32[16,64,128]{2,1,0:T(8,128)S(1)}, f32[16,64,128]{2,1,0:T(8,128)S(1)}, u32[]{:S(2)}, u32[]{:S(2)}) collective-permute-start(f32[16,64,128]{2,1,0:T(8,128)S(1)} %get-tuple-element.34), channel_id=1, source_target_pairs={{16,2},{144,130},{17,3},{145,131},{177,163},{49,35},{176,162},{48,... | collective-permute-start | bytes 1572872 | tf_op jit(solution)/shard_map/ppermute | solution.py:510
  29.6 0.8 collective-permute-start.3
  30.4 0.7 shard_map.39
  31.2 1.0 %shard_map.40 = (f32[16,2,64,128]{3,2,1,0:T(8,128)S(1)}, f32[16,2,64,128]{3,2,1,0:T(8,128)S(1)}) custom-call(f32[22,8,128]{2,1,0:T(8,128)S(1)} %get-tuple-element.28.coef, f32[16,6,8,128]{3,2,1,0:T(8,128)S(1)} %get-tuple-element.29.table, f32[16,2,64,128]{3,2,1,0:T(8,128)S(1)} %get-tuple-element.31.x, f32[16,2,64,128]{3,2,1,0:T(8,128)S(1)} %collective-permute-done.sib), custom_call_target="tpu_custom_call" | custom-call | bytes 7380000 | tf_op jit(solution)/shard_map/pallas_call | solution.py:525
  32.2 1.3 %collective-permute-done.2.row_a = f32[16,2,8,128]{3,2,1,0:T(8,128)S(1)} collective-permute-done((f32[16,2,8,128]{3,2,1,0:T(8,128)S(1)}, f32[16,2,8,128]{3,2,1,0:T(8,128)S(1)}, u32[]{:S(2)}, u32[]{:S(2)}) %collective-permute-start.2) | collective-permute-done | bytes 131104 | tf_op jit(solution)/shard_map/ppermute | solution.py:512
  33.5 1.5 %collective-permute-done.3.row_b = f32[16,2,8,128]{3,2,1,0:T(8,128)S(1)} collective-permute-done((f32[16,2,8,128]{3,2,1,0:T(8,128)S(1)}, f32[16,2,8,128]{3,2,1,0:T(8,128)S(1)}, u32[]{:S(2)}, u32[]{:S(2)}) %collective-permute-start.3) | collective-permute-done | bytes 131104 | tf_op jit(solution)/shard_map/ppermute | solution.py:513
  35.3 1.7 %collective-permute-done.1.outer = f32[16,64,128]{2,1,0:T(8,128)S(1)} collective-permute-done((f32[16,64,128]{2,1,0:T(8,128)S(1)}, f32[16,64,128]{2,1,0:T(8,128)S(1)}, u32[]{:S(2)}, u32[]{:S(2)}) %collective-permute-start.1) | collective-permute-done | bytes 524320 | tf_op jit(solution)/shard_map/ppermute | solution.py:510
  37.3 4.0 %collective-permute-start.4 = (f32[16,2,64,128]{3,2,1,0:T(8,128)S(1)}, f32[16,2,64,128]{3,2,1,0:T(8,128)S(1)}, u32[]{:S(2)}, u32[]{:S(2)}) collective-permute-start(f32[16,2,64,128]{3,2,1,0:T(8,128)S(1)} %get-tuple-element.37.x), channel_id=1, source_target_pairs={{0,16},{128,144},{1,17},{129,145},{161,177},{33,49},{160,176},{32,... | collective-permute-start | bytes 3145736 | tf_op jit(solution)/shard_map/ppermute | solution.py:511
  42.1 1.5 %collective-permute-done.4.sib = f32[16,2,64,128]{3,2,1,0:T(8,128)S(1)} collective-permute-done((f32[16,2,64,128]{3,2,1,0:T(8,128)S(1)}, f32[16,2,64,128]{3,2,1,0:T(8,128)S(1)}, u32[]{:S(2)}, u32[]{:S(2)}) %collective-permute-start.4) | collective-permute-done | bytes 1048608 | tf_op jit(solution)/shard_map/ppermute | solution.py:511
  43.6 1.0 %shard_map.43.part = f32[16,2,64,128]{3,2,1,0:T(8,128)S(1)} custom-call(f32[22,8,128]{2,1,0:T(8,128)S(1)} %get-tuple-element.28.coef, f32[16,6,8,128]{3,2,1,0:T(8,128)S(1)} %get-tuple-element.29.table, f32[16,2,64,128]{3,2,1,0:T(8,128)S(1)} %get-tuple-element.32.x0, f32[16,2,64,128]{3,2,1,0:T(8,128)S(1)} %get-tuple-element.37.x, ...), custom_call_target="tpu_custom_call" | custom-call | bytes 7380000 | tf_op jit(solution)/shard_map/pallas_call | solution.py:535
  44.6 0.8 %collective-permute-done.6.row_a = f32[16,2,8,128]{3,2,1,0:T(8,128)S(1)} collective-permute-done((f32[16,2,8,128]{3,2,1,0:T(8,128)S(1)}, f32[16,2,8,128]{3,2,1,0:T(8,128)S(1)}, u32[]{:S(2)}, u32[]{:S(2)}) %collective-permute-start.6) | collective-permute-done | bytes 131104 | tf_op jit(solution)/shard_map/ppermute | solution.py:512
  45.4 1.4 %collective-permute-done.7.row_b = f32[16,2,8,128]{3,2,1,0:T(8,128)S(1)} collective-permute-done((f32[16,2,8,128]{3,2,1,0:T(8,128)S(1)}, f32[16,2,8,128]{3,2,1,0:T(8,128)S(1)}, u32[]{:S(2)}, u32[]{:S(2)}) %collective-permute-start.7) | collective-permute-done | bytes 131104 | tf_op jit(solution)/shard_map/ppermute | solution.py:513
  47.1 3.2 %collective-permute-done.5.outer = f32[16,64,128]{2,1,0:T(8,128)S(1)} collective-permute-done((f32[16,64,128]{2,1,0:T(8,128)S(1)}, f32[16,64,128]{2,1,0:T(8,128)S(1)}, u32[]{:S(2)}, u32[]{:S(2)}) %collective-permute-start.5) | collective-permute-done | bytes 524320 | tf_op jit(solution)/shard_map/ppermute | solution.py:510
  50.6 1.1 %collective-permute-start.8 = (f32[16,2,64,128]{3,2,1,0:T(8,128)S(1)}, f32[16,2,64,128]{3,2,1,0:T(8,128)S(1)}, u32[]{:S(2)}, u32[]{:S(2)}) collective-permute-start(f32[16,2,64,128]{3,2,1,0:T(8,128)S(1)} %get-tuple-element.41.x), channel_id=1, source_target_pairs={{0,16},{128,144},{1,17},{129,145},{161,177},{33,49},{160,176},{32,... | collective-permute-start | bytes 3145736 | tf_op jit(solution)/shard_map/ppermute | solution.py:511
  52.5 1.5 %collective-permute-done.8.sib = f32[16,2,64,128]{3,2,1,0:T(8,128)S(1)} collective-permute-done((f32[16,2,64,128]{3,2,1,0:T(8,128)S(1)}, f32[16,2,64,128]{3,2,1,0:T(8,128)S(1)}, u32[]{:S(2)}, u32[]{:S(2)}) %collective-permute-start.8) | collective-permute-done | bytes 1048608 | tf_op jit(solution)/shard_map/ppermute | solution.py:511
  54.0 1.0 %shard_map.46.part = f32[16,2,64,128]{3,2,1,0:T(8,128)S(1)} custom-call(f32[22,8,128]{2,1,0:T(8,128)S(1)} %get-tuple-element.28.coef, f32[16,6,8,128]{3,2,1,0:T(8,128)S(1)} %get-tuple-element.29.table, f32[16,2,64,128]{3,2,1,0:T(8,128)S(1)} %get-tuple-element.32.x0, f32[16,2,64,128]{3,2,1,0:T(8,128)S(1)} %get-tuple-element.41.x, ...), custom_call_target="tpu_custom_call" | custom-call | bytes 7380000 | tf_op jit(solution)/shard_map/pallas_call | solution.py:535
  55.0 0.8 %collective-permute-done.10.row_a = f32[16,2,8,128]{3,2,1,0:T(8,128)S(1)} collective-permute-done((f32[16,2,8,128]{3,2,1,0:T(8,128)S(1)}, f32[16,2,8,128]{3,2,1,0:T(8,128)S(1)}, u32[]{:S(2)}, u32[]{:S(2)}) %collective-permute-start.10) | collective-permute-done | bytes 131104 | tf_op jit(solution)/shard_map/ppermute | solution.py:512
  55.9 1.3 %collective-permute-done.11.row_b = f32[16,2,8,128]{3,2,1,0:T(8,128)S(1)} collective-permute-done((f32[16,2,8,128]{3,2,1,0:T(8,128)S(1)}, f32[16,2,8,128]{3,2,1,0:T(8,128)S(1)}, u32[]{:S(2)}, u32[]{:S(2)}) %collective-permute-start.11) | collective-permute-done | bytes 131104 | tf_op jit(solution)/shard_map/ppermute | solution.py:513
  57.7 3.0 %collective-permute-done.9.outer = f32[16,64,128]{2,1,0:T(8,128)S(1)} collective-permute-done((f32[16,64,128]{2,1,0:T(8,128)S(1)}, f32[16,64,128]{2,1,0:T(8,128)S(1)}, u32[]{:S(2)}, u32[]{:S(2)}) %collective-permute-start.9) | collective-permute-done | bytes 524320 | tf_op jit(solution)/shard_map/ppermute | solution.py:510
  61.2 20.9 %all_to_all.11.src = f32[32,4,2,8,128]{4,3,2,1,0:T(8,128)S(1)} all-to-all(f32[32,4,2,8,128]{4,3,2,1,0:T(8,128)S(1)} %shard_map.48), channel_id=1, replica_groups=mesh['xl'=2,'y'=4,'c'=2,'z'=8,'xh'=2] {'xl','y','c','xh'}, dimensions={0} | all-to-all | bytes 2097152 | tf_op jit(solution)/shard_map/all_to_all | solution.py:507
  82.1 1.0 %shard_map.49 = f32[4,2,2,128,128]{4,3,2,1,0:T(8,128)} custom-call(f32[32,4,2,8,128]{4,3,2,1,0:T(8,128)S(1)} %all_to_all.11.src), custom_call_target="tpu_custom_call" | custom-call | tf_op jit(solution)/shard_map/pallas_call | solution.py:541
  (21 shorter events, 4.4 us)
Async XLA Ops:
  0.0 1.2 %copy-start = (f32[4,2,2,128,128]{4,3,2,1,0:T(8,128)S(1)}, f32[4,2,2,128,128]{4,3,2,1,0:T(8,128)}, u32[]{:S(2)}) copy-start(f32[4,2,2,128,128]{4,3,2,1,0:T(8,128)} %src.1) | copy-start | bytes 3145732
  26.7 3.7 %copy-start.1 = (s32[128,128]{1,0:T(8,128)S(1)}, s32[128,128]{1,0:T(8,128)}, u32[]{:S(2)}) copy-start(s32[128,128]{1,0:T(8,128)} %regions) | copy-start | bytes 196612
  27.1 4.0 %collective-permute-start = (f32[16,2,64,128]{3,2,1,0:T(8,128)S(1)}, f32[16,2,64,128]{3,2,1,0:T(8,128)S(1)}, u32[]{:S(2)}, u32[]{:S(2)}) collective-permute-start(f32[16,2,64,128]{3,2,1,0:T(8,128)S(1)} %get-tuple-element.31.x), channel_id=1, source_target_pairs={{0,16},{128,144},{1,17},{129,145},{161,177},{33,49},{160,176},{32,... | collective-permute-start | bytes 3145736 | tf_op jit(solution)/shard_map/ppermute | solution.py:511
  28.0 2.4 %copy-start.2 = (f32[3,4]{1,0:T(4,128)S(1)}, f32[3,4]{1,0:T(4,128)}, u32[]{:S(2)}) copy-start(f32[3,4]{1,0:T(4,128)} %material) | copy-start | bytes 148
  28.0 8.9 %collective-permute-start.1 = (f32[16,64,128]{2,1,0:T(8,128)S(1)}, f32[16,64,128]{2,1,0:T(8,128)S(1)}, u32[]{:S(2)}, u32[]{:S(2)}) collective-permute-start(f32[16,64,128]{2,1,0:T(8,128)S(1)} %get-tuple-element.34), channel_id=1, source_target_pairs={{16,2},{144,130},{17,3},{145,131},{177,163},{49,35},{176,162},{48,... | collective-permute-start | bytes 1572872 | tf_op jit(solution)/shard_map/ppermute | solution.py:510
  29.6 3.8 %collective-permute-start.2 = (f32[16,2,8,128]{3,2,1,0:T(8,128)S(1)}, f32[16,2,8,128]{3,2,1,0:T(8,128)S(1)}, u32[]{:S(2)}, u32[]{:S(2)}) collective-permute-start(f32[16,2,8,128]{3,2,1,0:T(8,128)S(1)} %get-tuple-element.35), channel_id=1, source_target_pairs={{0,128},{16,144},{1,129},{17,145},{161,33},{177,49},{160,32},{176,... | collective-permute-start | bytes 393224 | tf_op jit(solution)/shard_map/ppermute | solution.py:512
  29.6 5.3 %collective-permute-start.3 = (f32[16,2,8,128]{3,2,1,0:T(8,128)S(1)}, f32[16,2,8,128]{3,2,1,0:T(8,128)S(1)}, u32[]{:S(2)}, u32[]{:S(2)}) collective-permute-start(f32[16,2,8,128]{3,2,1,0:T(8,128)S(1)} %get-tuple-element.36), channel_id=1, source_target_pairs={{128,1},{144,17},{129,161},{145,177},{33,160},{49,176},{32,64},{48... | collective-permute-start | bytes 393224 | tf_op jit(solution)/shard_map/ppermute | solution.py:513
  37.3 6.3 %collective-permute-start.4 = (f32[16,2,64,128]{3,2,1,0:T(8,128)S(1)}, f32[16,2,64,128]{3,2,1,0:T(8,128)S(1)}, u32[]{:S(2)}, u32[]{:S(2)}) collective-permute-start(f32[16,2,64,128]{3,2,1,0:T(8,128)S(1)} %get-tuple-element.37.x), channel_id=1, source_target_pairs={{0,16},{128,144},{1,17},{129,145},{161,177},{33,49},{160,176},{32,... | collective-permute-start | bytes 3145736 | tf_op jit(solution)/shard_map/ppermute | solution.py:511
  41.3 8.9 %collective-permute-start.5 = (f32[16,64,128]{2,1,0:T(8,128)S(1)}, f32[16,64,128]{2,1,0:T(8,128)S(1)}, u32[]{:S(2)}, u32[]{:S(2)}) collective-permute-start(f32[16,64,128]{2,1,0:T(8,128)S(1)} %get-tuple-element.38), channel_id=1, source_target_pairs={{16,2},{144,130},{17,3},{145,131},{177,163},{49,35},{176,162},{48,... | collective-permute-start | bytes 1572872 | tf_op jit(solution)/shard_map/ppermute | solution.py:510
  41.3 4.1 %collective-permute-start.6 = (f32[16,2,8,128]{3,2,1,0:T(8,128)S(1)}, f32[16,2,8,128]{3,2,1,0:T(8,128)S(1)}, u32[]{:S(2)}, u32[]{:S(2)}) collective-permute-start(f32[16,2,8,128]{3,2,1,0:T(8,128)S(1)} %get-tuple-element.39), channel_id=1, source_target_pairs={{0,128},{16,144},{1,129},{17,145},{161,33},{177,49},{160,32},{176,... | collective-permute-start | bytes 393224 | tf_op jit(solution)/shard_map/ppermute | solution.py:512
  41.5 5.3 %collective-permute-start.7 = (f32[16,2,8,128]{3,2,1,0:T(8,128)S(1)}, f32[16,2,8,128]{3,2,1,0:T(8,128)S(1)}, u32[]{:S(2)}, u32[]{:S(2)}) collective-permute-start(f32[16,2,8,128]{3,2,1,0:T(8,128)S(1)} %get-tuple-element.40), channel_id=1, source_target_pairs={{128,1},{144,17},{129,161},{145,177},{33,160},{49,176},{32,64},{48... | collective-permute-start | bytes 393224 | tf_op jit(solution)/shard_map/ppermute | solution.py:513
  50.6 3.4 %collective-permute-start.8 = (f32[16,2,64,128]{3,2,1,0:T(8,128)S(1)}, f32[16,2,64,128]{3,2,1,0:T(8,128)S(1)}, u32[]{:S(2)}, u32[]{:S(2)}) collective-permute-start(f32[16,2,64,128]{3,2,1,0:T(8,128)S(1)} %get-tuple-element.41.x), channel_id=1, source_target_pairs={{0,16},{128,144},{1,17},{129,145},{161,177},{33,49},{160,176},{32,... | collective-permute-start | bytes 3145736 | tf_op jit(solution)/shard_map/ppermute | solution.py:511
  51.7 8.9 %collective-permute-start.9 = (f32[16,64,128]{2,1,0:T(8,128)S(1)}, f32[16,64,128]{2,1,0:T(8,128)S(1)}, u32[]{:S(2)}, u32[]{:S(2)}) collective-permute-start(f32[16,64,128]{2,1,0:T(8,128)S(1)} %get-tuple-element.42), channel_id=1, source_target_pairs={{16,2},{144,130},{17,3},{145,131},{177,163},{49,35},{176,162},{48,... | collective-permute-start | bytes 1572872 | tf_op jit(solution)/shard_map/ppermute | solution.py:510
  51.8 4.1 %collective-permute-start.10 = (f32[16,2,8,128]{3,2,1,0:T(8,128)S(1)}, f32[16,2,8,128]{3,2,1,0:T(8,128)S(1)}, u32[]{:S(2)}, u32[]{:S(2)}) collective-permute-start(f32[16,2,8,128]{3,2,1,0:T(8,128)S(1)} %get-tuple-element.43), channel_id=1, source_target_pairs={{0,128},{16,144},{1,129},{17,145},{161,33},{177,49},{160,32},{176,... | collective-permute-start | bytes 393224 | tf_op jit(solution)/shard_map/ppermute | solution.py:512
  51.9 5.3 %collective-permute-start.11 = (f32[16,2,8,128]{3,2,1,0:T(8,128)S(1)}, f32[16,2,8,128]{3,2,1,0:T(8,128)S(1)}, u32[]{:S(2)}, u32[]{:S(2)}) collective-permute-start(f32[16,2,8,128]{3,2,1,0:T(8,128)S(1)} %get-tuple-element.44), channel_id=1, source_target_pairs={{128,1},{144,17},{129,161},{145,177},{33,160},{49,176},{32,64},{48... | collective-permute-start | bytes 393224 | tf_op jit(solution)/shard_map/ppermute | solution.py:513

commit v8 on v7

--- a/solution.py
+++ b/solution.py
@@ -25,6 +25,10 @@
     return (3 - x if y % 2 else x), y
 
 
+def pos_of(x, y):
+    return y * 4 + (3 - x if y % 2 else x)
+
+
 def level_index(pos, core):
     x, y = chip_at(pos)
     return ((((x % 2) * 4 + y) * 2 + core) * 2) + x // 2
@@ -44,7 +48,12 @@
 
 
 def level_swap():
-    return both([(device_index(z, p, 1), device_index((z + 1) % 8, p, 0)) for z in range(8) for p in range(16)])
+    pairs = [(device_index(z, p, 1), device_index(z + 1, p, 0)) for z in range(7) for p in range(16)]
+    columns = [((x, y), (x, y + 1)) for x in range(3) for y in (0, 2)] + [((3, 1), (3, 2)), ((3, 3), (3, 0))]
+    for z, core in ((0, 0), (7, 1)):
+        for one, two in columns:
+            pairs.append((device_index(z, pos_of(*one), core), device_index(z, pos_of(*two), core)))
+    return both(pairs)
 
 
 def row_swap(parity):

time: 83.3 us -> 81.8 us (0.982)
  blocking collectives: 46.2 us -> 48.9 us
  waiting for transfers between devices: 18 us -> 15.7 us
  starting transfers between devices: 9.98 us -> 8.14 us
    ppermute x3, waiting for transfers between devices: 2.98 us -> 7.84 us  [exchange(): row_a = lax.ppermute(row_a, AXES, row_swap(0))]
    ppermute x3, waiting for transfers between devices: 7.81 us -> 3 us  [exchange(): outer = lax.ppermute(outer, AXES, level_swap())]
    ppermute x3, starting transfers between devices: 6.02 us -> 1.86 us  [exchange(): sib = lax.ppermute(v, AXES, sibling_swap())]
    all_to_all x2, blocking collectives: 46.2 us -> 48.9 us  [level(): return lax.all_to_all(v, LEVEL, 0, 0, tiled=True)]
    ppermute x3, starting transfers between devices: 1.64 us -> 3.95 us  [exchange(): outer = lax.ppermute(outer, AXES, level_swap())]
    ppermute x3, waiting for transfers between devices: 3.02 us -> 0.7 us  [exchange(): sib = lax.ppermute(v, AXES, sibling_swap())]
where the time goes in v8:
time: 81.8 us; the launch traced here: 81.6 us
  blocking collectives  48.9 us (60%)
  waiting for transfers between devices  15.7 us (19%)
  starting transfers between devices  8.14 us (10%)
  Pallas kernels  7.57 us (9%)
  local copies, waits for them, and re-layouts  1.23 us (2%)
    all_to_all x2, blocking collectives, level(): return lax.all_to_all(v, LEVEL, 0, 0, tiled=True)  48.9 us
    ppermute x3, waiting for transfers between devices, exchange(): row_a = lax.ppermute(row_a, AXES, row_swap(0))  7.84 us
    ppermute x3, waiting for transfers between devices, exchange(): row_b = lax.ppermute(row_b, AXES, row_swap(1))  4.15 us
    ppermute x3, starting transfers between devices, exchange(): outer = lax.ppermute(outer, AXES, level_swap())  3.95 us
    ppermute x3, waiting for transfers between devices, exchange(): outer = lax.ppermute(outer, AXES, level_swap())  3 us
    ppermute x3, starting transfers between devices, exchange(): row_b = lax.ppermute(row_b, AXES, row_swap(1))  2.32 us
    pallas_call x2, Pallas kernels, on_device(): call(functools.partial(own_kernel, False), [block], [vmem] * 5, limit=8,...  1.96 us
    ppermute x3, starting transfers between devices, exchange(): sib = lax.ppermute(v, AXES, sibling_swap())  1.86 us
  transfers between devices with their start and end apart: 12, of which 11 were waited for; matrix products, arithmetic and copies ran while one was open for 0% of the time, Pallas kernels for 6%

profile of v8, /device:TPU:1, one launch (start us, length us, event | category | flops | bytes accessed | tf_op | source)
XLA Modules:
  0.0 81.6 jit_solution(7077063979565187863)
XLA Ops:
  0.0 1.2 %copy-done = f32[4,2,2,128,128]{4,3,2,1,0:T(8,128)S(1)} copy-done((f32[4,2,2,128,128]{4,3,2,1,0:T(8,128)S(1)}, f32[4,2,2,128,128]{4,3,2,1,0:T(8,128)}, u32[]{:S(2)}) %copy-start) | copy-done | bytes 1048600
  1.4 25.3 %all_to_all.10.src = f32[32,4,2,8,128]{4,3,2,1,0:T(8,128)S(1)} all-to-all(f32[32,4,2,8,128]{4,3,2,1,0:T(8,128)S(1)} %shard_map.37), channel_id=1, replica_groups=mesh['xl'=2,'y'=4,'c'=2,'z'=8,'xh'=2] {'xl','y','c','xh'}, dimensions={0} | all-to-all | bytes 2097152 | tf_op jit(solution)/shard_map/all_to_all | solution.py:516
  27.1 0.9 %collective-permute-start = (f32[16,2,64,128]{3,2,1,0:T(8,128)S(1)}, f32[16,2,64,128]{3,2,1,0:T(8,128)S(1)}, u32[]{:S(2)}, u32[]{:S(2)}) collective-permute-start(f32[16,2,64,128]{3,2,1,0:T(8,128)S(1)} %get-tuple-element.31.x), channel_id=1, source_target_pairs={{0,16},{128,144},{1,17},{129,145},{161,177},{33,49},{160,176},{32,... | collective-permute-start | bytes 3145736 | tf_op jit(solution)/shard_map/ppermute | solution.py:520
  28.0 1.6 %collective-permute-start.1 = (f32[16,64,128]{2,1,0:T(8,128)S(1)}, f32[16,64,128]{2,1,0:T(8,128)S(1)}, u32[]{:S(2)}, u32[]{:S(2)}) collective-permute-start(f32[16,64,128]{2,1,0:T(8,128)S(1)} %get-tuple-element.34), channel_id=1, source_target_pairs={{16,2},{144,130},{17,3},{145,131},{177,163},{49,35},{176,162},{48,... | collective-permute-start | bytes 1572872 | tf_op jit(solution)/shard_map/ppermute | solution.py:519
  29.6 0.8 collective-permute-start.3
  30.4 0.7 shard_map.39
  31.2 1.0 %shard_map.40 = (f32[16,2,64,128]{3,2,1,0:T(8,128)S(1)}, f32[16,2,64,128]{3,2,1,0:T(8,128)S(1)}) custom-call(f32[22,8,128]{2,1,0:T(8,128)S(1)} %get-tuple-element.28.coef, f32[16,6,8,128]{3,2,1,0:T(8,128)S(1)} %get-tuple-element.29.table, f32[16,2,64,128]{3,2,1,0:T(8,128)S(1)} %get-tuple-element.31.x, f32[16,2,64,128]{3,2,1,0:T(8,128)S(1)} %collective-permute-done.sib), custom_call_target="tpu_custom_call" | custom-call | bytes 7380000 | tf_op jit(solution)/shard_map/pallas_call | solution.py:534
  32.2 2.0 %collective-permute-done.2.row_a = f32[16,2,8,128]{3,2,1,0:T(8,128)S(1)} collective-permute-done((f32[16,2,8,128]{3,2,1,0:T(8,128)S(1)}, f32[16,2,8,128]{3,2,1,0:T(8,128)S(1)}, u32[]{:S(2)}, u32[]{:S(2)}) %collective-permute-start.2) | collective-permute-done | bytes 131104 | tf_op jit(solution)/shard_map/ppermute | solution.py:521
  34.2 1.4 %collective-permute-done.3.row_b = f32[16,2,8,128]{3,2,1,0:T(8,128)S(1)} collective-permute-done((f32[16,2,8,128]{3,2,1,0:T(8,128)S(1)}, f32[16,2,8,128]{3,2,1,0:T(8,128)S(1)}, u32[]{:S(2)}, u32[]{:S(2)}) %collective-permute-start.3) | collective-permute-done | bytes 131104 | tf_op jit(solution)/shard_map/ppermute | solution.py:522
  35.8 1.1 %collective-permute-done.1.outer = f32[16,64,128]{2,1,0:T(8,128)S(1)} collective-permute-done((f32[16,64,128]{2,1,0:T(8,128)S(1)}, f32[16,64,128]{2,1,0:T(8,128)S(1)}, u32[]{:S(2)}, u32[]{:S(2)}) %collective-permute-start.1) | collective-permute-done | bytes 524320 | tf_op jit(solution)/shard_map/ppermute | solution.py:519
  37.8 1.4 %collective-permute-start.5 = (f32[16,64,128]{2,1,0:T(8,128)S(1)}, f32[16,64,128]{2,1,0:T(8,128)S(1)}, u32[]{:S(2)}, u32[]{:S(2)}) collective-permute-start(f32[16,64,128]{2,1,0:T(8,128)S(1)} %get-tuple-element.38), channel_id=1, source_target_pairs={{16,2},{144,130},{17,3},{145,131},{177,163},{49,35},{176,162},{48,... | collective-permute-start | bytes 1572872 | tf_op jit(solution)/shard_map/ppermute | solution.py:519
  39.2 0.8 collective-permute-start.7
  40.1 1.0 %shard_map.43.part = f32[16,2,64,128]{3,2,1,0:T(8,128)S(1)} custom-call(f32[22,8,128]{2,1,0:T(8,128)S(1)} %get-tuple-element.28.coef, f32[16,6,8,128]{3,2,1,0:T(8,128)S(1)} %get-tuple-element.29.table, f32[16,2,64,128]{3,2,1,0:T(8,128)S(1)} %get-tuple-element.32.x0, f32[16,2,64,128]{3,2,1,0:T(8,128)S(1)} %get-tuple-element.37.x, ...), custom_call_target="tpu_custom_call" | custom-call | bytes 7380000 | tf_op jit(solution)/shard_map/pallas_call | solution.py:544
  41.1 2.9 %collective-permute-done.6.row_a = f32[16,2,8,128]{3,2,1,0:T(8,128)S(1)} collective-permute-done((f32[16,2,8,128]{3,2,1,0:T(8,128)S(1)}, f32[16,2,8,128]{3,2,1,0:T(8,128)S(1)}, u32[]{:S(2)}, u32[]{:S(2)}) %collective-permute-start.6) | collective-permute-done | bytes 131104 | tf_op jit(solution)/shard_map/ppermute | solution.py:521
  44.0 1.4 %collective-permute-done.7.row_b = f32[16,2,8,128]{3,2,1,0:T(8,128)S(1)} collective-permute-done((f32[16,2,8,128]{3,2,1,0:T(8,128)S(1)}, f32[16,2,8,128]{3,2,1,0:T(8,128)S(1)}, u32[]{:S(2)}, u32[]{:S(2)}) %collective-permute-start.7) | collective-permute-done | bytes 131104 | tf_op jit(solution)/shard_map/ppermute | solution.py:522
  45.7 1.0 %collective-permute-done.5.outer = f32[16,64,128]{2,1,0:T(8,128)S(1)} collective-permute-done((f32[16,64,128]{2,1,0:T(8,128)S(1)}, f32[16,64,128]{2,1,0:T(8,128)S(1)}, u32[]{:S(2)}, u32[]{:S(2)}) %collective-permute-start.5) | collective-permute-done | bytes 524320 | tf_op jit(solution)/shard_map/ppermute | solution.py:519
  47.6 1.0 %collective-permute-start.9 = (f32[16,64,128]{2,1,0:T(8,128)S(1)}, f32[16,64,128]{2,1,0:T(8,128)S(1)}, u32[]{:S(2)}, u32[]{:S(2)}) collective-permute-start(f32[16,64,128]{2,1,0:T(8,128)S(1)} %get-tuple-element.42), channel_id=1, source_target_pairs={{16,2},{144,130},{17,3},{145,131},{177,163},{49,35},{176,162},{48,... | collective-permute-start | bytes 1572872 | tf_op jit(solution)/shard_map/ppermute | solution.py:519
  48.5 0.8 collective-permute-start.11
  49.9 1.0 %shard_map.46.part = f32[16,2,64,128]{3,2,1,0:T(8,128)S(1)} custom-call(f32[22,8,128]{2,1,0:T(8,128)S(1)} %get-tuple-element.28.coef, f32[16,6,8,128]{3,2,1,0:T(8,128)S(1)} %get-tuple-element.29.table, f32[16,2,64,128]{3,2,1,0:T(8,128)S(1)} %get-tuple-element.32.x0, f32[16,2,64,128]{3,2,1,0:T(8,128)S(1)} %get-tuple-element.41.x, ...), custom_call_target="tpu_custom_call" | custom-call | bytes 7380000 | tf_op jit(solution)/shard_map/pallas_call | solution.py:544
  50.9 2.9 %collective-permute-done.10.row_a = f32[16,2,8,128]{3,2,1,0:T(8,128)S(1)} collective-permute-done((f32[16,2,8,128]{3,2,1,0:T(8,128)S(1)}, f32[16,2,8,128]{3,2,1,0:T(8,128)S(1)}, u32[]{:S(2)}, u32[]{:S(2)}) %collective-permute-start.10) | collective-permute-done | bytes 131104 | tf_op jit(solution)/shard_map/ppermute | solution.py:521
  53.8 1.4 %collective-permute-done.11.row_b = f32[16,2,8,128]{3,2,1,0:T(8,128)S(1)} collective-permute-done((f32[16,2,8,128]{3,2,1,0:T(8,128)S(1)}, f32[16,2,8,128]{3,2,1,0:T(8,128)S(1)}, u32[]{:S(2)}, u32[]{:S(2)}) %collective-permute-start.11) | collective-permute-done | bytes 131104 | tf_op jit(solution)/shard_map/ppermute | solution.py:522
  55.6 0.9 %collective-permute-done.9.outer = f32[16,64,128]{2,1,0:T(8,128)S(1)} collective-permute-done((f32[16,64,128]{2,1,0:T(8,128)S(1)}, f32[16,64,128]{2,1,0:T(8,128)S(1)}, u32[]{:S(2)}, u32[]{:S(2)}) %collective-permute-start.9) | collective-permute-done | bytes 524320 | tf_op jit(solution)/shard_map/ppermute | solution.py:519
  57.0 23.5 %all_to_all.11.src = f32[32,4,2,8,128]{4,3,2,1,0:T(8,128)S(1)} all-to-all(f32[32,4,2,8,128]{4,3,2,1,0:T(8,128)S(1)} %shard_map.48), channel_id=1, replica_groups=mesh['xl'=2,'y'=4,'c'=2,'z'=8,'xh'=2] {'xl','y','c','xh'}, dimensions={0} | all-to-all | bytes 2097152 | tf_op jit(solution)/shard_map/all_to_all | solution.py:516
  80.6 1.0 %shard_map.49 = f32[4,2,2,128,128]{4,3,2,1,0:T(8,128)} custom-call(f32[32,4,2,8,128]{4,3,2,1,0:T(8,128)S(1)} %all_to_all.11.src), custom_call_target="tpu_custom_call" | custom-call | tf_op jit(solution)/shard_map/pallas_call | solution.py:550
  (21 shorter events, 4.5 us)
Async XLA Ops:
  0.0 1.2 %copy-start = (f32[4,2,2,128,128]{4,3,2,1,0:T(8,128)S(1)}, f32[4,2,2,128,128]{4,3,2,1,0:T(8,128)}, u32[]{:S(2)}) copy-start(f32[4,2,2,128,128]{4,3,2,1,0:T(8,128)} %src.1) | copy-start | bytes 3145732
  26.7 3.7 %copy-start.1 = (s32[128,128]{1,0:T(8,128)S(1)}, s32[128,128]{1,0:T(8,128)}, u32[]{:S(2)}) copy-start(s32[128,128]{1,0:T(8,128)} %regions) | copy-start | bytes 196612
  27.1 4.0 %collective-permute-start = (f32[16,2,64,128]{3,2,1,0:T(8,128)S(1)}, f32[16,2,64,128]{3,2,1,0:T(8,128)S(1)}, u32[]{:S(2)}, u32[]{:S(2)}) collective-permute-start(f32[16,2,64,128]{3,2,1,0:T(8,128)S(1)} %get-tuple-element.31.x), channel_id=1, source_target_pairs={{0,16},{128,144},{1,17},{129,145},{161,177},{33,49},{160,176},{32,... | collective-permute-start | bytes 3145736 | tf_op jit(solution)/shard_map/ppermute | solution.py:520
  28.0 2.4 %copy-start.2 = (f32[3,4]{1,0:T(4,128)S(1)}, f32[3,4]{1,0:T(4,128)}, u32[]{:S(2)}) copy-start(f32[3,4]{1,0:T(4,128)} %material) | copy-start | bytes 148
  28.0 8.9 %collective-permute-start.1 = (f32[16,64,128]{2,1,0:T(8,128)S(1)}, f32[16,64,128]{2,1,0:T(8,128)S(1)}, u32[]{:S(2)}, u32[]{:S(2)}) collective-permute-start(f32[16,64,128]{2,1,0:T(8,128)S(1)} %get-tuple-element.34), channel_id=1, source_target_pairs={{16,2},{144,130},{17,3},{145,131},{177,163},{49,35},{176,162},{48,... | collective-permute-start | bytes 1572872 | tf_op jit(solution)/shard_map/ppermute | solution.py:519
  29.6 4.6 %collective-permute-start.2 = (f32[16,2,8,128]{3,2,1,0:T(8,128)S(1)}, f32[16,2,8,128]{3,2,1,0:T(8,128)S(1)}, u32[]{:S(2)}, u32[]{:S(2)}) collective-permute-start(f32[16,2,8,128]{3,2,1,0:T(8,128)S(1)} %get-tuple-element.35), channel_id=1, source_target_pairs={{0,128},{16,144},{1,129},{17,145},{161,33},{177,49},{160,32},{176,... | collective-permute-start | bytes 393224 | tf_op jit(solution)/shard_map/ppermute | solution.py:521
  29.6 5.9 %collective-permute-start.3 = (f32[16,2,8,128]{3,2,1,0:T(8,128)S(1)}, f32[16,2,8,128]{3,2,1,0:T(8,128)S(1)}, u32[]{:S(2)}, u32[]{:S(2)}) collective-permute-start(f32[16,2,8,128]{3,2,1,0:T(8,128)S(1)} %get-tuple-element.36), channel_id=1, source_target_pairs={{128,1},{144,17},{129,161},{145,177},{33,160},{49,176},{32,64},{48... | collective-permute-start | bytes 393224 | tf_op jit(solution)/shard_map/ppermute | solution.py:522
  37.3 2.8 %collective-permute-start.4 = (f32[16,2,64,128]{3,2,1,0:T(8,128)S(1)}, f32[16,2,64,128]{3,2,1,0:T(8,128)S(1)}, u32[]{:S(2)}, u32[]{:S(2)}) collective-permute-start(f32[16,2,64,128]{3,2,1,0:T(8,128)S(1)} %get-tuple-element.37.x), channel_id=1, source_target_pairs={{0,16},{128,144},{1,17},{129,145},{161,177},{33,49},{160,176},{32,... | collective-permute-start | bytes 3145736 | tf_op jit(solution)/shard_map/ppermute | solution.py:520
  37.8 8.9 %collective-permute-start.5 = (f32[16,64,128]{2,1,0:T(8,128)S(1)}, f32[16,64,128]{2,1,0:T(8,128)S(1)}, u32[]{:S(2)}, u32[]{:S(2)}) collective-permute-start(f32[16,64,128]{2,1,0:T(8,128)S(1)} %get-tuple-element.38), channel_id=1, source_target_pairs={{16,2},{144,130},{17,3},{145,131},{177,163},{49,35},{176,162},{48,... | collective-permute-start | bytes 1572872 | tf_op jit(solution)/shard_map/ppermute | solution.py:519
  39.2 4.8 %collective-permute-start.6 = (f32[16,2,8,128]{3,2,1,0:T(8,128)S(1)}, f32[16,2,8,128]{3,2,1,0:T(8,128)S(1)}, u32[]{:S(2)}, u32[]{:S(2)}) collective-permute-start(f32[16,2,8,128]{3,2,1,0:T(8,128)S(1)} %get-tuple-element.39), channel_id=1, source_target_pairs={{0,128},{16,144},{1,129},{17,145},{161,33},{177,49},{160,32},{176,... | collective-permute-start | bytes 393224 | tf_op jit(solution)/shard_map/ppermute | solution.py:521
  39.2 6.2 %collective-permute-start.7 = (f32[16,2,8,128]{3,2,1,0:T(8,128)S(1)}, f32[16,2,8,128]{3,2,1,0:T(8,128)S(1)}, u32[]{:S(2)}, u32[]{:S(2)}) collective-permute-start(f32[16,2,8,128]{3,2,1,0:T(8,128)S(1)} %get-tuple-element.40), channel_id=1, source_target_pairs={{128,1},{144,17},{129,161},{145,177},{33,160},{49,176},{32,64},{48... | collective-permute-start | bytes 393224 | tf_op jit(solution)/shard_map/ppermute | solution.py:522
  47.1 2.8 %collective-permute-start.8 = (f32[16,2,64,128]{3,2,1,0:T(8,128)S(1)}, f32[16,2,64,128]{3,2,1,0:T(8,128)S(1)}, u32[]{:S(2)}, u32[]{:S(2)}) collective-permute-start(f32[16,2,64,128]{3,2,1,0:T(8,128)S(1)} %get-tuple-element.41.x), channel_id=1, source_target_pairs={{0,16},{128,144},{1,17},{129,145},{161,177},{33,49},{160,176},{32,... | collective-permute-start | bytes 3145736 | tf_op jit(solution)/shard_map/ppermute | solution.py:520
  47.6 8.9 %collective-permute-start.9 = (f32[16,64,128]{2,1,0:T(8,128)S(1)}, f32[16,64,128]{2,1,0:T(8,128)S(1)}, u32[]{:S(2)}, u32[]{:S(2)}) collective-permute-start(f32[16,64,128]{2,1,0:T(8,128)S(1)} %get-tuple-element.42), channel_id=1, source_target_pairs={{16,2},{144,130},{17,3},{145,131},{177,163},{49,35},{176,162},{48,... | collective-permute-start | bytes 1572872 | tf_op jit(solution)/shard_map/ppermute | solution.py:519
  48.5 5.2 %collective-permute-start.10 = (f32[16,2,8,128]{3,2,1,0:T(8,128)S(1)}, f32[16,2,8,128]{3,2,1,0:T(8,128)S(1)}, u32[]{:S(2)}, u32[]{:S(2)}) collective-permute-start(f32[16,2,8,128]{3,2,1,0:T(8,128)S(1)} %get-tuple-element.43), channel_id=1, source_target_pairs={{0,128},{16,144},{1,129},{17,145},{161,33},{177,49},{160,32},{176,... | collective-permute-start | bytes 393224 | tf_op jit(solution)/shard_map/ppermute | solution.py:521
  48.5 6.6 %collective-permute-start.11 = (f32[16,2,8,128]{3,2,1,0:T(8,128)S(1)}, f32[16,2,8,128]{3,2,1,0:T(8,128)S(1)}, u32[]{:S(2)}, u32[]{:S(2)}) collective-permute-start(f32[16,2,8,128]{3,2,1,0:T(8,128)S(1)} %get-tuple-element.44), channel_id=1, source_target_pairs={{128,1},{144,17},{129,161},{145,177},{33,160},{49,176},{32,64},{48... | collective-permute-start | bytes 393224 | tf_op jit(solution)/shard_map/ppermute | solution.py:522
